TPU v7x, 512 devices: a whole 4x4x16 slice. The times are simulated.
512 devices in a mesh: blk: 64 (over x_lo, z, core), tensor: 8 (over y, x_hi).
Axes of the slice: x: 4 (x_hi: 2, x_lo: 2; x = x_hi * 2 + x_lo), y: 4, z: 16, core: 2. Of those that a mesh axis runs over, the one named last changes fastest.
Arguments:
- weights: float32 [16384, 18944], P('blk', 'tensor'), may hold values from -6 to 6
- warm_q: float32 [64, 18944, 16], P('blk', 'tensor'), may hold values from -6 to 6
Outputs:
- new_weights: float32 [16384, 18944], P('blk', 'tensor')
- next_q: float32 [64, 18944, 16], P('blk', 'tensor')
All inputs are finite; a program needn't handle non-finite values.
Results may differ from a plain program's by a relative error of at most 0.0003.
Values sent between devices are 32-bit elements; how exact they have to be, the bound alone decides.
No kernel may reach another device: no remote copies, remote signals or barrier semaphores. Data moves between devices by JAX's collectives and lax.ppermute only.
A program may use at most 64 MiB of HBM per device.

v0:
```python
import jax
import jax.numpy as jnp
from jax import lax
from jax.sharding import PartitionSpec as P

HIGH = lax.Precision.HIGHEST
step_size = 0.5


def shifted(block, axis, distance):
    devices = range(lax.axis_size(axis))
    route = [((i - distance) % len(devices), i) for i in devices]
    return lax.ppermute(block, axis, route)


def take_left(value):
    return shifted(value, "blk", 1)


def take_right(value):
    return shifted(value, "blk", -1)


def across(own, rank):
    return jnp.concatenate([take_left(own[:, rank:]), take_right(own[:, :rank])], axis=1)


def blocks(matrix, rank):
    return jnp.stack([matrix[:, :rank], matrix[:, rank:]])


def unblock(stacked):
    return jnp.concatenate([stacked[0], stacked[1]], axis=1)


def gram_of(stacked):
    return jnp.einsum("enr,ens->ers", stacked, stacked, precision=HIGH)


def apply_lower(stacked, gram):
    lower = jnp.linalg.cholesky(gram)
    return lax.linalg.triangular_solve(
        lower, stacked, left_side=False, lower=True, transpose_a=True
    )


def row_phase(weights, factors, rank):
    partial_rows = jnp.dot(weights, factors, precision=HIGH)
    own = lax.psum(partial_rows, "tensor")
    differ = own - across(own, rank)
    rows = blocks(differ, rank)
    return apply_lower(rows, gram_of(rows))


def column_phase(weights, rows, rank):
    mine = jnp.einsum("nf,nr->fr", weights, unblock(rows), precision=HIGH)
    return blocks(mine + across(mine, rank), rank)


def shards(weights, warm_q):
    start = warm_q[0]
    rank = start.shape[1]
    factors = jnp.concatenate([take_left(start), start], axis=1)
    rows = row_phase(weights, factors, rank)
    cols = column_phase(weights, rows, rank)
    rows = row_phase(weights, unblock(cols), rank)
    cols = column_phase(weights, rows, rank)
    change = jnp.einsum("enr,efr->nf", rows, cols, precision=HIGH)
    new_weights = weights - step_size * change
    return (new_weights, cols[1][None])


def solution(mesh):
    in_specs = (P("blk", "tensor"), P("blk", "tensor", None))
    out_specs = (P("blk", "tensor"), P("blk", "tensor", None))
    return jax.shard_map(shards, mesh=mesh, in_specs=in_specs, out_specs=out_specs, check_vma=False)
```

profile of v0, /device:TPU:2, one launch (start us, length us, event | category | flops | bytes accessed | tf_op | source)
XLA Modules:
  0.0 156.9 jit_solution(7243911241121868976)
XLA Ops:
  0.6 2.1 %collective-permute-start = (f32[2368,16]{0,1:T(8,128)}, f32[2368,16]{0,1:T(8,128)S(1)}, u32[]{:S(2)}, u32[]{:S(2)}) collective-permute-start(f32[2368,16]{0,1:T(8,128)} %bitcast.62), channel_id=1, source_target_pairs={{504,0},{0,8},{8,16},{16,24},{24,32},{32,40},{40,48},{48,56},{56,6... | collective-permute-start | bytes 454664 | tf_op jit(solution)/shard_map/ppermute | solution.py:13
  2.7 12.0 %collective-permute-done = f32[2368,16]{0,1:T(8,128)S(1)} collective-permute-done((f32[2368,16]{0,1:T(8,128)}, f32[2368,16]{0,1:T(8,128)S(1)}, u32[]{:S(2)}, u32[]{:S(2)}) %collective-permute-start) | collective-permute-done | bytes 151584 | tf_op jit(solution)/shard_map/ppermute | solution.py:13
  14.7 3.0 %convolution_bitcast_fusion.6 = f32[256,32]{0,1:T(8,128)S(1)} fusion(f32[256,2368]{0,1:T(8,128)} %param.5, f32[2368,16]{0,1:T(8,128)} %bitcast.63, f32[2368,16]{0,1:T(8,128)S(1)} %collective-permute-done), kind=kOutput, calls=%fused_computation.8 | convolution fusion | flops 232859648 | bytes 2760704 | tf_op jit(solution)/shard_map/dot_general | solution.py:48
  17.7 41.6 %psum.14 = f32[256,32]{0,1:T(8,128)S(1)} all-reduce(f32[256,32]{0,1:T(8,128)S(1)} %convolution_bitcast_fusion.6), channel_id=1, replica_groups=mesh['blk'=64,'tensor'=8] {'tensor'}, use_global_device_ids=true, to_apply=%region_0.0 | all-reduce | flops 8192 | bytes 65536 | tf_op jit(solution)/shard_map/psum | solution.py:49
  59.3 1.9 %collective-permute-start.1 = (f32[256,16]{0,1:T(8,128)S(1)}, f32[256,16]{0,1:T(8,128)S(1)}, u32[]{:S(2)}, u32[]{:S(2)}) collective-permute-start(f32[256,16]{0,1:T(8,128)S(1)} %get-tuple-element.20), channel_id=1, source_target_pairs={{504,0},{0,8},{8,16},{16,24},{24,32},{32,40},{40,48},{48,56},{56,6... | collective-permute-start | bytes 49160 | tf_op jit(solution)/shard_map/ppermute | solution.py:13
  61.2 5.8 %collective-permute-start.2 = (f32[256,16]{0,1:T(8,128)S(1)}, f32[256,16]{0,1:T(8,128)S(1)}, u32[]{:S(2)}, u32[]{:S(2)}) collective-permute-start(f32[256,16]{0,1:T(8,128)S(1)} %get-tuple-element.21), channel_id=1, source_target_pairs={{8,0},{16,8},{24,16},{32,24},{40,32},{48,40},{56,48},{64,56},{72,6... | collective-permute-start | bytes 49160 | tf_op jit(solution)/shard_map/ppermute | solution.py:13
  67.0 1.4 collective-permute-done.2
  68.4 0.2 fusion.17
  68.7 2.9 %custom-call.8 = f32[2,16,16]{2,1,0:T(8,128)S(1)} custom-call(f32[2,16,16]{2,1,0:T(8,128)S(1)} %fusion.21), custom_call_target="Cholesky" | custom-call | tf_op jit(solution)/shard_map/jit(cholesky)/cholesky | solution.py:41
  71.6 0.1 compare_reduce_fusion.1
  71.8 2.5 %custom-call.9 = f32[2,1,16,16]{2,3,1,0:T(8,128)S(1)} custom-call(f32[2,1,16,16]{3,2,1,0:T(8,128)S(1)} %select_bitcast_fusion.1), custom_call_target="InvertDiagBlocksLowerTriangular" | custom-call | tf_op jit(solution)/shard_map/triangular_solve/custom-call.0 | solution.py:42
  74.3 0.3 convolution_bitcast_fusion.5
  74.6 2.2 %convolution_bitcast_fusion.2 = f32[2368,32]{0,1:T(8,128)S(1)} fusion(f32[256,2368]{0,1:T(8,128)S(1)} %copy-done, f32[256,16]{0,1:T(8,128)S(1)} %get-tuple-element.17, f32[256,16]{0,1:T(8,128)S(1)} %get-tuple-element.16), kind=kOutput, calls=%fused_computation.4 | convolution fusion | flops 232792064 | bytes 2760704 | tf_op jit(solution)/shard_map/nf,nr->fr/dot_general | solution.py:56
  76.8 1.9 %collective-permute-start.3 = (f32[2368,16]{0,1:T(8,128)S(1)}, f32[2368,16]{0,1:T(8,128)S(1)}, u32[]{:S(2)}, u32[]{:S(2)}) collective-permute-start(f32[2368,16]{0,1:T(8,128)S(1)} %get-tuple-element.8), channel_id=1, source_target_pairs={{504,0},{0,8},{8,16},{16,24},{24,32},{32,40},{40,48},{48,56},{56,6... | collective-permute-start | bytes 454664 | tf_op jit(solution)/shard_map/ppermute | solution.py:13
  78.7 5.8 %collective-permute-start.4 = (f32[2368,16]{0,1:T(8,128)S(1)}, f32[2368,16]{0,1:T(8,128)S(1)}, u32[]{:S(2)}, u32[]{:S(2)}) collective-permute-start(f32[2368,16]{0,1:T(8,128)S(1)} %get-tuple-element.9), channel_id=1, source_target_pairs={{8,0},{16,8},{24,16},{32,24},{40,32},{48,40},{56,48},{64,56},{72,6... | collective-permute-start | bytes 454664 | tf_op jit(solution)/shard_map/ppermute | solution.py:13
  84.5 1.0 collective-permute-done.3
  85.4 1.8 %collective-permute-done.4 = f32[2368,16]{0,1:T(8,128)S(1)} collective-permute-done((f32[2368,16]{0,1:T(8,128)S(1)}, f32[2368,16]{0,1:T(8,128)S(1)}, u32[]{:S(2)}, u32[]{:S(2)}) %collective-permute-start.4) | collective-permute-done | bytes 151584 | tf_op jit(solution)/shard_map/ppermute | solution.py:13
  87.2 1.2 convolution_bitcast_fusion.4
  88.4 36.9 %psum.15 = f32[256,32]{0,1:T(8,128)S(1)} all-reduce(f32[256,32]{0,1:T(8,128)S(1)} %convolution_bitcast_fusion.4), channel_id=1, replica_groups=mesh['blk'=64,'tensor'=8] {'tensor'}, use_global_device_ids=true, to_apply=%region_3.6 | all-reduce | flops 8192 | bytes 65536 | tf_op jit(solution)/shard_map/psum | solution.py:49
  125.3 1.9 %collective-permute-start.5 = (f32[256,16]{0,1:T(8,128)S(1)}, f32[256,16]{0,1:T(8,128)S(1)}, u32[]{:S(2)}, u32[]{:S(2)}) collective-permute-start(f32[256,16]{0,1:T(8,128)S(1)} %get-tuple-element.14), channel_id=1, source_target_pairs={{504,0},{0,8},{8,16},{16,24},{24,32},{32,40},{40,48},{48,56},{56,6... | collective-permute-start | bytes 49160 | tf_op jit(solution)/shard_map/ppermute | solution.py:13
  127.2 5.8 %collective-permute-start.6 = (f32[256,16]{0,1:T(8,128)S(1)}, f32[256,16]{0,1:T(8,128)S(1)}, u32[]{:S(2)}, u32[]{:S(2)}) collective-permute-start(f32[256,16]{0,1:T(8,128)S(1)} %get-tuple-element.15), channel_id=1, source_target_pairs={{8,0},{16,8},{24,16},{32,24},{40,32},{48,40},{56,48},{64,56},{72,6... | collective-permute-start | bytes 49160 | tf_op jit(solution)/shard_map/ppermute | solution.py:13
  133.0 1.4 collective-permute-done.6
  134.4 0.2 fusion.16
  134.7 2.9 %custom-call.10 = f32[2,16,16]{2,1,0:T(8,128)S(1)} custom-call(f32[2,16,16]{2,1,0:T(8,128)S(1)} %fusion.19), custom_call_target="Cholesky" | custom-call | tf_op jit(solution)/shard_map/jit(cholesky)/cholesky | solution.py:41
  137.8 2.5 %custom-call.11 = f32[2,1,16,16]{2,3,1,0:T(8,128)S(1)} custom-call(f32[2,1,16,16]{3,2,1,0:T(8,128)S(1)} %select_bitcast_fusion), custom_call_target="InvertDiagBlocksLowerTriangular" | custom-call | tf_op jit(solution)/shard_map/triangular_solve/custom-call.0 | solution.py:42
  140.3 0.3 convolution_bitcast_fusion.3
  140.6 2.2 %convolution_bitcast_fusion.1 = f32[2368,32]{0,1:T(8,128)S(1)} fusion(f32[256,2368]{0,1:T(8,128)S(1)} %copy-done, f32[256,16]{0,1:T(8,128)S(1)} %get-tuple-element.11, f32[256,16]{0,1:T(8,128)S(1)} %get-tuple-element.10), kind=kOutput, calls=%fused_computation.3 | convolution fusion | flops 232792064 | bytes 2760704 | tf_op jit(solution)/shard_map/nf,nr->fr/dot_general | solution.py:56
  142.7 1.9 %collective-permute-start.7 = (f32[2368,16]{0,1:T(8,128)S(1)}, f32[2368,16]{0,1:T(8,128)S(1)}, u32[]{:S(2)}, u32[]{:S(2)}) collective-permute-start(f32[2368,16]{0,1:T(8,128)S(1)} %get-tuple-element.6), channel_id=1, source_target_pairs={{504,0},{0,8},{8,16},{16,24},{24,32},{32,40},{40,48},{48,56},{56,6... | collective-permute-start | bytes 454664 | tf_op jit(solution)/shard_map/ppermute | solution.py:13
  144.7 5.8 %collective-permute-start.8 = (f32[2368,16]{0,1:T(8,128)S(1)}, f32[2368,16]{0,1:T(8,128)S(1)}, u32[]{:S(2)}, u32[]{:S(2)}) collective-permute-start(f32[2368,16]{0,1:T(8,128)S(1)} %get-tuple-element.7), channel_id=1, source_target_pairs={{8,0},{16,8},{24,16},{32,24},{40,32},{48,40},{56,48},{64,56},{72,6... | collective-permute-start | bytes 454664 | tf_op jit(solution)/shard_map/ppermute | solution.py:13
  150.4 1.0 collective-permute-done.7
  151.4 1.8 %collective-permute-done.8 = f32[2368,16]{0,1:T(8,128)S(1)} collective-permute-done((f32[2368,16]{0,1:T(8,128)S(1)}, f32[2368,16]{0,1:T(8,128)S(1)}, u32[]{:S(2)}, u32[]{:S(2)}) %collective-permute-start.8) | collective-permute-done | bytes 151584 | tf_op jit(solution)/shard_map/ppermute | solution.py:13
  153.3 3.6 %fusion.1 = f32[256,2368]{0,1:T(8,128)} fusion(f32[256,2368]{0,1:T(8,128)S(1)} %copy-done, f32[2,256,16]{1,2,0:T(8,128)S(1)} %convolution_bitcast_fusion.3, f32[1,2368,16]{1,2,0:T(8,128)S(1)} %get-tuple-element.5, f32[1,2368,16]{1,2,0:T(8,128)S(1)} %get-tuple-element.4), kind=kOutput, calls=%fused_computation.2 | convolution fusion | flops 234072064 | bytes 5185536 | tf_op jit(solution)/shard_map/enr,efr->nf/dot_general | solution.py:68
  (29 shorter events, 0.7 us)
Async XLA Ops:
  0.6 73.9 %copy-start = (f32[256,2368]{0,1:T(8,128)S(1)}, f32[256,2368]{0,1:T(8,128)}, u32[]{:S(2)}) copy-start(f32[256,2368]{0,1:T(8,128)} %param.5) | copy-start | bytes 7274500
  0.6 14.1 %collective-permute-start = (f32[2368,16]{0,1:T(8,128)}, f32[2368,16]{0,1:T(8,128)S(1)}, u32[]{:S(2)}, u32[]{:S(2)}) collective-permute-start(f32[2368,16]{0,1:T(8,128)} %bitcast.62), channel_id=1, source_target_pairs={{504,0},{0,8},{8,16},{16,24},{24,32},{32,40},{40,48},{48,56},{56,6... | collective-permute-start | bytes 454664 | tf_op jit(solution)/shard_map/ppermute | solution.py:13
  59.3 7.7 %collective-permute-start.1 = (f32[256,16]{0,1:T(8,128)S(1)}, f32[256,16]{0,1:T(8,128)S(1)}, u32[]{:S(2)}, u32[]{:S(2)}) collective-permute-start(f32[256,16]{0,1:T(8,128)S(1)} %get-tuple-element.20), channel_id=1, source_target_pairs={{504,0},{0,8},{8,16},{16,24},{24,32},{32,40},{40,48},{48,56},{56,6... | collective-permute-start | bytes 49160 | tf_op jit(solution)/shard_map/ppermute | solution.py:13
  61.2 7.2 %collective-permute-start.2 = (f32[256,16]{0,1:T(8,128)S(1)}, f32[256,16]{0,1:T(8,128)S(1)}, u32[]{:S(2)}, u32[]{:S(2)}) collective-permute-start(f32[256,16]{0,1:T(8,128)S(1)} %get-tuple-element.21), channel_id=1, source_target_pairs={{8,0},{16,8},{24,16},{32,24},{40,32},{48,40},{56,48},{64,56},{72,6... | collective-permute-start | bytes 49160 | tf_op jit(solution)/shard_map/ppermute | solution.py:13
  76.8 8.7 %collective-permute-start.3 = (f32[2368,16]{0,1:T(8,128)S(1)}, f32[2368,16]{0,1:T(8,128)S(1)}, u32[]{:S(2)}, u32[]{:S(2)}) collective-permute-start(f32[2368,16]{0,1:T(8,128)S(1)} %get-tuple-element.8), channel_id=1, source_target_pairs={{504,0},{0,8},{8,16},{16,24},{24,32},{32,40},{40,48},{48,56},{56,6... | collective-permute-start | bytes 454664 | tf_op jit(solution)/shard_map/ppermute | solution.py:13
  78.7 8.5 %collective-permute-start.4 = (f32[2368,16]{0,1:T(8,128)S(1)}, f32[2368,16]{0,1:T(8,128)S(1)}, u32[]{:S(2)}, u32[]{:S(2)}) collective-permute-start(f32[2368,16]{0,1:T(8,128)S(1)} %get-tuple-element.9), channel_id=1, source_target_pairs={{8,0},{16,8},{24,16},{32,24},{40,32},{48,40},{56,48},{64,56},{72,6... | collective-permute-start | bytes 454664 | tf_op jit(solution)/shard_map/ppermute | solution.py:13
  125.3 7.7 %collective-permute-start.5 = (f32[256,16]{0,1:T(8,128)S(1)}, f32[256,16]{0,1:T(8,128)S(1)}, u32[]{:S(2)}, u32[]{:S(2)}) collective-permute-start(f32[256,16]{0,1:T(8,128)S(1)} %get-tuple-element.14), channel_id=1, source_target_pairs={{504,0},{0,8},{8,16},{16,24},{24,32},{32,40},{40,48},{48,56},{56,6... | collective-permute-start | bytes 49160 | tf_op jit(solution)/shard_map/ppermute | solution.py:13
  127.2 7.2 %collective-permute-start.6 = (f32[256,16]{0,1:T(8,128)S(1)}, f32[256,16]{0,1:T(8,128)S(1)}, u32[]{:S(2)}, u32[]{:S(2)}) collective-permute-start(f32[256,16]{0,1:T(8,128)S(1)} %get-tuple-element.15), channel_id=1, source_target_pairs={{8,0},{16,8},{24,16},{32,24},{40,32},{48,40},{56,48},{64,56},{72,6... | collective-permute-start | bytes 49160 | tf_op jit(solution)/shard_map/ppermute | solution.py:13
  142.7 8.7 %collective-permute-start.7 = (f32[2368,16]{0,1:T(8,128)S(1)}, f32[2368,16]{0,1:T(8,128)S(1)}, u32[]{:S(2)}, u32[]{:S(2)}) collective-permute-start(f32[2368,16]{0,1:T(8,128)S(1)} %get-tuple-element.6), channel_id=1, source_target_pairs={{504,0},{0,8},{8,16},{16,24},{24,32},{32,40},{40,48},{48,56},{56,6... | collective-permute-start | bytes 454664 | tf_op jit(solution)/shard_map/ppermute | solution.py:13
  144.7 8.5 %collective-permute-start.8 = (f32[2368,16]{0,1:T(8,128)S(1)}, f32[2368,16]{0,1:T(8,128)S(1)}, u32[]{:S(2)}, u32[]{:S(2)}) collective-permute-start(f32[2368,16]{0,1:T(8,128)S(1)} %get-tuple-element.7), channel_id=1, source_target_pairs={{8,0},{16,8},{24,16},{32,24},{40,32},{48,40},{56,48},{64,56},{72,6... | collective-permute-start | bytes 454664 | tf_op jit(solution)/shard_map/ppermute | solution.py:13
  153.2 3.6 %copy-start.1 = (f32[1,2368,16]{1,2,0:T(8,128)}, f32[1,2368,16]{1,2,0:T(8,128)S(1)}, u32[]{:S(2)}) copy-start(f32[1,2368,16]{1,2,0:T(8,128)S(1)} %get-tuple-element.5) | copy-start | bytes 454660
where the time goes:
time: 157 us
  blocking collectives  78.4 us (50%)
  starting transfers between devices  32.7 us (21%)
  waiting for transfers between devices  20.3 us (13%)
  matrix products  13 us (8%)
  other arithmetic  11.3 us (7%)
    psum x2, blocking collectives, row_phase(): own = lax.psum(partial_rows, 'tensor')  78.4 us
    ppermute x9, starting transfers between devices, shifted(): return lax.ppermute(block, axis, route)  32.7 us
    ppermute x9, waiting for transfers between devices, shifted(): return lax.ppermute(block, axis, route)  20.3 us
    another operation x7, other arithmetic, apply_lower(): lower = jnp.linalg.cholesky(gram)  6.17 us
    another operation x5, other arithmetic, apply_lower(): lax.linalg.triangular_solve(lower, stacked, left_side=False, lower=True,...  5.08 us
    dot_general x2, matrix products, column_phase(): mine = jnp.einsum('nf,nr->fr', weights, unblock(rows), precision=HIGH)  4.32 us
    dot_general x2, matrix products, row_phase(): partial_rows = jnp.dot(weights, factors, precision=HIGH)  4.27 us
    dot_general x1, matrix products, shards(): change = jnp.einsum('enr,efr->nf', rows, cols, precision=HIGH)  3.6 us
  transfers between devices with their start and end apart: 9, of which 7 were waited for; matrix products, arithmetic and copies ran while one was open for 0% of the time, Pallas kernels for 0%

commit v1 on v0

v1 whole, which is shorter than its diff:
```python
import jax
import jax.numpy as jnp
from jax import lax
from jax.experimental import pallas as pl
from jax.experimental.pallas import tpu as pltpu
from jax.sharding import PartitionSpec as P

HIGH = lax.Precision.HIGHEST
step_size = 0.5


def swapped(block, partner):
    devices = lax.axis_size("blk")
    return lax.ppermute(block, "blk", [(i, partner(i) % devices) for i in range(devices)])


def take_left(block):
    return swapped(block, lambda i: i + 1)


def take_chip(block):
    return swapped(block, lambda i: i ^ 1)


def take_z(block):
    return swapped(block, lambda i: ((i + 1) ^ 1) - 1)


def orth_kernel(parts_ref, out_ref):
    total = parts_ref[0]
    for k in range(1, parts_ref.shape[0]):
        total = total + parts_ref[k]
    both = total.shape[0]
    rank = both // 2
    gram = lax.dot_general(
        total, total, (((1,), (1,)), ((), ())), precision=HIGH, preferred_element_type=jnp.float32
    )
    row = lax.broadcasted_iota(jnp.int32, (rank, 1), 0)
    for edge in range(2):
        rows = slice(edge * rank, (edge + 1) * rank)
        g = gram[rows, rows]
        m = total[rows]
        for j in range(rank):
            inverse = 1.0 / g[j : j + 1, j : j + 1]
            factor = jnp.where(row > j, g[:, j : j + 1] * inverse, 0.0)
            g_row, m_row = g[j : j + 1], m[j : j + 1]
            scale = jnp.where(row == j, lax.rsqrt(g[j : j + 1, j : j + 1]), 1.0)
            g = g - factor * g_row
            m = (m - factor * m_row) * scale
        out_ref[rows] = m


def orthonormal(parts):
    return pl.pallas_call(
        orth_kernel,
        out_shape=jax.ShapeDtypeStruct(parts.shape[1:], jnp.float32),
        in_specs=[pl.BlockSpec(memory_space=pltpu.VMEM)],
        out_specs=pl.BlockSpec(memory_space=pltpu.VMEM),
    )(parts)


def gathered(block):
    ranks = lax.axis_size("tensor")
    copies = jnp.broadcast_to(block[None], (ranks, *block.shape))
    return lax.all_to_all(copies, "tensor", 0, 0, tiled=True)


def shards(weights, warm_q):
    own = weights.T
    start = warm_q[0].T
    rank = start.shape[0]
    even = lax.axis_index("blk") % 2 == 0
    left = take_left(start)
    first = own.shape[0] // 512 * 128
    near_z = [take_z(own[:first])]
    q_chip = jnp.where(even, start, left)
    q_z = jnp.where(even, left, start)
    mine = jnp.dot(jnp.concatenate([q_chip, q_z], axis=0), own, precision=HIGH)
    theirs_z = take_z(mine[rank:])
    theirs_chip = take_chip(mine[:rank])
    rest, mine = lax.optimization_barrier((own[first:], mine))
    near_z = jnp.concatenate(near_z + [take_z(rest)], axis=0)
    near_chip = take_chip(lax.optimization_barrier((own, mine))[0])
    rows = mine - jnp.concatenate([theirs_chip, theirs_z], axis=0)
    basis = orthonormal(gathered(rows))
    d_chip, d_z = own - near_chip, own - near_z

    def columns(basis):
        c = lax.dot_general(basis[:rank], d_chip, (((1,), (1,)), ((), ())), precision=HIGH)
        z = lax.dot_general(basis[rank:], d_z, (((1,), (1,)), ((), ())), precision=HIGH)
        return c, z

    cols_chip, cols_z = columns(basis)
    rows = jnp.concatenate(
        [jnp.dot(cols_chip, d_chip, precision=HIGH), jnp.dot(cols_z, d_z, precision=HIGH)], axis=0
    )
    basis = orthonormal(gathered(rows))
    cols_chip, cols_z = columns(basis)
    change = lax.dot_general(
        jnp.concatenate([cols_chip, cols_z], axis=0), basis, (((0,), (0,)), ((), ())), precision=HIGH
    )
    new = own - step_size * change
    return new.T, jnp.where(even, cols_chip, cols_z).T[None]


def solution(mesh):
    in_specs = (P("blk", "tensor"), P("blk", "tensor", None))
    out_specs = (P("blk", "tensor"), P("blk", "tensor", None))
    return jax.shard_map(shards, mesh=mesh, in_specs=in_specs, out_specs=out_specs, check_vma=False)
```

time: 157 us -> 108 us (0.69)
  blocking collectives: 78.4 us -> 26.9 us
  starting transfers between devices: 32.7 us -> 16.1 us
  matrix products: 13 us -> 25.2 us
  other arithmetic: 11.3 us -> 0.74 us
  waiting for transfers between devices: 20.3 us -> 28.5 us
  Pallas kernels: 0 us -> 6.02 us
  local copies, waits for them, and re-layouts: 0.28 us -> 2.99 us
    psum x2 -> x0, blocking collectives: 78.4 us -> none  [row_phase(): own = lax.psum(partial_rows, 'tensor')]
    all_to_all x0 -> x2, blocking collectives: none -> 26.9 us  [gathered(): return lax.all_to_all(copies, 'tensor', 0, 0, tiled=True)]
    ppermute x9 -> x6, starting transfers between devices: 32.7 us -> 16.1 us  [swapped(): lax.ppermute(block, 'blk', [(i, partner(i) % devices) for i in range(devi...]
    dot_general x7 -> x8, matrix products: 12.5 us -> 25.2 us  [the longest x2 7.56 us: columns(): lax.dot_general(basis[:rank], d_chip, (((1,), (1,)), ((), ())), precision...]
    another operation x12 -> x0, other arithmetic: 11.2 us -> none  [the longest x7 6.17 us: apply_lower(): lower = jnp.linalg.cholesky(gram)]
    ppermute x9 -> x6, waiting for transfers between devices: 20.3 us -> 28.5 us  [swapped(): lax.ppermute(block, 'blk', [(i, partner(i) % devices) for i in range(devi...]
    pallas_call x0 -> x2, Pallas kernels: none -> 6.02 us  [orthonormal(): pl.pallas_call(orth_kernel, out_shape=jax.ShapeDtypeStruct(parts.shape[1:...]
    slice x4 -> x3, local copies, waits for them, and re-layouts: 0.06 us -> 2.94 us  [the longest x1 2.9 us: shards(): rest, mine = lax.optimization_barrier((own[first:], mine))]
  transfers between devices with their start and end apart: 9 -> 6, of which waited for: 7 -> 2; matrix products, arithmetic and copies ran while one was open for 0% -> 9% of each run, Pallas kernels for 0% -> 3%
where the time goes in v1:
time: 108 us; the launch traced here: 107 us
  waiting for transfers between devices  28.5 us (26%)
  blocking collectives  26.9 us (25%)
  matrix products  25.2 us (23%)
  starting transfers between devices  16.1 us (15%)
  Pallas kernels  6.02 us (6%)
  local copies, waits for them, and re-layouts  2.99 us (3%)
    ppermute x6, waiting for transfers between devices, swapped(): lax.ppermute(block, 'blk', [(i, partner(i) % devices) for i in range(devi...  28.5 us
    all_to_all x2, blocking collectives, gathered(): return lax.all_to_all(copies, 'tensor', 0, 0, tiled=True)  26.9 us
    ppermute x6, starting transfers between devices, swapped(): lax.ppermute(block, 'blk', [(i, partner(i) % devices) for i in range(devi...  16.1 us
    dot_general x2, matrix products, columns(): lax.dot_general(basis[:rank], d_chip, (((1,), (1,)), ((), ())), precision...  7.56 us
    dot_general x2, matrix products, columns(): lax.dot_general(basis[rank:], d_z, (((1,), (1,)), ((), ())), precision=HIGH)  7.26 us
    pallas_call x2, Pallas kernels, orthonormal(): pl.pallas_call(orth_kernel, out_shape=jax.ShapeDtypeStruct(parts.shape[1:...  6.02 us
    dot_general x1, matrix products, shards(): lax.dot_general(jnp.concatenate([cols_chip, cols_z], axis=0), basis, (((0...  3.6 us
    slice x1, local copies, waits for them, and re-layouts, shards(): rest, mine = lax.optimization_barrier((own[first:], mine))  2.9 us
  transfers between devices with their start and end apart: 6, of which 2 were waited for; matrix products, arithmetic and copies ran while one was open for 9% of the time, Pallas kernels for 3%

profile of v1, /device:TPU:2, one launch (start us, length us, event | category | flops | bytes accessed | tf_op | source)
XLA Modules:
  0.0 107.2 jit_solution(865061936703860574)
XLA Ops:
  0.6 0.0 copy-start.2
  0.6 0.0 copy-start
  0.6 2.2 %collective-permute-start = (f32[16,2368]{1,0:T(8,128)}, f32[16,2368]{1,0:T(8,128)S(1)}, u32[]{:S(2)}, u32[]{:S(2)}) collective-permute-start(f32[16,2368]{1,0:T(8,128)} %bitcast.25), channel_id=1, source_target_pairs={{0,8},{8,16},{16,24},{24,32},{32,40},{40,48},{48,56},{56,64},{64,7... | collective-permute-start | bytes 454664 | tf_op jit(solution)/shard_map/ppermute | solution.py:14
  2.9 2.9 %slice.32 = f32[1856,256]{1,0:T(8,128)} slice(f32[2368,256]{1,0:T(8,128)} %bitcast.22), slice={[512:2368], [0:256]} | slice | bytes 3801088 | tf_op jit(solution)/shard_map/slice | solution.py:81
  5.7 9.1 %collective-permute-done = f32[16,2368]{1,0:T(8,128)S(1)} collective-permute-done((f32[16,2368]{1,0:T(8,128)}, f32[16,2368]{1,0:T(8,128)S(1)}, u32[]{:S(2)}, u32[]{:S(2)}) %collective-permute-start) | collective-permute-done | bytes 151584 | tf_op jit(solution)/shard_map/ppermute | solution.py:14
  14.8 0.0 copy-done.2
  14.9 0.0 copy-done
  14.9 1.3 %fusion.1 = f32[32,256]{1,0:T(8,128)S(1)} fusion(f32[256,2368]{0,1:T(8,128)S(1)} %copy-done, f32[16,2368]{1,0:T(8,128)S(1)} %get-tuple-element.9, f32[16,2368]{1,0:T(8,128)S(1)} %get-tuple-element.8), kind=kOutput, calls=%fused_computation.3 | convolution fusion | flops 232859648 | bytes 2760704 | tf_op jit(solution)/shard_map/dot_general | solution.py:78
  16.2 1.9 %collective-permute-start.5 = (f32[1856,256]{1,0:T(8,128)}, f32[1856,256]{1,0:T(8,128)}, u32[]{:S(2)}, u32[]{:S(2)}) collective-permute-start(f32[1856,256]{1,0:T(8,128)} %slice.32), channel_id=1, source_target_pairs={{0,504},{8,16},{16,8},{24,32},{32,24},{40,48},{48,40},{56,64},{64,... | collective-permute-start | bytes 5701640 | tf_op jit(solution)/shard_map/ppermute | solution.py:14
  18.1 1.9 %collective-permute-start.3 = (f32[2368,256]{1,0:T(8,128)S(1)}, f32[2368,256]{1,0:T(8,128)}, u32[]{:S(2)}, u32[]{:S(2)}) collective-permute-start(f32[2368,256]{1,0:T(8,128)S(1)} %bitcast.23), channel_id=1, source_target_pairs={{0,8},{8,0},{16,24},{24,16},{32,40},{40,32},{48,56},{56,48},{64,72... | collective-permute-start | bytes 7274504 | tf_op jit(solution)/shard_map/ppermute | solution.py:14
  20.1 5.8 %collective-permute-start.4 = (f32[512,256]{1,0:T(8,128)S(1)}, f32[512,256]{1,0:T(8,128)S(1)}, u32[]{:S(2)}, u32[]{:S(2)}) collective-permute-start(f32[512,256]{1,0:T(8,128)S(1)} %slice.37), channel_id=1, source_target_pairs={{0,504},{8,16},{16,8},{24,32},{32,24},{40,48},{48,40},{56,64},{64,... | collective-permute-start | bytes 1572872 | tf_op jit(solution)/shard_map/ppermute | solution.py:14
  25.8 1.9 %collective-permute-start.1 = (f32[16,256]{1,0:T(8,128)S(1)}, f32[16,256]{1,0:T(8,128)S(1)}, u32[]{:S(2)}, u32[]{:S(2)}) collective-permute-start(f32[16,256]{1,0:T(8,128)S(1)} %get-tuple-element.10), channel_id=1, source_target_pairs={{0,8},{8,0},{16,24},{24,16},{32,40},{40,32},{48,56},{56,48},{64,72... | collective-permute-start | bytes 49160 | tf_op jit(solution)/shard_map/ppermute | solution.py:14
  27.8 2.4 %collective-permute-start.2 = (f32[16,256]{1,0:T(8,128)S(1)}, f32[16,256]{1,0:T(8,128)S(1)}, u32[]{:S(2)}, u32[]{:S(2)}) collective-permute-start(f32[16,256]{1,0:T(8,128)S(1)} %get-tuple-element.11), channel_id=1, source_target_pairs={{0,504},{8,16},{16,8},{24,32},{32,24},{40,48},{48,40},{56,64},{64,... | collective-permute-start | bytes 49160 | tf_op jit(solution)/shard_map/ppermute | solution.py:14
  30.2 0.0 collective-permute-done.1
  30.2 19.4 %collective-permute-done.2 = f32[16,256]{1,0:T(8,128)S(1)} collective-permute-done((f32[16,256]{1,0:T(8,128)S(1)}, f32[16,256]{1,0:T(8,128)S(1)}, u32[]{:S(2)}, u32[]{:S(2)}) %collective-permute-start.2) | collective-permute-done | bytes 16416 | tf_op jit(solution)/shard_map/ppermute | solution.py:14
  49.6 15.0 %all_to_all.10.parts_ref = f32[8,32,256]{2,1,0:T(8,128)} all-to-all(f32[8,32,256]{2,1,0:T(8,128)S(1)} %broadcast_in_dim.6), channel_id=1, replica_groups=mesh['blk'=64,'tensor'=8] {'tensor'}, dimensions={0} | all-to-all | bytes 524288 | tf_op jit(solution)/shard_map/all_to_all | solution.py:65
  64.6 3.0 %shard_map.41 = f32[32,256]{1,0:T(8,128)} custom-call(f32[8,32,256]{2,1,0:T(8,128)} %all_to_all.10.parts_ref), custom_call_target="tpu_custom_call" | custom-call | tf_op jit(solution)/shard_map/pallas_call | solution.py:54
  67.6 0.0 collective-permute-done.4
  67.6 0.0 collective-permute-done.5
  67.6 3.6 %fusion.12 = f32[16,2368]{1,0:T(8,128)S(1)} fusion(f32[32,256]{1,0:T(8,128)} %shard_map.41, f32[1856,256]{1,0:T(8,128)} %collective-permute-done.5, f32[512,256]{1,0:T(8,128)S(1)} %collective-permute-done.4, f32[256,2368]{0,1:T(8,128)S(1)} %copy-done), kind=kOutput, calls=%fused_computation.19 | convolution fusion | flops 117604352 | bytes 5017600 | tf_op jit(solution)/shard_map/dot_general | solution.py:90
  71.3 2.7 %fusion.19 = f32[16,256]{1,0:T(8,128)S(1)} fusion(f32[16,2368]{1,0:T(8,128)S(1)} %fusion.12, f32[1856,256]{1,0:T(8,128)} %collective-permute-done.5, f32[512,256]{1,0:T(8,128)S(1)} %collective-permute-done.4, f32[256,2368]{0,1:T(8,128)S(1)} %copy-done), kind=kOutput, calls=%fused_computation.27 | convolution fusion | flops 117604352 | bytes 5017600 | tf_op jit(solution)/shard_map/dot_general | solution.py:95
  73.9 0.0 collective-permute-done.3
  74.0 0.0 copy-done.3
  74.0 3.8 %fusion.14 = f32[16,2368]{1,0:T(8,128)S(1)} fusion(f32[32,256]{1,0:T(8,128)S(1)} %copy-done.3, f32[2368,256]{1,0:T(8,128)} %collective-permute-done.3, f32[256,2368]{0,1:T(8,128)S(1)} %copy-done), kind=kOutput, calls=%fused_computation.21 | convolution fusion | flops 116998144 | bytes 5017600 | tf_op jit(solution)/shard_map/dot_general | solution.py:89
  77.7 2.8 %fusion.18 = f32[16,256]{1,0:T(8,128)S(1)} fusion(f32[16,2368]{1,0:T(8,128)S(1)} %fusion.14, f32[2368,256]{1,0:T(8,128)} %collective-permute-done.3, f32[256,2368]{0,1:T(8,128)S(1)} %copy-done), kind=kOutput, calls=%fused_computation.26 | convolution fusion | flops 116998144 | bytes 5017600 | tf_op jit(solution)/shard_map/dot_general | solution.py:95
  80.6 11.9 %all_to_all.11.parts_ref = f32[8,32,256]{2,1,0:T(8,128)} all-to-all(f32[8,32,256]{2,1,0:T(8,128)S(1)} %broadcast_in_dim.7), channel_id=1, replica_groups=mesh['blk'=64,'tensor'=8] {'tensor'}, dimensions={0} | all-to-all | bytes 524288 | tf_op jit(solution)/shard_map/all_to_all | solution.py:65
  92.5 3.0 %shard_map.42 = f32[32,256]{1,0:T(8,128)} custom-call(f32[8,32,256]{2,1,0:T(8,128)} %all_to_all.11.parts_ref), custom_call_target="tpu_custom_call" | custom-call | tf_op jit(solution)/shard_map/pallas_call | solution.py:54
  95.5 3.6 %fusion.8 = f32[16,2368]{1,0:T(8,128)S(1)} fusion(f32[32,256]{1,0:T(8,128)} %shard_map.42, f32[1856,256]{1,0:T(8,128)} %collective-permute-done.5, f32[512,256]{1,0:T(8,128)S(1)} %collective-permute-done.4, f32[256,2368]{0,1:T(8,128)S(1)} %copy-done), kind=kOutput, calls=%fused_computation.15 | convolution fusion | flops 117604352 | bytes 5017600 | tf_op jit(solution)/shard_map/dot_general | solution.py:90
  99.1 0.0 copy-done.1
  99.1 3.8 %fusion.10 = f32[16,2368]{1,0:T(8,128)S(1)} fusion(f32[32,256]{1,0:T(8,128)S(1)} %copy-done.1, f32[2368,256]{1,0:T(8,128)} %collective-permute-done.3, f32[256,2368]{0,1:T(8,128)S(1)} %copy-done), kind=kOutput, calls=%fused_computation.17 | convolution fusion | flops 116998144 | bytes 5017600 | tf_op jit(solution)/shard_map/dot_general | solution.py:89
  102.9 0.7 select_bitcast_fusion
  103.6 3.6 %fusion = f32[256,2368]{0,1:T(8,128)} fusion(f32[256,2368]{0,1:T(8,128)S(1)} %copy-done, f32[32,256]{1,0:T(8,128)S(1)} %copy-done.1, f32[16,2368]{1,0:T(8,128)S(1)} %fusion.8, f32[16,2368]{1,0:T(8,128)S(1)} %fusion.10), kind=kOutput, calls=%fused_computation.1 | convolution fusion | flops 234072064 | bytes 5185536 | tf_op jit(solution)/shard_map/dot_general | solution.py:99
  (9 shorter events, 0.1 us)
Async XLA Ops:
  0.6 14.2 %copy-start.2 = (f32[1,2368,16]{1,2,0:T(8,128)S(1)}, f32[1,2368,16]{1,2,0:T(8,128)}, u32[]{:S(2)}) copy-start(f32[1,2368,16]{1,2,0:T(8,128)} %param.3) | copy-start | bytes 454660
  0.6 14.2 %copy-start = (f32[256,2368]{0,1:T(8,128)S(1)}, f32[256,2368]{0,1:T(8,128)}, u32[]{:S(2)}) copy-start(f32[256,2368]{0,1:T(8,128)} %param.2) | copy-start | bytes 7274500
  0.6 14.2 %collective-permute-start = (f32[16,2368]{1,0:T(8,128)}, f32[16,2368]{1,0:T(8,128)S(1)}, u32[]{:S(2)}, u32[]{:S(2)}) collective-permute-start(f32[16,2368]{1,0:T(8,128)} %bitcast.25), channel_id=1, source_target_pairs={{0,8},{8,16},{16,24},{24,32},{32,40},{40,48},{48,56},{56,64},{64,7... | collective-permute-start | bytes 454664 | tf_op jit(solution)/shard_map/ppermute | solution.py:14
  16.2 51.5 %collective-permute-start.5 = (f32[1856,256]{1,0:T(8,128)}, f32[1856,256]{1,0:T(8,128)}, u32[]{:S(2)}, u32[]{:S(2)}) collective-permute-start(f32[1856,256]{1,0:T(8,128)} %slice.32), channel_id=1, source_target_pairs={{0,504},{8,16},{16,8},{24,32},{32,24},{40,48},{48,40},{56,64},{64,... | collective-permute-start | bytes 5701640 | tf_op jit(solution)/shard_map/ppermute | solution.py:14
  18.1 55.9 %collective-permute-start.3 = (f32[2368,256]{1,0:T(8,128)S(1)}, f32[2368,256]{1,0:T(8,128)}, u32[]{:S(2)}, u32[]{:S(2)}) collective-permute-start(f32[2368,256]{1,0:T(8,128)S(1)} %bitcast.23), channel_id=1, source_target_pairs={{0,8},{8,0},{16,24},{24,16},{32,40},{40,32},{48,56},{56,48},{64,72... | collective-permute-start | bytes 7274504 | tf_op jit(solution)/shard_map/ppermute | solution.py:14
  20.1 47.6 %collective-permute-start.4 = (f32[512,256]{1,0:T(8,128)S(1)}, f32[512,256]{1,0:T(8,128)S(1)}, u32[]{:S(2)}, u32[]{:S(2)}) collective-permute-start(f32[512,256]{1,0:T(8,128)S(1)} %slice.37), channel_id=1, source_target_pairs={{0,504},{8,16},{16,8},{24,32},{32,24},{40,48},{48,40},{56,64},{64,... | collective-permute-start | bytes 1572872 | tf_op jit(solution)/shard_map/ppermute | solution.py:14
  25.8 4.3 %collective-permute-start.1 = (f32[16,256]{1,0:T(8,128)S(1)}, f32[16,256]{1,0:T(8,128)S(1)}, u32[]{:S(2)}, u32[]{:S(2)}) collective-permute-start(f32[16,256]{1,0:T(8,128)S(1)} %get-tuple-element.10), channel_id=1, source_target_pairs={{0,8},{8,0},{16,24},{24,16},{32,40},{40,32},{48,56},{56,48},{64,72... | collective-permute-start | bytes 49160 | tf_op jit(solution)/shard_map/ppermute | solution.py:14
  27.8 21.8 %collective-permute-start.2 = (f32[16,256]{1,0:T(8,128)S(1)}, f32[16,256]{1,0:T(8,128)S(1)}, u32[]{:S(2)}, u32[]{:S(2)}) collective-permute-start(f32[16,256]{1,0:T(8,128)S(1)} %get-tuple-element.11), channel_id=1, source_target_pairs={{0,504},{8,16},{16,8},{24,32},{32,24},{40,48},{48,40},{56,64},{64,... | collective-permute-start | bytes 49160 | tf_op jit(solution)/shard_map/ppermute | solution.py:14
  71.3 2.7 %copy-start.3 = (f32[32,256]{1,0:T(8,128)S(1)}, f32[32,256]{1,0:T(8,128)}, u32[]{:S(2)}) copy-start(f32[32,256]{1,0:T(8,128)} %shard_map.41) | copy-start | bytes 98308
  95.5 3.6 %copy-start.1 = (f32[32,256]{1,0:T(8,128)S(1)}, f32[32,256]{1,0:T(8,128)}, u32[]{:S(2)}) copy-start(f32[32,256]{1,0:T(8,128)} %shard_map.42) | copy-start | bytes 98308

commit v2 on v1

v2 whole, which is shorter than its diff:
```python
import functools

import jax
import jax.numpy as jnp
from jax import lax
from jax.experimental import pallas as pl
from jax.experimental.pallas import tpu as pltpu
from jax.sharding import PartitionSpec as P

HIGH = lax.Precision.HIGHEST
f32 = jnp.float32
bf16 = jnp.bfloat16
step_size = 0.5
VMEM = pl.BlockSpec(memory_space=pltpu.VMEM)
HBM = pl.BlockSpec(memory_space=pl.ANY)
NN = (((1,), (0,)), ((), ()))
NT = (((1,), (1,)), ((), ()))


def swapped(block, partner):
    devices = lax.axis_size("blk")
    return lax.ppermute(block, "blk", [(i, partner(i) % devices) for i in range(devices)])


def take_left(block):
    return swapped(block, lambda i: i + 1)


def take_chip(block):
    return swapped(block, lambda i: i ^ 1)


def take_z(block):
    return swapped(block, lambda i: ((i + 1) ^ 1) - 1)


def is_even():
    return lax.rem(lax.axis_index("blk"), 2) == 0


def planes(x):
    one = x.astype(bf16)
    rest = x - one.astype(f32)
    two = rest.astype(bf16)
    return one, two, (rest - two.astype(f32)).astype(bf16)


def dot(a, b, dims=NN):
    return lax.dot_general(a, b, dims, preferred_element_type=f32)


def product(small, large):
    rows = small[0].shape[0]
    a = dot(jnp.concatenate(small, axis=0), large[0])
    b = dot(jnp.concatenate(small[:2], axis=0), large[1])
    c = dot(small[0], large[2])
    return a[:rows] + ((a[rows : 2 * rows] + b[:rows]) + (a[2 * rows :] + b[rows:] + c))


def tiles(extent, tile):
    return [(at, min(tile, extent - at)) for at in range(0, extent, tile)]


def orthonormal_rows(total):
    both, width = total.shape
    rank = both // 2
    gram = lax.dot_general(total, total, NT, precision=HIGH, preferred_element_type=f32)
    g = jnp.stack([gram[:rank, :rank], gram[rank:, rank:]])
    m = total.reshape(2, rank, width)
    row = lax.broadcasted_iota(jnp.int32, (2, rank, 1), 1)
    scale = jnp.ones((2, rank, 1), f32)
    for j in range(rank):
        pivot = g[:, j : j + 1, j : j + 1]
        factor = jnp.where(row > j, g[:, :, j : j + 1] * (1.0 / pivot), 0.0)
        scale = jnp.where(row == j, lax.rsqrt(pivot), scale)
        m = m - factor * m[:, j : j + 1]
        g = g - factor * g[:, j : j + 1]
    return (m * scale).reshape(both, width)


def summed(parts_ref):
    total = parts_ref[0]
    for k in range(1, parts_ref.shape[0]):
        total = total + parts_ref[k]
    return total


def rows_kernel(start_ref, left_ref, own_ref, near_chip_ref, chip_ref, z_ref):
    even = is_even()
    rank, width = z_ref.shape
    chip = jnp.zeros((rank, width), f32)
    z = jnp.zeros((rank, width), f32)
    for at, size in tiles(own_ref.shape[0], 256):
        part = pl.ds(at, size)
        start, left, own = start_ref[:, part], left_ref[:, part], own_ref[part]
        chip = chip + product(planes(jnp.where(even, start, left)), planes(own - near_chip_ref[part]))
        z = z + product(planes(jnp.where(even, left, start)), planes(own))
    for k in range(chip_ref.shape[0]):
        chip_ref[k] = chip
    z_ref[...] = z


def basis_kernel(parts_ref, out_ref):
    out_ref[...] = orthonormal_rows(summed(parts_ref))


def right_sides(basis):
    rank = basis.shape[0] // 2
    zero = jnp.zeros((rank, basis.shape[1]), f32)
    sides = []
    for edge in range(2):
        p = [x.astype(f32) for x in planes(basis[edge * rank : (edge + 1) * rank])]
        for kept in (3, 2, 1):
            groups = []
            for k in range(4):
                x = p[k] if k < kept else zero
                groups += [x, zero] if edge == 0 else [zero, x]
            sides.append(jnp.transpose(jnp.concatenate(groups, axis=0)).astype(bf16))
    return jnp.concatenate(sides, axis=0)


def columns(differences, right):
    left = jnp.concatenate([p for d in differences for p in d], axis=1)
    groups = dot(left, right)
    groups = groups + pltpu.roll(groups, 64, 1)
    return groups + pltpu.roll(groups, 32, 1)


def power_kernel(basis_ref, own_ref, near_chip_ref, first_ref, rest_ref, out_ref):
    both, width = basis_ref.shape
    rank = both // 2
    right = right_sides(basis_ref[...])
    totals = [jnp.zeros((rank, width), f32)] * 2
    for at, size in tiles(own_ref.shape[0], 640):
        part = pl.ds(at, size)
        first = first_ref.shape[0]
        near_z = first_ref[part] if at < first else rest_ref[pl.ds(at - first, size)]
        own = own_ref[part]
        differences = [planes(own - near_chip_ref[part]), planes(own - near_z)]
        cols = jnp.transpose(columns(differences, right))[:both]
        for edge in range(2):
            c = planes(cols[edge * rank : (edge + 1) * rank])
            totals[edge] = totals[edge] + product(c, differences[edge])
    total = jnp.concatenate(totals, axis=0)
    for k in range(out_ref.shape[0]):
        out_ref[k] = total


def update_kernel(parts_ref, own_ref, near_chip_ref, first_ref, rest_ref, new_ref, cols_ref, held, sems):
    even = is_even()
    basis = orthonormal_rows(summed(parts_ref))
    both, width = basis.shape
    rank = both // 2
    right = right_sides(basis)
    b = planes(-step_size * basis)
    zero = jnp.zeros_like(b[0])
    change_right = jnp.concatenate([b[0], b[1], b[2], b[0], b[1], b[0], zero, zero], axis=0)
    copies = []
    for k, (at, size) in enumerate(tiles(own_ref.shape[0], 640)):
        part = pl.ds(at, size)
        first = first_ref.shape[0]
        near_z = first_ref[part] if at < first else rest_ref[pl.ds(at - first, size)]
        own = own_ref[part]
        cols = columns([planes(own - near_chip_ref[part]), planes(own - near_z)], right)
        turned = jnp.transpose(cols)
        cols_ref[:, part] = jnp.where(even, turned[:rank], turned[rank:both])
        group = lax.broadcasted_iota(jnp.int32, cols.shape, 1) // both
        c = planes(cols)
        low = jnp.where(group < 3, c[0].astype(f32), c[1].astype(f32))
        high = jnp.where(group == 0, c[1].astype(f32), c[2].astype(f32))
        left = jnp.concatenate([low, high], axis=1).astype(bf16)
        held[part] = own + dot(left, change_right)
        copy = pltpu.make_async_copy(held.at[part], new_ref.at[part], sems.at[k])
        copy.start()
        copies.append(copy)
    for copy in copies:
        copy.wait()


def call(kernel, name, out_shape, out_specs, cost_us, scratch=(), mib=16):
    return lambda *args: pl.pallas_call(
        kernel,
        out_shape=out_shape,
        in_specs=[VMEM] * len(args),
        out_specs=out_specs,
        scratch_shapes=scratch,
        compiler_params=pltpu.CompilerParams(vmem_limit_bytes=mib * 2**20),
        cost_estimate=pl.CostEstimate(flops=int(cost_us*1.15e9), bytes_accessed=0, transcendentals=0),
        name=name,
    )(*args)


def gathered(copies):
    return lax.all_to_all(copies, "tensor", 0, 0, tiled=True)


COST = dict(rows=8, basis=14, power=4, update=6)
FIRST = 640


def shards(weights, warm_q):
    own = weights.T
    start = warm_q[0].T
    rank, extent = start.shape
    width = own.shape[1]
    ranks = lax.axis_size("tensor")
    shape = lambda *dims: jax.ShapeDtypeStruct(dims, f32)

    left = take_left(start)
    first_z = take_z(own[:FIRST])
    near_chip = take_chip(own)
    chip, z = call(
        rows_kernel, "rows", (shape(ranks, rank, width), shape(rank, width)), (VMEM, VMEM), COST["rows"]
    )(start, left, own, near_chip)
    theirs = take_z(z)
    rest, chip = lax.optimization_barrier((own[FIRST:], chip))
    rest_z = take_z(rest)
    z, first_z = lax.optimization_barrier((z - theirs, first_z))
    rows = jnp.concatenate([chip, jnp.broadcast_to(z[None], chip.shape)], axis=1)
    parts = gathered(rows)
    basis = call(basis_kernel, "basis", shape(2 * rank, width), VMEM, COST["basis"], mib=4)(parts)
    copies = call(power_kernel, "power", shape(ranks, 2 * rank, width), VMEM, COST["power"])(
        basis, own, near_chip, first_z, rest_z
    )
    parts = gathered(copies)
    new, cols = call(
        update_kernel,
        "update",
        (shape(extent, width), shape(rank, extent)),
        (HBM, VMEM),
        COST["update"],
        scratch=[pltpu.VMEM((extent, width), f32), pltpu.SemaphoreType.DMA((len(tiles(extent, 640)),))],
    )(parts, own, near_chip, first_z, rest_z)
    return new.T, cols.T[None]


def solution(mesh):
    in_specs = (P("blk", "tensor"), P("blk", "tensor", None))
    out_specs = (P("blk", "tensor"), P("blk", "tensor", None))
    return jax.shard_map(shards, mesh=mesh, in_specs=in_specs, out_specs=out_specs, check_vma=False)
```

time: 108 us -> 82.3 us (0.76)
  waiting for transfers between devices: 28.5 us -> 0.06 us
  matrix products: 25.2 us -> 0 us
  Pallas kernels: 6.02 us -> 16.9 us
  blocking collectives: 26.9 us -> 37.1 us
  starting transfers between devices: 16.1 us -> 23 us
    ppermute x6 -> x5, waiting for transfers between devices: 28.5 us -> 0.06 us  [swapped(): lax.ppermute(block, 'blk', [(i, partner(i) % devices) for i in range(devi...]
    dot_general x8 -> x0, matrix products: 25.2 us -> none  [the longest x2 7.56 us: columns(): lax.dot_general(basis[:rank], d_chip, (((1,), (1,)), ((), ())), precision...]
    pallas_call x2 -> x4, Pallas kernels: 6.02 us -> 16.9 us  [call(): pl.pallas_call(kernel, out_shape=out_shape, in_specs=[VMEM] * len(args),...]
    all_to_all x2, blocking collectives: 26.9 us -> 37.1 us  [gathered(): return lax.all_to_all(copies, 'tensor', 0, 0, tiled=True)]
    ppermute x6 -> x5, starting transfers between devices: 16.1 us -> 23 us  [swapped(): lax.ppermute(block, 'blk', [(i, partner(i) % devices) for i in range(devi...]
    unnamed x8 -> x6, local copies, waits for them, and re-layouts: 0.02 us -> 2.6 us
    slice x3 -> x2, local copies, waits for them, and re-layouts: 2.94 us -> 1.25 us  [the longest x1 1.13 us: shards(): first_z = take_z(own[:FIRST])]
  transfers between devices with their start and end apart: 6 -> 5, of which waited for: 2 -> 0; matrix products, arithmetic and copies ran while one was open for 9% -> 2% of each run, Pallas kernels for 3% -> 4%
where the time goes in v2:
time: 82.3 us; the launch traced here: 81.9 us
  blocking collectives  37.1 us (45%)
  starting transfers between devices  23 us (28%)
  Pallas kernels  16.9 us (21%)
  local copies, waits for them, and re-layouts  3.86 us (5%)
  between operations  0.9 us (1%)
    all_to_all x2, blocking collectives, gathered(): return lax.all_to_all(copies, 'tensor', 0, 0, tiled=True)  37.1 us
    ppermute x5, starting transfers between devices, swapped(): lax.ppermute(block, 'blk', [(i, partner(i) % devices) for i in range(devi...  23 us
    pallas_call x4, Pallas kernels, call(): pl.pallas_call(kernel, out_shape=out_shape, in_specs=[VMEM] * len(args),...  16.9 us
    unnamed x6, local copies, waits for them, and re-layouts  2.6 us
  transfers between devices with their start and end apart: 5, of which 0 were waited for; matrix products, arithmetic and copies ran while one was open for 2% of the time, Pallas kernels for 4%

profile of v2, /device:TPU:2, one launch (start us, length us, event | category | flops | bytes accessed | tf_op | source)
XLA Modules:
  0.0 81.9 jit_solution(7991426317382880917)
XLA Ops:
  0.6 1.9 %collective-permute-start.1 = (f32[2368,256]{1,0:T(8,128)}, f32[2368,256]{1,0:T(8,128)S(1)}, u32[]{:S(2)}, u32[]{:S(2)}) collective-permute-start(f32[2368,256]{1,0:T(8,128)} %bitcast.8), channel_id=1, source_target_pairs={{0,8},{8,0},{16,24},{24,16},{32,40},{40,32},{48,56},{56,48},{64,72... | collective-permute-start | bytes 7274504 | tf_op jit(solution)/shard_map/ppermute | solution.py:22
  2.6 2.4 %collective-permute-start = (f32[16,2368]{1,0:T(8,128)}, f32[16,2368]{1,0:T(8,128)S(1)}, u32[]{:S(2)}, u32[]{:S(2)}) collective-permute-start(f32[16,2368]{1,0:T(8,128)} %bitcast.14), channel_id=1, source_target_pairs={{0,8},{8,16},{16,24},{24,32},{32,40},{40,48},{48,56},{56,64},{64,7... | collective-permute-start | bytes 454664 | tf_op jit(solution)/shard_map/ppermute | solution.py:22
  5.0 1.1 %slice.9 = f32[640,256]{1,0:T(8,128)S(1)} slice(f32[2368,256]{1,0:T(8,128)} %bitcast.9), slice={[0:640], [0:256]} | slice | bytes 1310720 | tf_op jit(solution)/shard_map/slice | solution.py:210
  6.1 11.0 %collective-permute-start.3 = (f32[640,256]{1,0:T(8,128)S(1)}, f32[640,256]{1,0:T(8,128)S(1)}, u32[]{:S(2)}, u32[]{:S(2)}) collective-permute-start(f32[640,256]{1,0:T(8,128)S(1)} %slice.9), channel_id=1, source_target_pairs={{0,504},{8,16},{16,8},{24,32},{32,24},{40,48},{48,40},{56,64},{64,... | collective-permute-start | bytes 1966088 | tf_op jit(solution)/shard_map/ppermute | solution.py:22
  17.1 0.0 collective-permute-done.left_ref
  17.2 0.0 collective-permute-done.1.near_chip_ref
  17.2 0.0 copy-start
  17.2 1.7 %copy-done = f32[256,2368]{0,1:T(8,128)S(1)} copy-done((f32[256,2368]{0,1:T(8,128)S(1)}, f32[256,2368]{0,1:T(8,128)}, u32[]{:S(2)}) %copy-start) | copy-done | bytes 2424856
  18.8 0.0 copy-start.2
  18.8 0.9 %copy-done.2 = f32[1,2368,16]{1,2,0:T(8,128)S(1)} copy-done((f32[1,2368,16]{1,2,0:T(8,128)S(1)}, f32[1,2368,16]{1,2,0:T(8,128)}, u32[]{:S(2)}) %copy-start.2) | copy-done | bytes 151576
  19.8 0.0 copy-start.1
  19.8 1.4 %rows.1 = (f32[8,16,256]{2,1,0:T(8,128)S(1)}, f32[16,256]{1,0:T(8,128)S(1)}) custom-call(f32[16,2368]{1,0:T(8,128)S(1)} %bitcast.15, f32[16,2368]{1,0:T(8,128)S(1)} %collective-permute-done.left_ref, f32[2368,256]{1,0:T(8,128)S(1)} %bitcast.10, f32[2368,256]{1,0:T(8,128)S(1)} %collective-permute-done.1.near_chip_ref), custom_call_target="tpu_custom_call" | custom-call | flops 9200000000 | tf_op jit(solution)/shard_map/rows/pallas_call | solution.py:181
  21.1 1.9 %collective-permute-start.2 = (f32[16,256]{1,0:T(8,128)S(1)}, f32[16,256]{1,0:T(8,128)S(1)}, u32[]{:S(2)}, u32[]{:S(2)}) collective-permute-start(f32[16,256]{1,0:T(8,128)S(1)} %get-tuple-element.12), channel_id=1, source_target_pairs={{0,504},{8,16},{16,8},{24,32},{32,24},{40,48},{48,40},{56,64},{64,... | collective-permute-start | bytes 49160 | tf_op jit(solution)/shard_map/ppermute | solution.py:22
  23.1 0.0 copy-done.1
  23.1 0.1 slice.8
  23.2 5.8 %collective-permute-start.4 = (f32[1728,256]{1,0:T(8,128)S(1)}, f32[1728,256]{1,0:T(8,128)S(1)}, u32[]{:S(2)}, u32[]{:S(2)}) collective-permute-start(f32[1728,256]{1,0:T(8,128)S(1)} %slice.8), channel_id=1, source_target_pairs={{0,504},{8,16},{16,8},{24,32},{32,24},{40,48},{48,40},{56,64},{64,... | collective-permute-start | bytes 5308424 | tf_op jit(solution)/shard_map/ppermute | solution.py:22
  29.0 0.0 collective-permute-done.2
  29.0 0.0 collective-permute-done.3.first_ref
  29.0 25.6 %all_to_all.10.parts_ref = f32[8,32,256]{2,1,0:T(8,128)S(1)} all-to-all(f32[8,32,256]{2,1,0:T(8,128)S(1)} %pad_maximum_fusion), channel_id=1, replica_groups=mesh['blk'=64,'tensor'=8] {'tensor'}, dimensions={0} | all-to-all | bytes 524288 | tf_op jit(solution)/shard_map/all_to_all | solution.py:194
  54.6 1.6 %basis.1.basis_ref = f32[32,256]{1,0:T(8,128)S(1)} custom-call(f32[8,32,256]{2,1,0:T(8,128)S(1)} %all_to_all.10.parts_ref), custom_call_target="tpu_custom_call" | custom-call | flops 16099999744 | tf_op jit(solution)/shard_map/basis/pallas_call | solution.py:181
  56.2 0.0 collective-permute-done.4.rest_ref
  56.2 4.7 %power.1 = f32[8,32,256]{2,1,0:T(8,128)S(1)} custom-call(f32[32,256]{1,0:T(8,128)S(1)} %basis.1.basis_ref, f32[2368,256]{1,0:T(8,128)S(1)} %bitcast.12, f32[2368,256]{1,0:T(8,128)S(1)} %collective-permute-done.1.near_chip_ref, f32[640,256]{1,0:T(8,128)S(1)} %collective-permute-done.3.first_ref, f32[1728,256]{1,0:T(8,128)S(1)} %collective-permute-done.4.rest_ref), custom_call_target="tpu_custom_call" | custom-call | flops 4600000000 | tf_op jit(solution)/shard_map/power/pallas_call | solution.py:181
  60.9 11.6 %all_to_all.11.parts_ref = f32[8,32,256]{2,1,0:T(8,128)S(1)} all-to-all(f32[8,32,256]{2,1,0:T(8,128)S(1)} %power.1), channel_id=1, replica_groups=mesh['blk'=64,'tensor'=8] {'tensor'}, dimensions={0} | all-to-all | bytes 524288 | tf_op jit(solution)/shard_map/all_to_all | solution.py:194
  72.5 9.2 %update.1 = (f32[2368,256]{1,0:T(8,128)}, f32[16,2368]{1,0:T(8,128)}) custom-call(f32[8,32,256]{2,1,0:T(8,128)S(1)} %all_to_all.11.parts_ref, f32[2368,256]{1,0:T(8,128)S(1)} %bitcast.13, f32[2368,256]{1,0:T(8,128)S(1)} %collective-permute-done.1.near_chip_ref, f32[640,256]{1,0:T(8,128)S(1)} %collective-permute-done.3.first_ref, ...), custom_call_target="tpu_custom_call" | custom-call | flops 6899999744 | tf_op jit(solution)/shard_map/update/pallas_call | solution.py:181
  (3 shorter events, 0.0 us)
Async XLA Ops:
  0.6 16.5 %collective-permute-start.1 = (f32[2368,256]{1,0:T(8,128)}, f32[2368,256]{1,0:T(8,128)S(1)}, u32[]{:S(2)}, u32[]{:S(2)}) collective-permute-start(f32[2368,256]{1,0:T(8,128)} %bitcast.8), channel_id=1, source_target_pairs={{0,8},{8,0},{16,24},{24,16},{32,40},{40,32},{48,56},{56,48},{64,72... | collective-permute-start | bytes 7274504 | tf_op jit(solution)/shard_map/ppermute | solution.py:22
  2.6 14.6 %collective-permute-start = (f32[16,2368]{1,0:T(8,128)}, f32[16,2368]{1,0:T(8,128)S(1)}, u32[]{:S(2)}, u32[]{:S(2)}) collective-permute-start(f32[16,2368]{1,0:T(8,128)} %bitcast.14), channel_id=1, source_target_pairs={{0,8},{8,16},{16,24},{24,32},{32,40},{40,48},{48,56},{56,64},{64,7... | collective-permute-start | bytes 454664 | tf_op jit(solution)/shard_map/ppermute | solution.py:22
  6.1 22.9 %collective-permute-start.3 = (f32[640,256]{1,0:T(8,128)S(1)}, f32[640,256]{1,0:T(8,128)S(1)}, u32[]{:S(2)}, u32[]{:S(2)}) collective-permute-start(f32[640,256]{1,0:T(8,128)S(1)} %slice.9), channel_id=1, source_target_pairs={{0,504},{8,16},{16,8},{24,32},{32,24},{40,48},{48,40},{56,64},{64,... | collective-permute-start | bytes 1966088 | tf_op jit(solution)/shard_map/ppermute | solution.py:22
  17.2 1.7 %copy-start = (f32[256,2368]{0,1:T(8,128)S(1)}, f32[256,2368]{0,1:T(8,128)}, u32[]{:S(2)}) copy-start(f32[256,2368]{0,1:T(8,128)} %param.2) | copy-start | bytes 7274500
  18.8 0.9 %copy-start.2 = (f32[1,2368,16]{1,2,0:T(8,128)S(1)}, f32[1,2368,16]{1,2,0:T(8,128)}, u32[]{:S(2)}) copy-start(f32[1,2368,16]{1,2,0:T(8,128)} %param.3) | copy-start | bytes 454660
  19.8 3.3 %copy-start.1 = (f32[256,2368]{0,1:T(8,128)S(1)}, f32[256,2368]{0,1:T(8,128)}, u32[]{:S(2)}) copy-start(f32[256,2368]{0,1:T(8,128)} %param.2) | copy-start | bytes 7274500
  21.1 7.8 %collective-permute-start.2 = (f32[16,256]{1,0:T(8,128)S(1)}, f32[16,256]{1,0:T(8,128)S(1)}, u32[]{:S(2)}, u32[]{:S(2)}) collective-permute-start(f32[16,256]{1,0:T(8,128)S(1)} %get-tuple-element.12), channel_id=1, source_target_pairs={{0,504},{8,16},{16,8},{24,32},{32,24},{40,48},{48,40},{56,64},{64,... | collective-permute-start | bytes 49160 | tf_op jit(solution)/shard_map/ppermute | solution.py:22
  23.2 33.0 %collective-permute-start.4 = (f32[1728,256]{1,0:T(8,128)S(1)}, f32[1728,256]{1,0:T(8,128)S(1)}, u32[]{:S(2)}, u32[]{:S(2)}) collective-permute-start(f32[1728,256]{1,0:T(8,128)S(1)} %slice.8), channel_id=1, source_target_pairs={{0,504},{8,16},{16,8},{24,32},{32,24},{40,48},{48,40},{56,64},{64,... | collective-permute-start | bytes 5308424 | tf_op jit(solution)/shard_map/ppermute | solution.py:22

commit v3 on v2

v3 whole, which is shorter than its diff:
```python
import functools

import jax
import jax.numpy as jnp
from jax import lax
from jax.experimental import pallas as pl
from jax.experimental.pallas import tpu as pltpu
from jax.sharding import PartitionSpec as P

HIGH = lax.Precision.HIGHEST
f32 = jnp.float32
bf16 = jnp.bfloat16
step_size = 0.5
VMEM = pl.BlockSpec(memory_space=pltpu.VMEM)
HBM = pl.BlockSpec(memory_space=pl.ANY)
NN = (((1,), (0,)), ((), ()))
NT = (((1,), (1,)), ((), ()))


def shifted(block, distance):
    devices = lax.axis_size("blk")
    return lax.ppermute(block, "blk", [(i, (i + distance) % devices) for i in range(devices)])


def planes(x):
    one = x.astype(bf16)
    rest = x - one.astype(f32)
    two = rest.astype(bf16)
    return one, two, (rest - two.astype(f32)).astype(bf16)


def dot(a, b, dims=NN):
    return lax.dot_general(a, b, dims, preferred_element_type=f32)


def product(small, large):
    rows = small[0].shape[0]
    a = dot(jnp.concatenate(small, axis=0), large[0])
    b = dot(jnp.concatenate(small[:2], axis=0), large[1])
    c = dot(small[0], large[2])
    return a[:rows] + ((a[rows : 2 * rows] + b[:rows]) + (a[2 * rows :] + b[rows:] + c))


def tiles(extent, tile):
    return [(at, min(tile, extent - at)) for at in range(0, extent, tile)]


def orthonormal_rows(m):
    rank = m.shape[0]
    g = lax.dot_general(m, m, NT, precision=HIGH, preferred_element_type=f32)
    row = lax.broadcasted_iota(jnp.int32, (rank, 1), 0)
    scale = jnp.ones((rank, 1), f32)
    for j in range(rank):
        pivot = g[j : j + 1, j : j + 1]
        factor = jnp.where(row > j, g[:, j : j + 1] * (1.0 / pivot), 0.0)
        scale = jnp.where(row == j, lax.rsqrt(pivot), scale)
        m = m - factor * m[j : j + 1]
        g = g - factor * g[j : j + 1]
    return m * scale


def summed(parts_ref):
    total = parts_ref[0]
    for k in range(1, parts_ref.shape[0]):
        total = total + parts_ref[k]
    return total


def times(factor_ref, own_ref, skip):
    total = jnp.zeros((factor_ref.shape[0], own_ref.shape[1]), f32)
    for at, size in tiles(own_ref.shape[0], 256):
        total = total + product(planes(factor_ref[:, pl.ds(skip + at, size)]), planes(own_ref[pl.ds(at, size)]))
    return total


def message_kernel(start_ref, own_ref, out_ref):
    width = own_ref.shape[1]
    out_ref[:, pl.ds(width, start_ref.shape[1])] = start_ref[...]
    out_ref[:, pl.ds(0, width)] = times(start_ref, own_ref, 0)


def rows_kernel(left_ref, own_ref, out_ref):
    width = own_ref.shape[1]
    rows = left_ref[:, pl.ds(0, width)] - times(left_ref, own_ref, width)
    for k in range(out_ref.shape[0]):
        out_ref[k] = rows


def basis_kernel(parts_ref, out_ref):
    out_ref[...] = orthonormal_rows(summed(parts_ref))


def right_side(basis):
    rank, width = basis.shape
    zero = jnp.zeros((rank, width), f32)
    p = [x.astype(f32) for x in planes(basis)]
    sides = []
    for kept in (3, 2, 1):
        groups = []
        for k in range(4):
            groups += [p[k] if k < kept else zero, zero]
        sides.append(jnp.transpose(jnp.concatenate(groups, axis=0)).astype(bf16))
    return jnp.concatenate(sides, axis=0)


def columns(difference, right, rank):
    groups = jnp.transpose(dot(jnp.concatenate(difference, axis=1), right))
    return groups[:rank] + (groups[2 * rank : 3 * rank] + groups[4 * rank : 5 * rank])


def power_kernel(basis_ref, own_ref, left_ref, out_ref):
    rank = basis_ref.shape[0]
    right = right_side(basis_ref[...])
    total = jnp.zeros(basis_ref.shape, f32)
    for at, size in tiles(own_ref.shape[0], 640):
        part = pl.ds(at, size)
        difference = planes(left_ref[part] - own_ref[part])
        total = total + product(planes(columns(difference, right, rank)), difference)
    for k in range(out_ref.shape[0]):
        out_ref[k] = total


def factor_kernel(parts_ref, own_ref, left_ref, out_ref):
    basis = orthonormal_rows(summed(parts_ref))
    rank, width = basis.shape
    right = right_side(basis)
    out_ref[:, pl.ds(0, width)] = basis
    for at, size in tiles(own_ref.shape[0], 640):
        part = pl.ds(at, size)
        difference = planes(left_ref[part] - own_ref[part])
        out_ref[:, pl.ds(width + at, size)] = columns(difference, right, rank)


def change_side(basis):
    b = [x.astype(f32) for x in planes(basis)]
    zero = jnp.zeros_like(b[0])
    return jnp.concatenate([b[0], b[1], b[2], b[0], b[1], b[0], zero, zero], axis=0).astype(bf16)


def change(cols, side):
    c = [x.astype(f32) for x in planes(cols)]
    zero = jnp.zeros_like(cols)
    left = jnp.concatenate([c[0], c[0], c[0], c[1], c[1], c[2], zero, zero], axis=0)
    return dot(jnp.transpose(left).astype(bf16), side)


def half_kernel(message_ref, own_ref, out_ref):
    width = own_ref.shape[1]
    side = change_side(step_size * message_ref[:, pl.ds(0, width)])
    for at, size in tiles(own_ref.shape[0], 640):
        part = pl.ds(at, size)
        out_ref[part] = own_ref[part] + change(message_ref[:, pl.ds(width + at, size)], side)


def final_kernel(message_ref, half_ref, new_ref, cols_ref, held, sems):
    width = half_ref.shape[1]
    side = change_side(-step_size * message_ref[:, pl.ds(0, width)])
    copies = []
    for k, (at, size) in enumerate(tiles(half_ref.shape[0], 640)):
        part = pl.ds(at, size)
        cols = message_ref[:, pl.ds(width + at, size)]
        cols_ref[:, part] = cols
        held[part] = half_ref[part] + change(cols, side)
        copy = pltpu.make_async_copy(held.at[part], new_ref.at[part], sems.at[k])
        copy.start()
        copies.append(copy)
    for copy in copies:
        copy.wait()


def call(kernel, name, out_shape, out_specs, cost_us, scratch=(), mib=16):
    return lambda *args: pl.pallas_call(
        kernel,
        out_shape=out_shape,
        in_specs=[VMEM] * len(args),
        out_specs=out_specs,
        scratch_shapes=scratch,
        compiler_params=pltpu.CompilerParams(vmem_limit_bytes=mib * 2**20),
        cost_estimate=pl.CostEstimate(flops=int(cost_us * 1.15e9), bytes_accessed=0, transcendentals=0),
        name=name,
    )(*args)


def gathered(copies):
    return lax.all_to_all(copies, "tensor", 0, 0, tiled=True)


COST = dict(message=2, rows=8, basis=14, power=3, factor=3, half=3, final=3)


def shards(weights, warm_q):
    own = weights.T
    start = warm_q[0].T
    rank, extent = start.shape
    width = own.shape[1]
    ranks = lax.axis_size("tensor")
    shape = lambda *dims: jax.ShapeDtypeStruct(dims, f32)
    whole = shape(rank, width + extent)
    copies = shape(ranks, rank, width)

    message = call(message_kernel, "message", whole, VMEM, COST["message"])(start, own)
    sent, message = lax.optimization_barrier((own, message))
    left = shifted(message, 1)
    left_own = shifted(sent, 1)
    rows = call(rows_kernel, "rows", copies, VMEM, COST["rows"])(left, own)
    basis = call(basis_kernel, "basis", shape(rank, width), VMEM, COST["basis"], mib=4)(gathered(rows))
    power = call(power_kernel, "power", copies, VMEM, COST["power"])(basis, own, left_own)
    factor = call(factor_kernel, "factor", whole, VMEM, COST["factor"])(gathered(power), own, left_own)
    right = shifted(factor, -1)
    half = call(half_kernel, "half", shape(extent, width), VMEM, COST["half"])(factor, own)
    new, cols = call(
        final_kernel,
        "final",
        (shape(extent, width), shape(rank, extent)),
        (HBM, VMEM),
        COST["final"],
        scratch=[pltpu.VMEM((extent, width), f32), pltpu.SemaphoreType.DMA((len(tiles(extent, 640)),))],
    )(right, half)
    return new.T, cols.T[None]


def solution(mesh):
    in_specs = (P("blk", "tensor"), P("blk", "tensor", None))
    out_specs = (P("blk", "tensor"), P("blk", "tensor", None))
    return jax.shard_map(shards, mesh=mesh, in_specs=in_specs, out_specs=out_specs, check_vma=False)
```

time: 82.3 us -> 80.8 us (0.982)
  the two profiles are of different devices: /device:TPU:2 before, /device:TPU:1 now
where the time goes in v3:
time: 80.8 us; the launch traced here: 80.3 us
  blocking collectives  44.9 us (56%)
  Pallas kernels  19.7 us (24%)
  starting transfers between devices  10.4 us (13%)
  waiting for transfers between devices  3.75 us (5%)
  local copies, waits for them, and re-layouts  0.91 us (1%)
    all_to_all x2, blocking collectives, gathered(): return lax.all_to_all(copies, 'tensor', 0, 0, tiled=True)  44.9 us
    pallas_call x7, Pallas kernels, call(): pl.pallas_call(kernel, out_shape=out_shape, in_specs=[VMEM] * len(args),...  19.7 us
    ppermute x3, starting transfers between devices, shifted(): lax.ppermute(block, 'blk', [(i, (i + distance) % devices) for i in range(...  10.4 us
    ppermute x3, waiting for transfers between devices, shifted(): lax.ppermute(block, 'blk', [(i, (i + distance) % devices) for i in range(...  3.75 us
  transfers between devices with their start and end apart: 3, of which 2 were waited for; matrix products, arithmetic and copies ran while one was open for 0% of the time, Pallas kernels for 8%

profile of v3, /device:TPU:1, one launch (start us, length us, event | category | flops | bytes accessed | tf_op | source)
XLA Modules:
  0.0 80.3 jit_solution(3056906669202178010)
XLA Ops:
  0.6 0.0 copy-start
  0.6 0.9 %copy-done = f32[1,2368,16]{1,2,0:T(8,128)S(1)} copy-done((f32[1,2368,16]{1,2,0:T(8,128)S(1)}, f32[1,2368,16]{1,2,0:T(8,128)}, u32[]{:S(2)}) %copy-start) | copy-done | bytes 151576
  1.5 2.4 %message.1 = f32[16,2624]{1,0:T(8,128)S(1)} custom-call(f32[16,2368]{1,0:T(8,128)S(1)} %bitcast.8, f32[2368,256]{1,0:T(8,128)} %bitcast.own_ref), custom_call_target="tpu_custom_call" | custom-call | flops 2300000000 | tf_op jit(solution)/shard_map/message/pallas_call | solution.py:172
  3.9 4.9 %collective-permute-start = (f32[16,2624]{1,0:T(8,128)S(1)}, f32[16,2624]{1,0:T(8,128)S(1)}, u32[]{:S(2)}, u32[]{:S(2)}) collective-permute-start(f32[16,2624]{1,0:T(8,128)S(1)} %message.1), channel_id=1, source_target_pairs={{0,8},{8,16},{16,24},{24,32},{32,40},{40,48},{48,56},{56,64},{64,7... | collective-permute-start | bytes 503816 | tf_op jit(solution)/shard_map/ppermute | solution.py:22
  8.9 1.9 %collective-permute-start.1 = (f32[2368,256]{1,0:T(8,128)}, f32[2368,256]{1,0:T(8,128)S(1)}, u32[]{:S(2)}, u32[]{:S(2)}) collective-permute-start(f32[2368,256]{1,0:T(8,128)} %bitcast.own_ref), channel_id=1, source_target_pairs={{0,8},{8,16},{16,24},{24,32},{32,40},{40,48},{48,56},{56,64},{64,7... | collective-permute-start | bytes 7274504 | tf_op jit(solution)/shard_map/ppermute | solution.py:22
  10.8 2.8 %collective-permute-done.left_ref = f32[16,2624]{1,0:T(8,128)S(1)} collective-permute-done((f32[16,2624]{1,0:T(8,128)S(1)}, f32[16,2624]{1,0:T(8,128)S(1)}, u32[]{:S(2)}, u32[]{:S(2)}) %collective-permute-start) | collective-permute-done | bytes 167968 | tf_op jit(solution)/shard_map/ppermute | solution.py:22
  13.6 2.4 %rows.1 = f32[8,16,256]{2,1,0:T(8,128)S(1)} custom-call(f32[16,2624]{1,0:T(8,128)S(1)} %collective-permute-done.left_ref, f32[2368,256]{1,0:T(8,128)} %bitcast.own_ref), custom_call_target="tpu_custom_call" | custom-call | flops 9200000000 | tf_op jit(solution)/shard_map/rows/pallas_call | solution.py:172
  16.0 35.4 %all_to_all.10.parts_ref = f32[8,16,256]{2,1,0:T(8,128)S(1)} all-to-all(f32[8,16,256]{2,1,0:T(8,128)S(1)} %rows.1), channel_id=1, replica_groups=mesh['blk'=64,'tensor'=8] {'tensor'}, dimensions={0} | all-to-all | bytes 262144 | tf_op jit(solution)/shard_map/all_to_all | solution.py:185
  51.5 1.5 %basis.1.basis_ref = f32[16,256]{1,0:T(8,128)S(1)} custom-call(f32[8,16,256]{2,1,0:T(8,128)S(1)} %all_to_all.10.parts_ref), custom_call_target="tpu_custom_call" | custom-call | flops 16099999744 | tf_op jit(solution)/shard_map/basis/pallas_call | solution.py:172
  52.9 0.0 collective-permute-done.1.left_ref
  52.9 4.2 %power.1 = f32[8,16,256]{2,1,0:T(8,128)S(1)} custom-call(f32[16,256]{1,0:T(8,128)S(1)} %basis.1.basis_ref, f32[2368,256]{1,0:T(8,128)} %bitcast.own_ref, f32[2368,256]{1,0:T(8,128)S(1)} %collective-permute-done.1.left_ref), custom_call_target="tpu_custom_call" | custom-call | flops 3449999872 | tf_op jit(solution)/shard_map/power/pallas_call | solution.py:172
  57.1 9.4 %all_to_all.11.parts_ref = f32[8,16,256]{2,1,0:T(8,128)S(1)} all-to-all(f32[8,16,256]{2,1,0:T(8,128)S(1)} %power.1), channel_id=1, replica_groups=mesh['blk'=64,'tensor'=8] {'tensor'}, dimensions={0} | all-to-all | bytes 262144 | tf_op jit(solution)/shard_map/all_to_all | solution.py:185
  66.5 4.6 %factor.1.message_ref = f32[16,2624]{1,0:T(8,128)S(1)} custom-call(f32[8,16,256]{2,1,0:T(8,128)S(1)} %all_to_all.11.parts_ref, f32[2368,256]{1,0:T(8,128)} %bitcast.own_ref, f32[2368,256]{1,0:T(8,128)S(1)} %collective-permute-done.1.left_ref), custom_call_target="tpu_custom_call" | custom-call | flops 3449999872 | tf_op jit(solution)/shard_map/factor/pallas_call | solution.py:172
  71.1 3.6 %collective-permute-start.2 = (f32[16,2624]{1,0:T(8,128)S(1)}, f32[16,2624]{1,0:T(8,128)S(1)}, u32[]{:S(2)}, u32[]{:S(2)}) collective-permute-start(f32[16,2624]{1,0:T(8,128)S(1)} %factor.1.message_ref), channel_id=1, source_target_pairs={{0,504},{8,0},{16,8},{24,16},{32,24},{40,32},{48,40},{56,48},{64,5... | collective-permute-start | bytes 503816 | tf_op jit(solution)/shard_map/ppermute | solution.py:22
  74.7 2.2 %half.1.half_ref = f32[2368,256]{1,0:T(8,128)S(1)} custom-call(f32[16,2624]{1,0:T(8,128)S(1)} %factor.1.message_ref, f32[2368,256]{1,0:T(8,128)} %bitcast.own_ref), custom_call_target="tpu_custom_call" | custom-call | flops 3449999872 | tf_op jit(solution)/shard_map/half/pallas_call | solution.py:172
  76.9 0.9 %collective-permute-done.2.message_ref = f32[16,2624]{1,0:T(8,128)S(1)} collective-permute-done((f32[16,2624]{1,0:T(8,128)S(1)}, f32[16,2624]{1,0:T(8,128)S(1)}, u32[]{:S(2)}, u32[]{:S(2)}) %collective-permute-start.2) | collective-permute-done | bytes 167968 | tf_op jit(solution)/shard_map/ppermute | solution.py:22
  77.8 2.5 %final.1 = (f32[2368,256]{1,0:T(8,128)}, f32[16,2368]{1,0:T(8,128)}) custom-call(f32[16,2624]{1,0:T(8,128)S(1)} %collective-permute-done.2.message_ref, f32[2368,256]{1,0:T(8,128)S(1)} %half.1.half_ref), custom_call_target="tpu_custom_call" | custom-call | flops 3449999872 | tf_op jit(solution)/shard_map/final/pallas_call | solution.py:172
Async XLA Ops:
  0.6 0.9 %copy-start = (f32[1,2368,16]{1,2,0:T(8,128)S(1)}, f32[1,2368,16]{1,2,0:T(8,128)}, u32[]{:S(2)}) copy-start(f32[1,2368,16]{1,2,0:T(8,128)} %param.3) | copy-start | bytes 454660
  3.9 9.7 %collective-permute-start = (f32[16,2624]{1,0:T(8,128)S(1)}, f32[16,2624]{1,0:T(8,128)S(1)}, u32[]{:S(2)}, u32[]{:S(2)}) collective-permute-start(f32[16,2624]{1,0:T(8,128)S(1)} %message.1), channel_id=1, source_target_pairs={{0,8},{8,16},{16,24},{24,32},{32,40},{40,48},{48,56},{56,64},{64,7... | collective-permute-start | bytes 503816 | tf_op jit(solution)/shard_map/ppermute | solution.py:22
  8.9 44.1 %collective-permute-start.1 = (f32[2368,256]{1,0:T(8,128)}, f32[2368,256]{1,0:T(8,128)S(1)}, u32[]{:S(2)}, u32[]{:S(2)}) collective-permute-start(f32[2368,256]{1,0:T(8,128)} %bitcast.own_ref), channel_id=1, source_target_pairs={{0,8},{8,16},{16,24},{24,32},{32,40},{40,48},{48,56},{56,64},{64,7... | collective-permute-start | bytes 7274504 | tf_op jit(solution)/shard_map/ppermute | solution.py:22
  71.1 6.7 %collective-permute-start.2 = (f32[16,2624]{1,0:T(8,128)S(1)}, f32[16,2624]{1,0:T(8,128)S(1)}, u32[]{:S(2)}, u32[]{:S(2)}) collective-permute-start(f32[16,2624]{1,0:T(8,128)S(1)} %factor.1.message_ref), channel_id=1, source_target_pairs={{0,504},{8,0},{16,8},{24,16},{32,24},{40,32},{48,40},{56,48},{64,5... | collective-permute-start | bytes 503816 | tf_op jit(solution)/shard_map/ppermute | solution.py:22

commit v4 on v3

--- a/solution.py
+++ b/solution.py
@@ -12,7 +12,7 @@
 bf16 = jnp.bfloat16
 step_size = 0.5
 VMEM = pl.BlockSpec(memory_space=pltpu.VMEM)
-HBM = pl.BlockSpec(memory_space=pl.ANY)
+HBM = pl.BlockSpec(memory_space=pltpu.HBM)
 NN = (((1,), (0,)), ((), ()))
 NT = (((1,), (1,)), ((), ()))
 
@@ -42,7 +42,12 @@
 
 
 def tiles(extent, tile):
-    return [(at, min(tile, extent - at)) for at in range(0, extent, tile)]
+    out, at = [], 0
+    while at < extent:
+        size = extent - at if extent - at <= tile + 128 else tile
+        out.append((at, size))
+        at += size
+    return out
 
 
 def orthonormal_rows(m):
@@ -66,28 +71,48 @@
     return total
 
 
-def times(factor_ref, own_ref, skip):
-    total = jnp.zeros((factor_ref.shape[0], own_ref.shape[1]), f32)
-    for at, size in tiles(own_ref.shape[0], 256):
-        total = total + product(planes(factor_ref[:, pl.ds(skip + at, size)]), planes(own_ref[pl.ds(at, size)]))
-    return total
-
-
-def message_kernel(start_ref, own_ref, out_ref):
+def message_kernel(start_ref, own_ref, out_ref, *rest):
+    *own_refs, sems = rest
+    rank, extent = start_ref.shape
     width = own_ref.shape[1]
-    out_ref[:, pl.ds(width, start_ref.shape[1])] = start_ref[...]
-    out_ref[:, pl.ds(0, width)] = times(start_ref, own_ref, 0)
-
-
-def rows_kernel(left_ref, own_ref, out_ref):
-    width = own_ref.shape[1]
-    rows = left_ref[:, pl.ds(0, width)] - times(left_ref, own_ref, width)
+    copies, at = [], 0
+    for ref in own_refs:
+        for inner, size in tiles(ref.shape[0], 512):
+            copies.append((at, size, ref.at[pl.ds(inner, size)]))
+            at += size
+    copies = [
+        (at, size, ref, pltpu.make_async_copy(own_ref.at[pl.ds(at, size)], ref, sems.at[k]))
+        for k, (at, size, ref) in enumerate(copies)
+    ]
+    factor = out_ref.at[:, pl.ds(width, extent)]
+    fetch = pltpu.make_async_copy(start_ref, factor, sems.at[len(copies)])
+    fetch.start()
+    for *_, copy in copies:
+        copy.start()
+    fetch.wait()
+    total = jnp.zeros((rank, width), f32)
+    for at, size, ref, copy in copies:
+        copy.wait()
+        total = total + product(planes(factor[:, pl.ds(at, size)]), planes(ref[...]))
+    out_ref[:, pl.ds(0, width)] = total
+
+
+def pieces(refs, tile):
+    at = 0
+    for k, ref in enumerate(refs):
+        for inner, size in tiles(ref.shape[0], tile):
+            yield at + inner, size, pl.ds(inner, size), k
+        at += ref.shape[0]
+
+
+def rows_kernel(left_ref, *rest):
+    *own_refs, out_ref = rest
+    rank, width = out_ref.shape[1:]
+    rows = left_ref[:, pl.ds(0, width)]
+    for at, size, part, k in pieces(own_refs, 512):
+        rows = rows - product(planes(left_ref[:, pl.ds(width + at, size)]), planes(own_refs[k][part]))
     for k in range(out_ref.shape[0]):
         out_ref[k] = rows
-
-
-def basis_kernel(parts_ref, out_ref):
-    out_ref[...] = orthonormal_rows(summed(parts_ref))
 
 
 def right_side(basis):
@@ -108,26 +133,36 @@
     return groups[:rank] + (groups[2 * rank : 3 * rank] + groups[4 * rank : 5 * rank])
 
 
-def power_kernel(basis_ref, own_ref, left_ref, out_ref):
-    rank = basis_ref.shape[0]
-    right = right_side(basis_ref[...])
-    total = jnp.zeros(basis_ref.shape, f32)
-    for at, size in tiles(own_ref.shape[0], 640):
-        part = pl.ds(at, size)
+def powered(total, basis, own_ref, left_ref):
+    rank = basis.shape[0]
+    right = right_side(basis)
+    for _, size, part, _ in pieces([own_ref], 768):
         difference = planes(left_ref[part] - own_ref[part])
         total = total + product(planes(columns(difference, right, rank)), difference)
+    return total
+
+
+def basis_kernel(mine_ref, other_ref, own_ref, left_ref, basis_ref, total_ref):
+    basis = orthonormal_rows(mine_ref[...] + other_ref[...])
+    basis_ref[...] = basis
+    total_ref[...] = powered(jnp.zeros(basis.shape, f32), basis, own_ref, left_ref)
+
+
+def power_kernel(basis_ref, total_ref, own_ref, left_ref, out_ref):
+    total = powered(total_ref[...], basis_ref[...], own_ref, left_ref)
     for k in range(out_ref.shape[0]):
         out_ref[k] = total
 
 
-def factor_kernel(parts_ref, own_ref, left_ref, out_ref):
+def factor_kernel(parts_ref, *rest):
+    *both, out_ref = rest
+    own_refs, left_refs = both[: len(both) // 2], both[len(both) // 2 :]
     basis = orthonormal_rows(summed(parts_ref))
     rank, width = basis.shape
     right = right_side(basis)
     out_ref[:, pl.ds(0, width)] = basis
-    for at, size in tiles(own_ref.shape[0], 640):
-        part = pl.ds(at, size)
-        difference = planes(left_ref[part] - own_ref[part])
+    for at, size, part, k in pieces(own_refs, 768):
+        difference = planes(left_refs[k][part] - own_refs[k][part])
         out_ref[:, pl.ds(width + at, size)] = columns(difference, right, rank)
 
 
@@ -144,19 +179,19 @@
     return dot(jnp.transpose(left).astype(bf16), side)
 
 
-def half_kernel(message_ref, own_ref, out_ref):
-    width = own_ref.shape[1]
+def half_kernel(message_ref, *rest):
+    *own_refs, out_ref = rest
+    width = out_ref.shape[1]
     side = change_side(step_size * message_ref[:, pl.ds(0, width)])
-    for at, size in tiles(own_ref.shape[0], 640):
-        part = pl.ds(at, size)
-        out_ref[part] = own_ref[part] + change(message_ref[:, pl.ds(width + at, size)], side)
+    for at, size, part, k in pieces(own_refs, 768):
+        out_ref[pl.ds(at, size)] = own_refs[k][part] + change(message_ref[:, pl.ds(width + at, size)], side)
 
 
 def final_kernel(message_ref, half_ref, new_ref, cols_ref, held, sems):
     width = half_ref.shape[1]
     side = change_side(-step_size * message_ref[:, pl.ds(0, width)])
     copies = []
-    for k, (at, size) in enumerate(tiles(half_ref.shape[0], 640)):
+    for k, (at, size) in enumerate(tiles(half_ref.shape[0], 768)):
         part = pl.ds(at, size)
         cols = message_ref[:, pl.ds(width + at, size)]
         cols_ref[:, part] = cols
@@ -168,11 +203,11 @@
         copy.wait()
 
 
-def call(kernel, name, out_shape, out_specs, cost_us, scratch=(), mib=16):
+def call(kernel, name, out_shape, out_specs, cost_us, in_specs=None, scratch=(), mib=16):
     return lambda *args: pl.pallas_call(
         kernel,
         out_shape=out_shape,
-        in_specs=[VMEM] * len(args),
+        in_specs=in_specs or [VMEM] * len(args),
         out_specs=out_specs,
         scratch_shapes=scratch,
         compiler_params=pltpu.CompilerParams(vmem_limit_bytes=mib * 2**20),
@@ -181,11 +216,8 @@
     )(*args)
 
 
-def gathered(copies):
-    return lax.all_to_all(copies, "tensor", 0, 0, tiled=True)
-
-
-COST = dict(message=2, rows=8, basis=14, power=3, factor=3, half=3, final=3)
+COST = dict(message=2, rows=20, basis=14, power=3, factor=3, half=3, final=3)
+PARTS = (1536, 832)
 
 
 def shards(weights, warm_q):
@@ -196,25 +228,43 @@
     ranks = lax.axis_size("tensor")
     shape = lambda *dims: jax.ShapeDtypeStruct(dims, f32)
     whole = shape(rank, width + extent)
-    copies = shape(ranks, rank, width)
-
-    message = call(message_kernel, "message", whole, VMEM, COST["message"])(start, own)
-    sent, message = lax.optimization_barrier((own, message))
+    rows_shape = shape(rank, width)
+
+    message, *own = call(
+        message_kernel,
+        "message",
+        (whole, *(shape(rows, width) for rows in PARTS)),
+        (VMEM,) * 3,
+        COST["message"],
+        in_specs=[HBM, HBM],
+        scratch=[pltpu.SemaphoreType.DMA((1 + sum(len(tiles(rows, 512)) for rows in PARTS),))],
+        mib=60,
+    )(start, own)
     left = shifted(message, 1)
-    left_own = shifted(sent, 1)
-    rows = call(rows_kernel, "rows", copies, VMEM, COST["rows"])(left, own)
-    basis = call(basis_kernel, "basis", shape(rank, width), VMEM, COST["basis"], mib=4)(gathered(rows))
-    power = call(power_kernel, "power", copies, VMEM, COST["power"])(basis, own, left_own)
-    factor = call(factor_kernel, "factor", whole, VMEM, COST["factor"])(gathered(power), own, left_own)
+    left_first = shifted(own[0], 1)
+    copies = call(rows_kernel, "rows", shape(ranks // 2, rank, width), VMEM, COST["rows"])(left, *own)
+    along_y = [[2 * y + x for y in range(ranks // 2)] for x in range(2)]
+    rows = jnp.sum(lax.all_to_all(copies, "tensor", 0, 0, axis_index_groups=along_y, tiled=True), axis=0)
+    other = lax.ppermute(rows, "tensor", [(t, t ^ 1) for t in range(ranks)])
+    sent, rows = lax.optimization_barrier((own[1], rows))
+    left_second = shifted(sent, 1)
+    basis, total = call(basis_kernel, "basis", (rows_shape, rows_shape), (VMEM, VMEM), COST["basis"])(
+        rows, other, own[0], left_first
+    )
+    copies = call(power_kernel, "power", shape(ranks, rank, width), VMEM, COST["power"])(
+        basis, total, own[1], left_second
+    )
+    parts = lax.all_to_all(copies, "tensor", 0, 0, tiled=True)
+    factor = call(factor_kernel, "factor", whole, VMEM, COST["factor"])(parts, *own, left_first, left_second)
     right = shifted(factor, -1)
-    half = call(half_kernel, "half", shape(extent, width), VMEM, COST["half"])(factor, own)
+    half = call(half_kernel, "half", shape(extent, width), VMEM, COST["half"])(factor, *own)
     new, cols = call(
         final_kernel,
         "final",
         (shape(extent, width), shape(rank, extent)),
         (HBM, VMEM),
         COST["final"],
-        scratch=[pltpu.VMEM((extent, width), f32), pltpu.SemaphoreType.DMA((len(tiles(extent, 640)),))],
+        scratch=[pltpu.VMEM((extent, width), f32), pltpu.SemaphoreType.DMA((len(tiles(extent, 768)),))],
     )(right, half)
     return new.T, cols.T[None]
 

time: 80.8 us -> 75.7 us (0.937)
  blocking collectives: 44.9 us -> 17.3 us
  starting transfers between devices: 10.4 us -> 29.9 us
  waiting for transfers between devices: 3.75 us -> 9.97 us
  Pallas kernels: 19.7 us -> 14.9 us
  local copies, waits for them, and re-layouts: 0.91 us -> 2.57 us
    all_to_all x2, blocking collectives: 44.9 us -> 17.3 us  [the longest x1 10.2 us: shards(): parts = lax.all_to_all(copies, 'tensor', 0, 0, tiled=True)]
    ppermute x3 -> x4, starting transfers between devices: 10.4 us -> 25.8 us  [shifted(): lax.ppermute(block, 'blk', [(i, (i + distance) % devices) for i in range(...]
    pallas_call x7, Pallas kernels: 19.7 us -> 14.9 us  [call(): pl.pallas_call(kernel, out_shape=out_shape, in_specs=in_specs or [VMEM] *...]
    ppermute x0 -> x1, waiting for transfers between devices: none -> 4.33 us  [shards(): other = lax.ppermute(rows, 'tensor', [(t, t ^ 1) for t in range(ranks)])]
    ppermute x0 -> x1, starting transfers between devices: none -> 4.1 us  [shards(): other = lax.ppermute(rows, 'tensor', [(t, t ^ 1) for t in range(ranks)])]
    ppermute x3 -> x4, waiting for transfers between devices: 3.75 us -> 5.64 us  [shifted(): lax.ppermute(block, 'blk', [(i, (i + distance) % devices) for i in range(...]
    unnamed x2 -> x8, local copies, waits for them, and re-layouts: 0.91 us -> 2.57 us
  transfers between devices with their start and end apart: 3 -> 5, of which waited for: 2 -> 4; matrix products, arithmetic and copies ran while one was open for 0% -> 0% of each run, Pallas kernels for 8% -> 6%
where the time goes in v4:
time: 75.7 us; the launch traced here: 75.3 us
  starting transfers between devices  29.9 us (39%)
  blocking collectives  17.3 us (23%)
  Pallas kernels  14.9 us (20%)
  waiting for transfers between devices  9.97 us (13%)
  local copies, waits for them, and re-layouts  2.57 us (3%)
    ppermute x4, starting transfers between devices, shifted(): lax.ppermute(block, 'blk', [(i, (i + distance) % devices) for i in range(...  25.8 us
    pallas_call x7, Pallas kernels, call(): pl.pallas_call(kernel, out_shape=out_shape, in_specs=in_specs or [VMEM] *...  14.9 us
    all_to_all x1, blocking collectives, shards(): parts = lax.all_to_all(copies, 'tensor', 0, 0, tiled=True)  10.2 us
    all_to_all x1, blocking collectives, shards(): lax.all_to_all(copies, 'tensor', 0, 0, axis_index_groups=along_y, tiled=T...  7.14 us
    ppermute x4, waiting for transfers between devices, shifted(): lax.ppermute(block, 'blk', [(i, (i + distance) % devices) for i in range(...  5.64 us
    ppermute x1, waiting for transfers between devices, shards(): other = lax.ppermute(rows, 'tensor', [(t, t ^ 1) for t in range(ranks)])  4.33 us
    ppermute x1, starting transfers between devices, shards(): other = lax.ppermute(rows, 'tensor', [(t, t ^ 1) for t in range(ranks)])  4.1 us
    unnamed x8, local copies, waits for them, and re-layouts  2.57 us
  transfers between devices with their start and end apart: 5, of which 4 were waited for; matrix products, arithmetic and copies ran while one was open for 0% of the time, Pallas kernels for 6%

profile of v4, /device:TPU:1, one launch (start us, length us, event | category | flops | bytes accessed | tf_op | source)
XLA Modules:
  0.0 75.3 jit_solution(9903700002308620974)
XLA Ops:
  0.6 3.7 %message.1 = (f32[16,2624]{1,0:T(8,128)}, f32[1536,256]{1,0:T(8,128)}, f32[832,256]{1,0:T(8,128)}) custom-call(f32[16,2368]{1,0:T(8,128)} %bitcast.9, f32[2368,256]{1,0:T(8,128)} %bitcast.8), custom_call_target="tpu_custom_call" | custom-call | flops 2300000000 | tf_op jit(solution)/shard_map/message/pallas_call | solution.py:207
  4.3 4.9 %collective-permute-start = (f32[16,2624]{1,0:T(8,128)}, f32[16,2624]{1,0:T(8,128)S(1)}, u32[]{:S(2)}, u32[]{:S(2)}) collective-permute-start(f32[16,2624]{1,0:T(8,128)} %get-tuple-element.12), channel_id=1, source_target_pairs={{0,8},{8,16},{16,24},{24,32},{32,40},{40,48},{48,56},{56,64},{64,7... | collective-permute-start | bytes 503816 | tf_op jit(solution)/shard_map/ppermute | solution.py:22
  9.3 1.9 %collective-permute-start.2 = (f32[1536,256]{1,0:T(8,128)}, f32[1536,256]{1,0:T(8,128)S(1)}, u32[]{:S(2)}, u32[]{:S(2)}) collective-permute-start(f32[1536,256]{1,0:T(8,128)} %get-tuple-element.13.rest_0_.own_ref), channel_id=1, source_target_pairs={{0,8},{8,16},{16,24},{24,32},{32,40},{40,48},{48,56},{56,64},{64,7... | collective-permute-start | bytes 4718600 | tf_op jit(solution)/shard_map/ppermute | solution.py:22
  11.2 3.0 %collective-permute-done.left_ref = f32[16,2624]{1,0:T(8,128)S(1)} collective-permute-done((f32[16,2624]{1,0:T(8,128)}, f32[16,2624]{1,0:T(8,128)S(1)}, u32[]{:S(2)}, u32[]{:S(2)}) %collective-permute-start) | collective-permute-done | bytes 167968 | tf_op jit(solution)/shard_map/ppermute | solution.py:22
  14.2 0.0 copy-start
  14.2 1.4 %copy-done = f32[1536,256]{1,0:T(8,128)S(1)} copy-done((f32[1536,256]{1,0:T(8,128)S(1)}, f32[1536,256]{1,0:T(8,128)}, u32[]{:S(2)}) %copy-start) | copy-done | bytes 1572888
  15.6 0.0 copy-start.2
  15.6 1.2 %copy-done.2 = f32[832,256]{1,0:T(8,128)S(1)} copy-done((f32[832,256]{1,0:T(8,128)S(1)}, f32[832,256]{1,0:T(8,128)}, u32[]{:S(2)}) %copy-start.2) | copy-done | bytes 851992
  16.8 0.0 copy-start.1
  16.8 0.8 %rows.1 = f32[4,16,256]{2,1,0:T(8,128)S(1)} custom-call(f32[16,2624]{1,0:T(8,128)S(1)} %collective-permute-done.left_ref, f32[1536,256]{1,0:T(8,128)S(1)} %copy-done, f32[832,256]{1,0:T(8,128)S(1)} %copy-done.2), custom_call_target="tpu_custom_call" | custom-call | flops 23000000512 | tf_op jit(solution)/shard_map/rows/pallas_call | solution.py:207
  17.6 7.1 %all_to_all.10 = f32[4,16,256]{2,1,0:T(8,128)S(1)} all-to-all(f32[4,16,256]{2,1,0:T(8,128)S(1)} %rows.1), channel_id=1, replica_groups={{0,2,4,6},{1,3,5,7},{8,10,12,14},{9,11,13,15},{16,18,20,22},{17,19,21,2..., dimensions={0} | all-to-all | bytes 131072 | tf_op jit(solution)/shard_map/all_to_all | solution.py:247
  24.7 0.0 copy-start.3
  24.7 4.1 %collective-permute-start.1 = (f32[16,256]{1,0:T(8,128)S(1)}, f32[16,256]{1,0:T(8,128)S(1)}, u32[]{:S(2)}, u32[]{:S(2)}) collective-permute-start(f32[16,256]{1,0:T(8,128)S(1)} %reduce_sum.9.mine_ref), channel_id=1, source_target_pairs={{0,1},{1,0},{2,3},{3,2},{4,5},{5,4},{6,7},{7,6},{8,9},{9,8},{10,11... | collective-permute-start | bytes 49160 | tf_op jit(solution)/shard_map/ppermute | solution.py:248
  28.8 5.7 %collective-permute-start.3 = (f32[832,256]{1,0:T(8,128)}, f32[832,256]{1,0:T(8,128)S(1)}, u32[]{:S(2)}, u32[]{:S(2)}) collective-permute-start(f32[832,256]{1,0:T(8,128)} %get-tuple-element.17.rest_1_.own_ref), channel_id=1, source_target_pairs={{0,8},{8,16},{16,24},{24,32},{32,40},{40,48},{48,56},{56,64},{64,7... | collective-permute-start | bytes 2555912 | tf_op jit(solution)/shard_map/ppermute | solution.py:22
  34.5 4.3 %collective-permute-done.1.other_ref = f32[16,256]{1,0:T(8,128)S(1)} collective-permute-done((f32[16,256]{1,0:T(8,128)S(1)}, f32[16,256]{1,0:T(8,128)S(1)}, u32[]{:S(2)}, u32[]{:S(2)}) %collective-permute-start.1) | collective-permute-done | bytes 16416 | tf_op jit(solution)/shard_map/ppermute | solution.py:248
  38.9 0.0 collective-permute-done.2.left_ref.rest_2_
  38.9 0.0 copy-done.1
  38.9 3.4 %basis.1 = (f32[16,256]{1,0:T(8,128)S(1)}, f32[16,256]{1,0:T(8,128)S(1)}) custom-call(f32[16,256]{1,0:T(8,128)S(1)} %reduce_sum.9.mine_ref, f32[16,256]{1,0:T(8,128)S(1)} %collective-permute-done.1.other_ref, f32[1536,256]{1,0:T(8,128)S(1)} %copy-done.1, f32[1536,256]{1,0:T(8,128)S(1)} %collective-permute-done.2.left_ref.rest_2_), custom_call_target="tpu_custom_call" | custom-call | flops 16099999744 | tf_op jit(solution)/shard_map/basis/pallas_call | solution.py:207
  42.3 2.2 %collective-permute-done.3.left_ref.rest_3_ = f32[832,256]{1,0:T(8,128)S(1)} collective-permute-done((f32[832,256]{1,0:T(8,128)}, f32[832,256]{1,0:T(8,128)S(1)}, u32[]{:S(2)}, u32[]{:S(2)}) %collective-permute-start.3) | collective-permute-done | bytes 852000 | tf_op jit(solution)/shard_map/ppermute | solution.py:22
  44.5 0.0 copy-done.3
  44.5 1.2 %power.1 = f32[8,16,256]{2,1,0:T(8,128)S(1)} custom-call(f32[16,256]{1,0:T(8,128)S(1)} %get-tuple-element.15.basis_ref, f32[16,256]{1,0:T(8,128)S(1)} %get-tuple-element.16.total_ref, f32[832,256]{1,0:T(8,128)S(1)} %copy-done.3, f32[832,256]{1,0:T(8,128)S(1)} %collective-permute-done.3.left_ref.rest_3_), custom_call_target="tpu_custom_call" | custom-call | flops 3449999872 | tf_op jit(solution)/shard_map/power/pallas_call | solution.py:207
  45.6 10.2 %all_to_all.11.parts_ref = f32[8,16,256]{2,1,0:T(8,128)S(1)} all-to-all(f32[8,16,256]{2,1,0:T(8,128)S(1)} %power.1), channel_id=1, replica_groups=mesh['blk'=64,'tensor'=8] {'tensor'}, dimensions={0} | all-to-all | bytes 262144 | tf_op jit(solution)/shard_map/all_to_all | solution.py:257
  55.8 2.8 %factor.1.message_ref = f32[16,2624]{1,0:T(8,128)S(1)} custom-call(f32[8,16,256]{2,1,0:T(8,128)S(1)} %all_to_all.11.parts_ref, f32[1536,256]{1,0:T(8,128)S(1)} %copy-done.1, f32[832,256]{1,0:T(8,128)S(1)} %copy-done.3, f32[1536,256]{1,0:T(8,128)S(1)} %collective-permute-done.2.left_ref.rest_2_, f32[832,256]{1,0:T(8,128)S(1)} %collective-permute-done.3.left_ref.rest_3_), custom_call_target="tpu_custom_call" | custom-call | flops 3449999872 | tf_op jit(solution)/shard_map/factor/pallas_call | solution.py:207
  58.6 13.2 %collective-permute-start.4 = (f32[16,2624]{1,0:T(8,128)S(1)}, f32[16,2624]{1,0:T(8,128)S(1)}, u32[]{:S(2)}, u32[]{:S(2)}) collective-permute-start(f32[16,2624]{1,0:T(8,128)S(1)} %factor.1.message_ref), channel_id=1, source_target_pairs={{0,504},{8,0},{16,8},{24,16},{32,24},{40,32},{48,40},{56,48},{64,5... | collective-permute-start | bytes 503816 | tf_op jit(solution)/shard_map/ppermute | solution.py:22
  71.8 0.6 half.1.half_ref
  72.4 0.5 collective-permute-done.4.message_ref
  72.8 2.5 %final.1 = (f32[2368,256]{1,0:T(8,128)}, f32[16,2368]{1,0:T(8,128)}) custom-call(f32[16,2624]{1,0:T(8,128)S(1)} %collective-permute-done.4.message_ref, f32[2368,256]{1,0:T(8,128)S(1)} %half.1.half_ref), custom_call_target="tpu_custom_call" | custom-call | flops 3449999872 | tf_op jit(solution)/shard_map/final/pallas_call | solution.py:207
  (1 shorter events, 0.0 us)
Async XLA Ops:
  4.3 9.9 %collective-permute-start = (f32[16,2624]{1,0:T(8,128)}, f32[16,2624]{1,0:T(8,128)S(1)}, u32[]{:S(2)}, u32[]{:S(2)}) collective-permute-start(f32[16,2624]{1,0:T(8,128)} %get-tuple-element.12), channel_id=1, source_target_pairs={{0,8},{8,16},{16,24},{24,32},{32,40},{40,48},{48,56},{56,64},{64,7... | collective-permute-start | bytes 503816 | tf_op jit(solution)/shard_map/ppermute | solution.py:22
  9.3 29.6 %collective-permute-start.2 = (f32[1536,256]{1,0:T(8,128)}, f32[1536,256]{1,0:T(8,128)S(1)}, u32[]{:S(2)}, u32[]{:S(2)}) collective-permute-start(f32[1536,256]{1,0:T(8,128)} %get-tuple-element.13.rest_0_.own_ref), channel_id=1, source_target_pairs={{0,8},{8,16},{16,24},{24,32},{32,40},{40,48},{48,56},{56,64},{64,7... | collective-permute-start | bytes 4718600 | tf_op jit(solution)/shard_map/ppermute | solution.py:22
  14.2 1.4 %copy-start = (f32[1536,256]{1,0:T(8,128)S(1)}, f32[1536,256]{1,0:T(8,128)}, u32[]{:S(2)}) copy-start(f32[1536,256]{1,0:T(8,128)} %get-tuple-element.13.rest_0_.own_ref) | copy-start | bytes 4718596
  15.6 1.2 %copy-start.2 = (f32[832,256]{1,0:T(8,128)S(1)}, f32[832,256]{1,0:T(8,128)}, u32[]{:S(2)}) copy-start(f32[832,256]{1,0:T(8,128)} %get-tuple-element.17.rest_1_.own_ref) | copy-start | bytes 2555908
  16.8 22.1 %copy-start.1 = (f32[1536,256]{1,0:T(8,128)S(1)}, f32[1536,256]{1,0:T(8,128)}, u32[]{:S(2)}) copy-start(f32[1536,256]{1,0:T(8,128)} %get-tuple-element.13.rest_0_.own_ref) | copy-start | bytes 4718596
  24.7 19.8 %copy-start.3 = (f32[832,256]{1,0:T(8,128)S(1)}, f32[832,256]{1,0:T(8,128)}, u32[]{:S(2)}) copy-start(f32[832,256]{1,0:T(8,128)} %get-tuple-element.17.rest_1_.own_ref) | copy-start | bytes 2555908
  24.7 14.1 %collective-permute-start.1 = (f32[16,256]{1,0:T(8,128)S(1)}, f32[16,256]{1,0:T(8,128)S(1)}, u32[]{:S(2)}, u32[]{:S(2)}) collective-permute-start(f32[16,256]{1,0:T(8,128)S(1)} %reduce_sum.9.mine_ref), channel_id=1, source_target_pairs={{0,1},{1,0},{2,3},{3,2},{4,5},{5,4},{6,7},{7,6},{8,9},{9,8},{10,11... | collective-permute-start | bytes 49160 | tf_op jit(solution)/shard_map/ppermute | solution.py:248
  28.8 15.6 %collective-permute-start.3 = (f32[832,256]{1,0:T(8,128)}, f32[832,256]{1,0:T(8,128)S(1)}, u32[]{:S(2)}, u32[]{:S(2)}) collective-permute-start(f32[832,256]{1,0:T(8,128)} %get-tuple-element.17.rest_1_.own_ref), channel_id=1, source_target_pairs={{0,8},{8,16},{16,24},{24,32},{32,40},{40,48},{48,56},{56,64},{64,7... | collective-permute-start | bytes 2555912 | tf_op jit(solution)/shard_map/ppermute | solution.py:22
  58.6 14.3 %collective-permute-start.4 = (f32[16,2624]{1,0:T(8,128)S(1)}, f32[16,2624]{1,0:T(8,128)S(1)}, u32[]{:S(2)}, u32[]{:S(2)}) collective-permute-start(f32[16,2624]{1,0:T(8,128)S(1)} %factor.1.message_ref), channel_id=1, source_target_pairs={{0,504},{8,0},{16,8},{24,16},{32,24},{40,32},{48,40},{56,48},{64,5... | collective-permute-start | bytes 503816 | tf_op jit(solution)/shard_map/ppermute | solution.py:22

commit v5 on v4

--- a/solution.py
+++ b/solution.py
@@ -107,12 +107,11 @@
 
 def rows_kernel(left_ref, *rest):
     *own_refs, out_ref = rest
-    rank, width = out_ref.shape[1:]
+    rank, width = out_ref.shape
     rows = left_ref[:, pl.ds(0, width)]
     for at, size, part, k in pieces(own_refs, 512):
         rows = rows - product(planes(left_ref[:, pl.ds(width + at, size)]), planes(own_refs[k][part]))
-    for k in range(out_ref.shape[0]):
-        out_ref[k] = rows
+    out_ref[...] = rows
 
 
 def right_side(basis):
@@ -142,16 +141,19 @@
     return total
 
 
-def basis_kernel(mine_ref, other_ref, own_ref, left_ref, basis_ref, total_ref):
-    basis = orthonormal_rows(mine_ref[...] + other_ref[...])
+def basis_kernel(parts_ref, own_ref, left_ref, basis_ref, total_ref):
+    basis = orthonormal_rows(summed(parts_ref))
     basis_ref[...] = basis
     total_ref[...] = powered(jnp.zeros(basis.shape, f32), basis, own_ref, left_ref)
 
 
 def power_kernel(basis_ref, total_ref, own_ref, left_ref, out_ref):
     total = powered(total_ref[...], basis_ref[...], own_ref, left_ref)
-    for k in range(out_ref.shape[0]):
-        out_ref[k] = total
+    if len(out_ref.shape) == 2:
+        out_ref[...] = total
+    else:
+        for k in range(out_ref.shape[0]):
+            out_ref[k] = total
 
 
 def factor_kernel(parts_ref, *rest):
@@ -216,8 +218,8 @@
     )(*args)
 
 
-COST = dict(message=2, rows=20, basis=14, power=3, factor=3, half=3, final=3)
-PARTS = (1536, 832)
+COST = dict(message=2, rows=20, basis=10.45, power=3, factor=3, half=3, final=3)
+PARTS = (512, 1152, 704)
 
 
 def shards(weights, warm_q):
@@ -234,28 +236,31 @@
         message_kernel,
         "message",
         (whole, *(shape(rows, width) for rows in PARTS)),
-        (VMEM,) * 3,
+        (VMEM,) * (1 + len(PARTS)),
         COST["message"],
         in_specs=[HBM, HBM],
         scratch=[pltpu.SemaphoreType.DMA((1 + sum(len(tiles(rows, 512)) for rows in PARTS),))],
-        mib=60,
+        mib=50,
     )(start, own)
     left = shifted(message, 1)
-    left_first = shifted(own[0], 1)
-    copies = call(rows_kernel, "rows", shape(ranks // 2, rank, width), VMEM, COST["rows"])(left, *own)
+    lefts = [shifted(own[0], 1)]
+    rows = call(rows_kernel, "rows", rows_shape, VMEM, COST["rows"])(left, *own)
+    other = lax.ppermute(rows, "tensor", [(t, t ^ 1) for t in range(ranks)])
+    *sent, rows = lax.optimization_barrier((*own[1:], rows))
+    lefts += [shifted(piece, 1) for piece in sent]
     along_y = [[2 * y + x for y in range(ranks // 2)] for x in range(2)]
-    rows = jnp.sum(lax.all_to_all(copies, "tensor", 0, 0, axis_index_groups=along_y, tiled=True), axis=0)
-    other = lax.ppermute(rows, "tensor", [(t, t ^ 1) for t in range(ranks)])
-    sent, rows = lax.optimization_barrier((own[1], rows))
-    left_second = shifted(sent, 1)
+    copies = jnp.broadcast_to((rows + other)[None], (ranks // 2, rank, width))
+    parts = lax.all_to_all(copies, "tensor", 0, 0, axis_index_groups=along_y, tiled=True)
     basis, total = call(basis_kernel, "basis", (rows_shape, rows_shape), (VMEM, VMEM), COST["basis"])(
-        rows, other, own[0], left_first
+        parts, own[0], lefts[0]
     )
+    for piece, near in zip(own[1:-1], lefts[1:-1]):
+        total = call(power_kernel, "power", rows_shape, VMEM, COST["power"])(basis, total, piece, near)
     copies = call(power_kernel, "power", shape(ranks, rank, width), VMEM, COST["power"])(
-        basis, total, own[1], left_second
+        basis, total, own[-1], lefts[-1]
     )
     parts = lax.all_to_all(copies, "tensor", 0, 0, tiled=True)
-    factor = call(factor_kernel, "factor", whole, VMEM, COST["factor"])(parts, *own, left_first, left_second)
+    factor = call(factor_kernel, "factor", whole, VMEM, COST["factor"])(parts, *own, *lefts)
     right = shifted(factor, -1)
     half = call(half_kernel, "half", shape(extent, width), VMEM, COST["half"])(factor, *own)
     new, cols = call(

time: 75.7 us -> 80.5 us (1.063)
  blocking collectives: 17.3 us -> 11.1 us
  Pallas kernels: 14.9 us -> 20.4 us
  starting transfers between devices: 29.9 us -> 35 us
  local copies, waits for them, and re-layouts: 2.57 us -> 1.54 us
  waiting for transfers between devices: 9.97 us -> 11 us
    all_to_all x1 -> x0, blocking collectives: 7.14 us -> none  [shards(): lax.all_to_all(copies, 'tensor', 0, 0, axis_index_groups=along_y, tiled=T...]
    pallas_call x7 -> x8, Pallas kernels: 14.9 us -> 20.4 us  [call(): pl.pallas_call(kernel, out_shape=out_shape, in_specs=in_specs or [VMEM] *...]
    ppermute x1, waiting for transfers between devices: 4.33 us -> 0.01 us  [shards(): other = lax.ppermute(rows, 'tensor', [(t, t ^ 1) for t in range(ranks)])]
    all_to_all x0 -> x1, starting transfers between devices: none -> 4.18 us  [shards(): lax.all_to_all(copies, 'tensor', 0, 0, axis_index_groups=along_y, tiled=T...]
    ppermute x4 -> x5, waiting for transfers between devices: 5.64 us -> 8.99 us  [shifted(): lax.ppermute(block, 'blk', [(i, (i + distance) % devices) for i in range(...]
    ppermute x4 -> x5, starting transfers between devices: 25.8 us -> 28.6 us  [shifted(): lax.ppermute(block, 'blk', [(i, (i + distance) % devices) for i in range(...]
    all_to_all x0 -> x1, waiting for transfers between devices: none -> 2.03 us  [shards(): lax.all_to_all(copies, 'tensor', 0, 0, axis_index_groups=along_y, tiled=T...]
    ppermute x1, starting transfers between devices: 4.1 us -> 2.27 us  [shards(): other = lax.ppermute(rows, 'tensor', [(t, t ^ 1) for t in range(ranks)])]
  transfers between devices with their start and end apart: 5 -> 7, of which waited for: 4 -> 4; matrix products, arithmetic and copies ran while one was open for 0% -> 1% of each run, Pallas kernels for 6% -> 11%
where the time goes in v5:
time: 80.5 us; the launch traced here: 79.8 us
  starting transfers between devices  35 us (43%)
  Pallas kernels  20.4 us (25%)
  blocking collectives  11.1 us (14%)
  waiting for transfers between devices  11 us (14%)
  local copies, waits for them, and re-layouts  1.54 us (2%)
    ppermute x5, starting transfers between devices, shifted(): lax.ppermute(block, 'blk', [(i, (i + distance) % devices) for i in range(...  28.6 us
    pallas_call x8, Pallas kernels, call(): pl.pallas_call(kernel, out_shape=out_shape, in_specs=in_specs or [VMEM] *...  20.4 us
    all_to_all x1, blocking collectives, shards(): parts = lax.all_to_all(copies, 'tensor', 0, 0, tiled=True)  11.1 us
    ppermute x5, waiting for transfers between devices, shifted(): lax.ppermute(block, 'blk', [(i, (i + distance) % devices) for i in range(...  8.99 us
    all_to_all x1, starting transfers between devices, shards(): lax.all_to_all(copies, 'tensor', 0, 0, axis_index_groups=along_y, tiled=T...  4.18 us
    ppermute x1, starting transfers between devices, shards(): other = lax.ppermute(rows, 'tensor', [(t, t ^ 1) for t in range(ranks)])  2.27 us
    all_to_all x1, waiting for transfers between devices, shards(): lax.all_to_all(copies, 'tensor', 0, 0, axis_index_groups=along_y, tiled=T...  2.03 us
  transfers between devices with their start and end apart: 7, of which 4 were waited for; matrix products, arithmetic and copies ran while one was open for 1% of the time, Pallas kernels for 11%

profile of v5, /device:TPU:1, one launch (start us, length us, event | category | flops | bytes accessed | tf_op | source)
XLA Modules:
  0.0 79.8 jit_solution(16284740458067156478)
XLA Ops:
  0.6 0.0 copy-start
  0.6 0.9 %copy-done = f32[1,2368,16]{1,2,0:T(8,128)S(1)} copy-done((f32[1,2368,16]{1,2,0:T(8,128)S(1)}, f32[1,2368,16]{1,2,0:T(8,128)}, u32[]{:S(2)}) %copy-start) | copy-done | bytes 151576
  1.5 2.9 %message.1 = (f32[16,2624]{1,0:T(8,128)S(1)}, f32[512,256]{1,0:T(8,128)}, f32[1152,256]{1,0:T(8,128)S(1)}, f32[704,256]{1,0:T(8,128)S(1)}) custom-call(f32[16,2368]{1,0:T(8,128)S(1)} %bitcast.8, f32[2368,256]{1,0:T(8,128)} %bitcast.9), custom_call_target="tpu_custom_call" | custom-call | flops 2300000000 | tf_op jit(solution)/shard_map/message/pallas_call | solution.py:209
  4.4 4.9 %collective-permute-start = (f32[16,2624]{1,0:T(8,128)S(1)}, f32[16,2624]{1,0:T(8,128)S(1)}, u32[]{:S(2)}, u32[]{:S(2)}) collective-permute-start(f32[16,2624]{1,0:T(8,128)S(1)} %get-tuple-element.15), channel_id=1, source_target_pairs={{0,8},{8,16},{16,24},{24,32},{32,40},{40,48},{48,56},{56,64},{64,7... | collective-permute-start | bytes 503816 | tf_op jit(solution)/shard_map/ppermute | solution.py:22
  9.3 1.9 %collective-permute-start.2 = (f32[512,256]{1,0:T(8,128)}, f32[512,256]{1,0:T(8,128)}, u32[]{:S(2)}, u32[]{:S(2)}) collective-permute-start(f32[512,256]{1,0:T(8,128)} %get-tuple-element.16.rest_0_.own_ref), channel_id=1, source_target_pairs={{0,8},{8,16},{16,24},{24,32},{32,40},{40,48},{48,56},{56,64},{64,7... | collective-permute-start | bytes 1572872 | tf_op jit(solution)/shard_map/ppermute | solution.py:22
  11.3 2.8 %collective-permute-done.left_ref = f32[16,2624]{1,0:T(8,128)S(1)} collective-permute-done((f32[16,2624]{1,0:T(8,128)S(1)}, f32[16,2624]{1,0:T(8,128)S(1)}, u32[]{:S(2)}, u32[]{:S(2)}) %collective-permute-start) | collective-permute-done | bytes 167968 | tf_op jit(solution)/shard_map/ppermute | solution.py:22
  14.1 1.8 %rows.1 = f32[16,256]{1,0:T(8,128)S(1)} custom-call(f32[16,2624]{1,0:T(8,128)S(1)} %collective-permute-done.left_ref, f32[512,256]{1,0:T(8,128)} %get-tuple-element.16.rest_0_.own_ref, f32[1152,256]{1,0:T(8,128)S(1)} %get-tuple-element.20.rest_1_.own_ref, f32[704,256]{1,0:T(8,128)S(1)} %get-tuple-element.21.rest_2_.own_ref), custom_call_target="tpu_custom_call" | custom-call | flops 23000000512 | tf_op jit(solution)/shard_map/rows/pallas_call | solution.py:209
  15.8 2.3 %collective-permute-start.1 = (f32[16,256]{1,0:T(8,128)S(1)}, f32[16,256]{1,0:T(8,128)S(1)}, u32[]{:S(2)}, u32[]{:S(2)}) collective-permute-start(f32[16,256]{1,0:T(8,128)S(1)} %rows.1), channel_id=1, source_target_pairs={{0,1},{1,0},{2,3},{3,2},{4,5},{5,4},{6,7},{7,6},{8,9},{9,8},{10,11... | collective-permute-start | bytes 49160 | tf_op jit(solution)/shard_map/ppermute | solution.py:248
  18.1 4.7 %collective-permute-start.3 = (f32[1152,256]{1,0:T(8,128)S(1)}, f32[1152,256]{1,0:T(8,128)S(1)}, u32[]{:S(2)}, u32[]{:S(2)}) collective-permute-start(f32[1152,256]{1,0:T(8,128)S(1)} %get-tuple-element.20.rest_1_.own_ref), channel_id=1, source_target_pairs={{0,8},{8,16},{16,24},{24,32},{32,40},{40,48},{48,56},{56,64},{64,7... | collective-permute-start | bytes 3538952 | tf_op jit(solution)/shard_map/ppermute | solution.py:22
  22.8 0.0 collective-permute-done.1
  22.8 0.6 broadcast_in_dim.4
  23.5 4.2 %all-to-all-start = ((f32[4,16,256]{2,1,0:T(8,128)}), f32[4,16,256]{2,1,0:T(8,128)S(1)}, u32[]{:S(2)}, u32[]{:S(2)}) async-start(f32[4,16,256]{2,1,0:T(8,128)} %broadcast_in_dim.4), calls=%async_computation | async-start | bytes 131072 | tf_op jit(solution)/shard_map/all_to_all | solution.py:253
  27.6 2.4 %collective-permute-start.4 = (f32[704,256]{1,0:T(8,128)S(1)}, f32[704,256]{1,0:T(8,128)}, u32[]{:S(2)}, u32[]{:S(2)}) collective-permute-start(f32[704,256]{1,0:T(8,128)S(1)} %get-tuple-element.21.rest_2_.own_ref), channel_id=1, source_target_pairs={{0,8},{8,16},{16,24},{24,32},{32,40},{40,48},{48,56},{56,64},{64,7... | collective-permute-start | bytes 2162696 | tf_op jit(solution)/shard_map/ppermute | solution.py:22
  30.1 2.0 %all-to-all-done.parts_ref = f32[4,16,256]{2,1,0:T(8,128)S(1)} async-done(((f32[4,16,256]{2,1,0:T(8,128)}), f32[4,16,256]{2,1,0:T(8,128)S(1)}, u32[]{:S(2)}, u32[]{:S(2)}) %all-to-all-start) | async-done | bytes 65568 | tf_op jit(solution)/shard_map/all_to_all | solution.py:253
  32.1 0.0 collective-permute-done.2.left_ref.rest_3_
  32.1 3.6 %basis.1 = (f32[16,256]{1,0:T(8,128)S(1)}, f32[16,256]{1,0:T(8,128)S(1)}) custom-call(f32[4,16,256]{2,1,0:T(8,128)S(1)} %all-to-all-done.parts_ref, f32[512,256]{1,0:T(8,128)} %get-tuple-element.16.rest_0_.own_ref, f32[512,256]{1,0:T(8,128)} %collective-permute-done.2.left_ref.rest_3_), custom_call_target="tpu_custom_call" | custom-call | flops 12017500160 | tf_op jit(solution)/shard_map/basis/pallas_call | solution.py:209
  35.7 0.2 collective-permute-done.3.left_ref.rest_4_
  35.9 1.8 %power.2.total_ref = f32[16,256]{1,0:T(8,128)S(1)} custom-call(f32[16,256]{1,0:T(8,128)S(1)} %get-tuple-element.18.basis_ref, f32[16,256]{1,0:T(8,128)S(1)} %get-tuple-element.19.total_ref, f32[1152,256]{1,0:T(8,128)S(1)} %get-tuple-element.20.rest_1_.own_ref, f32[1152,256]{1,0:T(8,128)S(1)} %collective-permute-done.3.left_ref.rest_4_), custom_call_target="tpu_custom_call" | custom-call | flops 3449999872 | tf_op jit(solution)/shard_map/power/pallas_call | solution.py:209
  37.7 5.9 %collective-permute-done.4.left_ref.rest_5_ = f32[704,256]{1,0:T(8,128)} collective-permute-done((f32[704,256]{1,0:T(8,128)S(1)}, f32[704,256]{1,0:T(8,128)}, u32[]{:S(2)}, u32[]{:S(2)}) %collective-permute-start.4) | collective-permute-done | bytes 720928 | tf_op jit(solution)/shard_map/ppermute | solution.py:22
  43.6 2.2 %power.3 = f32[8,16,256]{2,1,0:T(8,128)S(1)} custom-call(f32[16,256]{1,0:T(8,128)S(1)} %get-tuple-element.18.basis_ref, f32[16,256]{1,0:T(8,128)S(1)} %power.2.total_ref, f32[704,256]{1,0:T(8,128)S(1)} %get-tuple-element.21.rest_2_.own_ref, f32[704,256]{1,0:T(8,128)} %collective-permute-done.4.left_ref.rest_5_), custom_call_target="tpu_custom_call" | custom-call | flops 3449999872 | tf_op jit(solution)/shard_map/power/pallas_call | solution.py:209
  45.8 11.1 %all_to_all.10.parts_ref = f32[8,16,256]{2,1,0:T(8,128)S(1)} all-to-all(f32[8,16,256]{2,1,0:T(8,128)S(1)} %power.3), channel_id=1, replica_groups=mesh['blk'=64,'tensor'=8] {'tensor'}, dimensions={0} | all-to-all | bytes 262144 | tf_op jit(solution)/shard_map/all_to_all | solution.py:262
  56.9 4.2 %factor.1.message_ref = f32[16,2624]{1,0:T(8,128)S(1)} custom-call(f32[8,16,256]{2,1,0:T(8,128)S(1)} %all_to_all.10.parts_ref, f32[512,256]{1,0:T(8,128)} %get-tuple-element.16.rest_0_.own_ref, f32[1152,256]{1,0:T(8,128)S(1)} %get-tuple-element.20.rest_1_.own_ref, f32[704,256]{1,0:T(8,128)S(1)} %get-tuple-element.21.rest_2_.own_ref, ...), custom_call_target="tpu_custom_call" | custom-call | flops 3449999872 | tf_op jit(solution)/shard_map/factor/pallas_call | solution.py:209
  61.1 14.6 %collective-permute-start.5 = (f32[16,2624]{1,0:T(8,128)S(1)}, f32[16,2624]{1,0:T(8,128)S(1)}, u32[]{:S(2)}, u32[]{:S(2)}) collective-permute-start(f32[16,2624]{1,0:T(8,128)S(1)} %factor.1.message_ref), channel_id=1, source_target_pairs={{0,504},{8,0},{16,8},{24,16},{32,24},{40,32},{48,40},{56,48},{64,5... | collective-permute-start | bytes 503816 | tf_op jit(solution)/shard_map/ppermute | solution.py:22
  75.8 1.6 %half.1.half_ref = f32[2368,256]{1,0:T(8,128)S(1)} custom-call(f32[16,2624]{1,0:T(8,128)S(1)} %factor.1.message_ref, f32[512,256]{1,0:T(8,128)} %get-tuple-element.16.rest_0_.own_ref, f32[1152,256]{1,0:T(8,128)S(1)} %get-tuple-element.20.rest_1_.own_ref, f32[704,256]{1,0:T(8,128)S(1)} %get-tuple-element.21.rest_2_.own_ref), custom_call_target="tpu_custom_call" | custom-call | flops 3449999872 | tf_op jit(solution)/shard_map/half/pallas_call | solution.py:209
  77.4 0.0 collective-permute-done.5.message_ref
  77.4 2.5 %final.1 = (f32[2368,256]{1,0:T(8,128)}, f32[16,2368]{1,0:T(8,128)}) custom-call(f32[16,2624]{1,0:T(8,128)S(1)} %collective-permute-done.5.message_ref, f32[2368,256]{1,0:T(8,128)S(1)} %half.1.half_ref), custom_call_target="tpu_custom_call" | custom-call | flops 3449999872 | tf_op jit(solution)/shard_map/final/pallas_call | solution.py:209
  (1 shorter events, 0.0 us)
Async XLA Ops:
  0.6 0.9 %copy-start = (f32[1,2368,16]{1,2,0:T(8,128)S(1)}, f32[1,2368,16]{1,2,0:T(8,128)}, u32[]{:S(2)}) copy-start(f32[1,2368,16]{1,2,0:T(8,128)} %param.3) | copy-start | bytes 454660
  4.4 9.7 %collective-permute-start = (f32[16,2624]{1,0:T(8,128)S(1)}, f32[16,2624]{1,0:T(8,128)S(1)}, u32[]{:S(2)}, u32[]{:S(2)}) collective-permute-start(f32[16,2624]{1,0:T(8,128)S(1)} %get-tuple-element.15), channel_id=1, source_target_pairs={{0,8},{8,16},{16,24},{24,32},{32,40},{40,48},{48,56},{56,64},{64,7... | collective-permute-start | bytes 503816 | tf_op jit(solution)/shard_map/ppermute | solution.py:22
  9.3 22.8 %collective-permute-start.2 = (f32[512,256]{1,0:T(8,128)}, f32[512,256]{1,0:T(8,128)}, u32[]{:S(2)}, u32[]{:S(2)}) collective-permute-start(f32[512,256]{1,0:T(8,128)} %get-tuple-element.16.rest_0_.own_ref), channel_id=1, source_target_pairs={{0,8},{8,16},{16,24},{24,32},{32,40},{40,48},{48,56},{56,64},{64,7... | collective-permute-start | bytes 1572872 | tf_op jit(solution)/shard_map/ppermute | solution.py:22
  15.8 7.0 %collective-permute-start.1 = (f32[16,256]{1,0:T(8,128)S(1)}, f32[16,256]{1,0:T(8,128)S(1)}, u32[]{:S(2)}, u32[]{:S(2)}) collective-permute-start(f32[16,256]{1,0:T(8,128)S(1)} %rows.1), channel_id=1, source_target_pairs={{0,1},{1,0},{2,3},{3,2},{4,5},{5,4},{6,7},{7,6},{8,9},{9,8},{10,11... | collective-permute-start | bytes 49160 | tf_op jit(solution)/shard_map/ppermute | solution.py:248
  18.1 17.8 %collective-permute-start.3 = (f32[1152,256]{1,0:T(8,128)S(1)}, f32[1152,256]{1,0:T(8,128)S(1)}, u32[]{:S(2)}, u32[]{:S(2)}) collective-permute-start(f32[1152,256]{1,0:T(8,128)S(1)} %get-tuple-element.20.rest_1_.own_ref), channel_id=1, source_target_pairs={{0,8},{8,16},{16,24},{24,32},{32,40},{40,48},{48,56},{56,64},{64,7... | collective-permute-start | bytes 3538952 | tf_op jit(solution)/shard_map/ppermute | solution.py:22
  23.5 8.7 %all-to-all-start = ((f32[4,16,256]{2,1,0:T(8,128)}), f32[4,16,256]{2,1,0:T(8,128)S(1)}, u32[]{:S(2)}, u32[]{:S(2)}) async-start(f32[4,16,256]{2,1,0:T(8,128)} %broadcast_in_dim.4), calls=%async_computation | async-start | bytes 131072 | tf_op jit(solution)/shard_map/all_to_all | solution.py:253
  27.6 16.0 %collective-permute-start.4 = (f32[704,256]{1,0:T(8,128)S(1)}, f32[704,256]{1,0:T(8,128)}, u32[]{:S(2)}, u32[]{:S(2)}) collective-permute-start(f32[704,256]{1,0:T(8,128)S(1)} %get-tuple-element.21.rest_2_.own_ref), channel_id=1, source_target_pairs={{0,8},{8,16},{16,24},{24,32},{32,40},{40,48},{48,56},{56,64},{64,7... | collective-permute-start | bytes 2162696 | tf_op jit(solution)/shard_map/ppermute | solution.py:22
  61.1 16.2 %collective-permute-start.5 = (f32[16,2624]{1,0:T(8,128)S(1)}, f32[16,2624]{1,0:T(8,128)S(1)}, u32[]{:S(2)}, u32[]{:S(2)}) collective-permute-start(f32[16,2624]{1,0:T(8,128)S(1)} %factor.1.message_ref), channel_id=1, source_target_pairs={{0,504},{8,0},{16,8},{24,16},{32,24},{40,32},{48,40},{56,48},{64,5... | collective-permute-start | bytes 503816 | tf_op jit(solution)/shard_map/ppermute | solution.py:22

commit v6 on v3

v6 whole, which is shorter than its diff:
```python
import functools

import jax
import jax.numpy as jnp
from jax import lax
from jax.experimental import pallas as pl
from jax.experimental.pallas import tpu as pltpu
from jax.sharding import PartitionSpec as P

HIGH = lax.Precision.HIGHEST
f32 = jnp.float32
bf16 = jnp.bfloat16
step_size = 0.5
VMEM = pl.BlockSpec(memory_space=pltpu.VMEM)
HBM = pl.BlockSpec(memory_space=pltpu.HBM)
NN = (((1,), (0,)), ((), ()))
NT = (((1,), (1,)), ((), ()))


def shifted(block, distance):
    devices = lax.axis_size("blk")
    return lax.ppermute(block, "blk", [(i, (i + distance) % devices) for i in range(devices)])


def planes(x):
    one = x.astype(bf16)
    rest = x - one.astype(f32)
    two = rest.astype(bf16)
    return one, two, (rest - two.astype(f32)).astype(bf16)


def dot(a, b, dims=NN):
    return lax.dot_general(a, b, dims, preferred_element_type=f32)


def product(small, large):
    rows = small[0].shape[0]
    a = dot(jnp.concatenate(small, axis=0), large[0])
    b = dot(jnp.concatenate(small[:2], axis=0), large[1])
    c = dot(small[0], large[2])
    return a[:rows] + ((a[rows : 2 * rows] + b[:rows]) + (a[2 * rows :] + b[rows:] + c))


def tiles(extent, tile):
    out, at = [], 0
    while at < extent:
        size = extent - at if extent - at <= tile + 128 else tile
        out.append((at, size))
        at += size
    return out


def orthonormal_rows(m):
    rank = m.shape[0]
    g = lax.dot_general(m, m, NT, precision=HIGH, preferred_element_type=f32)
    row = lax.broadcasted_iota(jnp.int32, (rank, 1), 0)
    scale = jnp.ones((rank, 1), f32)
    for j in range(rank):
        pivot = g[j : j + 1, j : j + 1]
        factor = jnp.where(row > j, g[:, j : j + 1] * (1.0 / pivot), 0.0)
        scale = jnp.where(row == j, lax.rsqrt(pivot), scale)
        m = m - factor * m[j : j + 1]
        g = g - factor * g[j : j + 1]
    return m * scale


def summed(parts_ref):
    total = parts_ref[0]
    for k in range(1, parts_ref.shape[0]):
        total = total + parts_ref[k]
    return total


def message_kernel(start_ref, own_ref, out_ref, held, sems):
    rank, extent = start_ref.shape
    width = own_ref.shape[1]
    factor = out_ref.at[:, pl.ds(width, extent)]
    fetch = pltpu.make_async_copy(start_ref, factor, sems.at[0])
    fetch.start()
    copies = []
    for k, (at, size) in enumerate(tiles(extent, 512)):
        part = pl.ds(at, size)
        copies.append((at, size, pltpu.make_async_copy(own_ref.at[part], held.at[part], sems.at[1 + k])))
        copies[-1][2].start()
    fetch.wait()
    total = jnp.zeros((rank, width), f32)
    for at, size, copy in copies:
        copy.wait()
        total = total + product(planes(factor[:, pl.ds(at, size)]), planes(held[pl.ds(at, size)]))
    out_ref[:, pl.ds(0, width)] = total


def rows_kernel(left_ref, own_ref, out_ref):
    width = own_ref.shape[1]
    rows = left_ref[:, pl.ds(0, width)]
    for at, size in tiles(own_ref.shape[0], 512):
        rows = rows - product(planes(left_ref[:, pl.ds(width + at, size)]), planes(own_ref[pl.ds(at, size)]))
    for k in range(out_ref.shape[0]):
        out_ref[k] = rows


def right_side(basis):
    rank, width = basis.shape
    zero = jnp.zeros((rank, width), f32)
    p = [x.astype(f32) for x in planes(basis)]
    sides = []
    for kept in (3, 2, 1):
        groups = []
        for k in range(4):
            groups += [p[k] if k < kept else zero, zero]
        sides.append(jnp.transpose(jnp.concatenate(groups, axis=0)).astype(bf16))
    return jnp.concatenate(sides, axis=0)


def columns(difference, right, rank):
    groups = jnp.transpose(dot(jnp.concatenate(difference, axis=1), right))
    return groups[:rank] + (groups[2 * rank : 3 * rank] + groups[4 * rank : 5 * rank])


def basis_kernel(mine_ref, other_ref, out_ref):
    out_ref[...] = orthonormal_rows(mine_ref[...] + other_ref[...])


def fetched(left_ref, held, sems):
    copies = []
    for k, (at, size) in enumerate(tiles(held.shape[0], 768)):
        part = pl.ds(at, size)
        copies.append((part, at, size, pltpu.make_async_copy(left_ref.at[part], held.at[part], sems.at[k])))
        copies[-1][3].start()
    return copies


def power_kernel(basis_ref, own_ref, left_ref, out_ref, held, sems):
    rank, width = basis_ref.shape
    copies = fetched(left_ref, held, sems)
    right = right_side(basis_ref[...])
    total = jnp.zeros((rank, width), f32)
    for part, _, _, copy in copies:
        copy.wait()
        difference = planes(held[part] - own_ref[part])
        total = total + product(planes(columns(difference, right, rank)), difference)
    for k in range(out_ref.shape[0]):
        out_ref[k] = total


def factor_kernel(parts_ref, own_ref, left_ref, out_ref, held, sems):
    copies = fetched(left_ref, held, sems)
    basis = orthonormal_rows(summed(parts_ref))
    rank, width = basis.shape
    right = right_side(basis)
    out_ref[:, pl.ds(0, width)] = basis
    for part, at, size, copy in copies:
        copy.wait()
        difference = planes(held[part] - own_ref[part])
        out_ref[:, pl.ds(width + at, size)] = columns(difference, right, rank)


def change_side(basis):
    b = [x.astype(f32) for x in planes(basis)]
    zero = jnp.zeros_like(b[0])
    return jnp.concatenate([b[0], b[1], b[2], b[0], b[1], b[0], zero, zero], axis=0).astype(bf16)


def change(cols, side):
    c = [x.astype(f32) for x in planes(cols)]
    zero = jnp.zeros_like(cols)
    left = jnp.concatenate([c[0], c[0], c[0], c[1], c[1], c[2], zero, zero], axis=0)
    return dot(jnp.transpose(left).astype(bf16), side)


def half_kernel(message_ref, own_ref, out_ref):
    width = own_ref.shape[1]
    side = change_side(step_size * message_ref[:, pl.ds(0, width)])
    for at, size in tiles(own_ref.shape[0], 768):
        part = pl.ds(at, size)
        out_ref[part] = own_ref[part] + change(message_ref[:, pl.ds(width + at, size)], side)


def final_kernel(message_ref, half_ref, new_ref, cols_ref, held, sems):
    extent, width = half_ref.shape
    copies = [pltpu.make_async_copy(message_ref.at[:, pl.ds(width, extent)], cols_ref, sems.at[0])]
    copies[0].start()
    side = change_side(-step_size * message_ref[:, pl.ds(0, width)])
    for k, (at, size) in enumerate(tiles(extent, 256)):
        part = pl.ds(at, size)
        held[part] = half_ref[part] + change(message_ref[:, pl.ds(width + at, size)], side)
        copies.append(pltpu.make_async_copy(held.at[part], new_ref.at[part], sems.at[1 + k]))
        copies[-1].start()
    for copy in copies:
        copy.wait()


def call(kernel, name, out_shape, out_specs, cost_us, in_specs=None, scratch=(), mib=16):
    return lambda *args: pl.pallas_call(
        kernel,
        out_shape=out_shape,
        in_specs=in_specs or [VMEM] * len(args),
        out_specs=out_specs,
        scratch_shapes=scratch,
        compiler_params=pltpu.CompilerParams(vmem_limit_bytes=mib * 2**20),
        cost_estimate=pl.CostEstimate(flops=int(cost_us * 1.15e9), bytes_accessed=0, transcendentals=0),
        name=name,
    )(*args)


COST = dict(message=2, rows=8, basis=14, power=3, factor=3, half=3, final=3)


def shards(weights, warm_q):
    own = weights.T
    start = warm_q[0].T
    rank, extent = start.shape
    width = own.shape[1]
    ranks = lax.axis_size("tensor")
    shape = lambda *dims: jax.ShapeDtypeStruct(dims, f32)
    whole = shape(rank, width + extent)
    held = pltpu.VMEM((extent, width), f32)
    sems = lambda tile: pltpu.SemaphoreType.DMA((1 + len(tiles(extent, tile)),))

    near = dict(in_specs=[VMEM, VMEM, HBM], scratch=[held, sems(768)])

    message = call(
        message_kernel,
        "message",
        whole,
        VMEM,
        COST["message"],
        in_specs=[HBM, HBM],
        scratch=[held, sems(512)],
        mib=60,
    )(start, own)
    left = shifted(message, 1)
    left_own = shifted(lax.optimization_barrier((own, message))[0], 1)
    copies = call(rows_kernel, "rows", shape(ranks // 2, rank, width), VMEM, COST["rows"])(left, own)
    along_y = [[2 * y + x for y in range(ranks // 2)] for x in range(2)]
    rows = jnp.sum(lax.all_to_all(copies, "tensor", 0, 0, axis_index_groups=along_y, tiled=True), axis=0)
    other = lax.ppermute(rows, "tensor", [(t, t ^ 1) for t in range(ranks)])
    basis = call(basis_kernel, "basis", shape(rank, width), VMEM, COST["basis"], mib=4)(rows, other)
    copies = call(power_kernel, "power", shape(ranks, rank, width), VMEM, COST["power"], **near)(basis, own, left_own)
    parts = lax.all_to_all(copies, "tensor", 0, 0, tiled=True)
    factor = call(factor_kernel, "factor", whole, VMEM, COST["factor"], **near)(parts, own, left_own)
    right = shifted(factor, -1)
    half = call(half_kernel, "half", shape(extent, width), VMEM, COST["half"])(factor, own)
    new, cols = call(
        final_kernel,
        "final",
        (shape(extent, width), shape(rank, extent)),
        (HBM, HBM),
        COST["final"],
        scratch=[held, sems(256)],
    )(right, half)
    return new.T, cols.T[None]


def solution(mesh):
    in_specs = (P("blk", "tensor"), P("blk", "tensor", None))
    out_specs = (P("blk", "tensor"), P("blk", "tensor", None))
    return jax.shard_map(shards, mesh=mesh, in_specs=in_specs, out_specs=out_specs, check_vma=False)
```

time: 80.8 us -> 77.4 us (0.958)
  blocking collectives: 44.9 us -> 18.3 us
  waiting for transfers between devices: 3.75 us -> 27.4 us
  starting transfers between devices: 10.4 us -> 14.6 us
  Pallas kernels: 19.7 us -> 16 us
  local copies, waits for them, and re-layouts: 0.91 us -> 0.01 us
    all_to_all x2, blocking collectives: 44.9 us -> 18.3 us  [the longest x1 11.1 us: shards(): parts = lax.all_to_all(copies, 'tensor', 0, 0, tiled=True)]
    ppermute x0 -> x1, waiting for transfers between devices: none -> 22.1 us  [shards(): other = lax.ppermute(rows, 'tensor', [(t, t ^ 1) for t in range(ranks)])]
    ppermute x0 -> x1, starting transfers between devices: none -> 3.97 us  [shards(): other = lax.ppermute(rows, 'tensor', [(t, t ^ 1) for t in range(ranks)])]
    pallas_call x7, Pallas kernels: 19.7 us -> 16 us  [call(): pl.pallas_call(kernel, out_shape=out_shape, in_specs=in_specs or [VMEM] *...]
    ppermute x3, waiting for transfers between devices: 3.75 us -> 5.38 us  [shifted(): lax.ppermute(block, 'blk', [(i, (i + distance) % devices) for i in range(...]
    unnamed x2, local copies, waits for them, and re-layouts: 0.91 us -> 0.01 us
  transfers between devices with their start and end apart: 3 -> 4, of which waited for: 2 -> 3; matrix products, arithmetic and copies ran while one was open for 0% -> 0% of each run, Pallas kernels for 8% -> 4%
where the time goes in v6:
time: 77.4 us; the launch traced here: 77.1 us
  waiting for transfers between devices  27.4 us (35%)
  blocking collectives  18.3 us (24%)
  Pallas kernels  16 us (21%)
  starting transfers between devices  14.6 us (19%)
    ppermute x1, waiting for transfers between devices, shards(): other = lax.ppermute(rows, 'tensor', [(t, t ^ 1) for t in range(ranks)])  22.1 us
    pallas_call x7, Pallas kernels, call(): pl.pallas_call(kernel, out_shape=out_shape, in_specs=in_specs or [VMEM] *...  16 us
    all_to_all x1, blocking collectives, shards(): parts = lax.all_to_all(copies, 'tensor', 0, 0, tiled=True)  11.1 us
    ppermute x3, starting transfers between devices, shifted(): lax.ppermute(block, 'blk', [(i, (i + distance) % devices) for i in range(...  10.6 us
    all_to_all x1, blocking collectives, shards(): lax.all_to_all(copies, 'tensor', 0, 0, axis_index_groups=along_y, tiled=T...  7.24 us
    ppermute x3, waiting for transfers between devices, shifted(): lax.ppermute(block, 'blk', [(i, (i + distance) % devices) for i in range(...  5.38 us
    ppermute x1, starting transfers between devices, shards(): other = lax.ppermute(rows, 'tensor', [(t, t ^ 1) for t in range(ranks)])  3.97 us
  transfers between devices with their start and end apart: 4, of which 3 were waited for; matrix products, arithmetic and copies ran while one was open for 0% of the time, Pallas kernels for 4%

profile of v6, /device:TPU:1, one launch (start us, length us, event | category | flops | bytes accessed | tf_op | source)
XLA Modules:
  0.0 77.1 jit_solution(18184506743754234933)
XLA Ops:
  0.6 0.0 copy-start
  0.6 3.2 %message.1 = f32[16,2624]{1,0:T(8,128)} custom-call(f32[16,2368]{1,0:T(8,128)} %bitcast.14, f32[2368,256]{1,0:T(8,128)} %bitcast.8), custom_call_target="tpu_custom_call" | custom-call | flops 2300000000 | tf_op jit(solution)/shard_map/message/pallas_call | solution.py:194
  3.9 4.9 %collective-permute-start = (f32[16,2624]{1,0:T(8,128)}, f32[16,2624]{1,0:T(8,128)S(1)}, u32[]{:S(2)}, u32[]{:S(2)}) collective-permute-start(f32[16,2624]{1,0:T(8,128)} %message.1), channel_id=1, source_target_pairs={{0,8},{8,16},{16,24},{24,32},{32,40},{40,48},{48,56},{56,64},{64,7... | collective-permute-start | bytes 503816 | tf_op jit(solution)/shard_map/ppermute | solution.py:22
  8.8 0.0 copy-done
  8.8 1.9 %collective-permute-start.2 = (f32[2368,256]{1,0:T(8,128)S(1)}, f32[2368,256]{1,0:T(8,128)}, u32[]{:S(2)}, u32[]{:S(2)}) collective-permute-start(f32[2368,256]{1,0:T(8,128)S(1)} %bitcast.9), channel_id=1, source_target_pairs={{0,8},{8,16},{16,24},{24,32},{32,40},{40,48},{48,56},{56,64},{64,7... | collective-permute-start | bytes 7274504 | tf_op jit(solution)/shard_map/ppermute | solution.py:22
  10.8 3.0 %collective-permute-done.left_ref = f32[16,2624]{1,0:T(8,128)S(1)} collective-permute-done((f32[16,2624]{1,0:T(8,128)}, f32[16,2624]{1,0:T(8,128)S(1)}, u32[]{:S(2)}, u32[]{:S(2)}) %collective-permute-start) | collective-permute-done | bytes 167968 | tf_op jit(solution)/shard_map/ppermute | solution.py:22
  13.8 0.8 rows.1
  14.5 7.2 %all_to_all.10 = f32[4,16,256]{2,1,0:T(8,128)S(1)} all-to-all(f32[4,16,256]{2,1,0:T(8,128)S(1)} %rows.1), channel_id=1, replica_groups={{0,2,4,6},{1,3,5,7},{8,10,12,14},{9,11,13,15},{16,18,20,22},{17,19,21,2..., dimensions={0} | all-to-all | bytes 131072 | tf_op jit(solution)/shard_map/all_to_all | solution.py:236
  21.8 4.0 %collective-permute-start.1 = (f32[16,256]{1,0:T(8,128)S(1)}, f32[16,256]{1,0:T(8,128)S(1)}, u32[]{:S(2)}, u32[]{:S(2)}) collective-permute-start(f32[16,256]{1,0:T(8,128)S(1)} %reduce_sum.9.mine_ref), channel_id=1, source_target_pairs={{0,1},{1,0},{2,3},{3,2},{4,5},{5,4},{6,7},{7,6},{8,9},{9,8},{10,11... | collective-permute-start | bytes 49160 | tf_op jit(solution)/shard_map/ppermute | solution.py:237
  25.8 22.1 %collective-permute-done.1.other_ref = f32[16,256]{1,0:T(8,128)S(1)} collective-permute-done((f32[16,256]{1,0:T(8,128)S(1)}, f32[16,256]{1,0:T(8,128)S(1)}, u32[]{:S(2)}, u32[]{:S(2)}) %collective-permute-start.1) | collective-permute-done | bytes 16416 | tf_op jit(solution)/shard_map/ppermute | solution.py:237
  47.8 1.5 %basis.1.basis_ref = f32[16,256]{1,0:T(8,128)S(1)} custom-call(f32[16,256]{1,0:T(8,128)S(1)} %reduce_sum.9.mine_ref, f32[16,256]{1,0:T(8,128)S(1)} %collective-permute-done.1.other_ref), custom_call_target="tpu_custom_call" | custom-call | flops 16099999744 | tf_op jit(solution)/shard_map/basis/pallas_call | solution.py:194
  49.3 0.0 collective-permute-done.2.left_ref
  49.3 4.3 %power.1 = f32[8,16,256]{2,1,0:T(8,128)S(1)} custom-call(f32[16,256]{1,0:T(8,128)S(1)} %basis.1.basis_ref, f32[2368,256]{1,0:T(8,128)S(1)} %bitcast.11, f32[2368,256]{1,0:T(8,128)} %collective-permute-done.2.left_ref), custom_call_target="tpu_custom_call" | custom-call | flops 3449999872 | tf_op jit(solution)/shard_map/power/pallas_call | solution.py:194
  53.6 11.1 %all_to_all.11.parts_ref = f32[8,16,256]{2,1,0:T(8,128)S(1)} all-to-all(f32[8,16,256]{2,1,0:T(8,128)S(1)} %power.1), channel_id=1, replica_groups=mesh['blk'=64,'tensor'=8] {'tensor'}, dimensions={0} | all-to-all | bytes 262144 | tf_op jit(solution)/shard_map/all_to_all | solution.py:240
  64.7 3.9 %factor.1.message_ref = f32[16,2624]{1,0:T(8,128)S(1)} custom-call(f32[8,16,256]{2,1,0:T(8,128)S(1)} %all_to_all.11.parts_ref, f32[2368,256]{1,0:T(8,128)S(1)} %bitcast.12, f32[2368,256]{1,0:T(8,128)} %collective-permute-done.2.left_ref), custom_call_target="tpu_custom_call" | custom-call | flops 3449999872 | tf_op jit(solution)/shard_map/factor/pallas_call | solution.py:194
  68.6 3.8 %collective-permute-start.3 = (f32[16,2624]{1,0:T(8,128)S(1)}, f32[16,2624]{1,0:T(8,128)S(1)}, u32[]{:S(2)}, u32[]{:S(2)}) collective-permute-start(f32[16,2624]{1,0:T(8,128)S(1)} %factor.1.message_ref), channel_id=1, source_target_pairs={{0,504},{8,0},{16,8},{24,16},{32,24},{40,32},{48,40},{56,48},{64,5... | collective-permute-start | bytes 503816 | tf_op jit(solution)/shard_map/ppermute | solution.py:22
  72.4 0.6 half.1.half_ref
  73.0 2.4 %collective-permute-done.3.message_ref = f32[16,2624]{1,0:T(8,128)S(1)} collective-permute-done((f32[16,2624]{1,0:T(8,128)S(1)}, f32[16,2624]{1,0:T(8,128)S(1)}, u32[]{:S(2)}, u32[]{:S(2)}) %collective-permute-start.3) | collective-permute-done | bytes 167968 | tf_op jit(solution)/shard_map/ppermute | solution.py:22
  75.4 1.8 %final.1 = (f32[2368,256]{1,0:T(8,128)}, f32[16,2368]{1,0:T(8,128)}) custom-call(f32[16,2624]{1,0:T(8,128)S(1)} %collective-permute-done.3.message_ref, f32[2368,256]{1,0:T(8,128)S(1)} %half.1.half_ref), custom_call_target="tpu_custom_call" | custom-call | flops 3449999872 | tf_op jit(solution)/shard_map/final/pallas_call | solution.py:194
  (1 shorter events, 0.0 us)
Async XLA Ops:
  0.6 8.2 %copy-start = (f32[256,2368]{0,1:T(8,128)S(1)}, f32[256,2368]{0,1:T(8,128)}, u32[]{:S(2)}) copy-start(f32[256,2368]{0,1:T(8,128)} %param.2) | copy-start | bytes 7274500
  3.9 9.9 %collective-permute-start = (f32[16,2624]{1,0:T(8,128)}, f32[16,2624]{1,0:T(8,128)S(1)}, u32[]{:S(2)}, u32[]{:S(2)}) collective-permute-start(f32[16,2624]{1,0:T(8,128)} %message.1), channel_id=1, source_target_pairs={{0,8},{8,16},{16,24},{24,32},{32,40},{40,48},{48,56},{56,64},{64,7... | collective-permute-start | bytes 503816 | tf_op jit(solution)/shard_map/ppermute | solution.py:22
  8.8 40.5 %collective-permute-start.2 = (f32[2368,256]{1,0:T(8,128)S(1)}, f32[2368,256]{1,0:T(8,128)}, u32[]{:S(2)}, u32[]{:S(2)}) collective-permute-start(f32[2368,256]{1,0:T(8,128)S(1)} %bitcast.9), channel_id=1, source_target_pairs={{0,8},{8,16},{16,24},{24,32},{32,40},{40,48},{48,56},{56,64},{64,7... | collective-permute-start | bytes 7274504 | tf_op jit(solution)/shard_map/ppermute | solution.py:22
  21.8 26.0 %collective-permute-start.1 = (f32[16,256]{1,0:T(8,128)S(1)}, f32[16,256]{1,0:T(8,128)S(1)}, u32[]{:S(2)}, u32[]{:S(2)}) collective-permute-start(f32[16,256]{1,0:T(8,128)S(1)} %reduce_sum.9.mine_ref), channel_id=1, source_target_pairs={{0,1},{1,0},{2,3},{3,2},{4,5},{5,4},{6,7},{7,6},{8,9},{9,8},{10,11... | collective-permute-start | bytes 49160 | tf_op jit(solution)/shard_map/ppermute | solution.py:237
  68.6 6.7 %collective-permute-start.3 = (f32[16,2624]{1,0:T(8,128)S(1)}, f32[16,2624]{1,0:T(8,128)S(1)}, u32[]{:S(2)}, u32[]{:S(2)}) collective-permute-start(f32[16,2624]{1,0:T(8,128)S(1)} %factor.1.message_ref), channel_id=1, source_target_pairs={{0,504},{8,0},{16,8},{24,16},{32,24},{40,32},{48,40},{56,48},{64,5... | collective-permute-start | bytes 503816 | tf_op jit(solution)/shard_map/ppermute | solution.py:22

commit v7 on v6

--- a/solution.py
+++ b/solution.py
@@ -117,42 +117,44 @@
     return groups[:rank] + (groups[2 * rank : 3 * rank] + groups[4 * rank : 5 * rank])
 
 
-def basis_kernel(mine_ref, other_ref, out_ref):
-    out_ref[...] = orthonormal_rows(mine_ref[...] + other_ref[...])
-
-
-def fetched(left_ref, held, sems):
-    copies = []
-    for k, (at, size) in enumerate(tiles(held.shape[0], 768)):
-        part = pl.ds(at, size)
-        copies.append((part, at, size, pltpu.make_async_copy(left_ref.at[part], held.at[part], sems.at[k])))
-        copies[-1][3].start()
-    return copies
-
-
-def power_kernel(basis_ref, own_ref, left_ref, out_ref, held, sems):
-    rank, width = basis_ref.shape
-    copies = fetched(left_ref, held, sems)
-    right = right_side(basis_ref[...])
-    total = jnp.zeros((rank, width), f32)
-    for part, _, _, copy in copies:
-        copy.wait()
-        difference = planes(held[part] - own_ref[part])
+def powered(total, basis, own_ref, left_ref, first):
+    rank = basis.shape[0]
+    right = right_side(basis)
+    for at, size in tiles(left_ref.shape[0], 768):
+        difference = planes(left_ref[pl.ds(at, size)] - own_ref[pl.ds(first + at, size)])
         total = total + product(planes(columns(difference, right, rank)), difference)
+    return total
+
+
+def sum_kernel(parts_ref, out_ref):
+    out_ref[...] = summed(parts_ref)
+
+
+def basis_kernel(mine_ref, other_ref, own_ref, left_ref, basis_ref, total_ref):
+    basis = orthonormal_rows(mine_ref[...] + other_ref[...])
+    basis_ref[...] = basis
+    total_ref[...] = powered(jnp.zeros(basis.shape, f32), basis, own_ref, left_ref, 0)
+
+
+def power_kernel(basis_ref, total_ref, own_ref, left_ref, out_ref):
+    first = own_ref.shape[0] - left_ref.shape[0]
+    total = powered(total_ref[...], basis_ref[...], own_ref, left_ref, first)
     for k in range(out_ref.shape[0]):
         out_ref[k] = total
 
 
-def factor_kernel(parts_ref, own_ref, left_ref, out_ref, held, sems):
-    copies = fetched(left_ref, held, sems)
+def factor_kernel(parts_ref, own_ref, *rest):
+    *left_refs, out_ref = rest
     basis = orthonormal_rows(summed(parts_ref))
     rank, width = basis.shape
     right = right_side(basis)
     out_ref[:, pl.ds(0, width)] = basis
-    for part, at, size, copy in copies:
-        copy.wait()
-        difference = planes(held[part] - own_ref[part])
-        out_ref[:, pl.ds(width + at, size)] = columns(difference, right, rank)
+    first = 0
+    for left_ref in left_refs:
+        for at, size in tiles(left_ref.shape[0], 768):
+            difference = planes(left_ref[pl.ds(at, size)] - own_ref[pl.ds(first + at, size)])
+            out_ref[:, pl.ds(width + first + at, size)] = columns(difference, right, rank)
+        first += left_ref.shape[0]
 
 
 def change_side(basis):
@@ -203,7 +205,8 @@
     )(*args)
 
 
-COST = dict(message=2, rows=8, basis=14, power=3, factor=3, half=3, final=3)
+COST = dict(message=2, sum=1, rows=20, basis=14, power=3, factor=3, half=3, final=3)
+FIRST = 1536
 
 
 def shards(weights, warm_q):
@@ -217,8 +220,6 @@
     held = pltpu.VMEM((extent, width), f32)
     sems = lambda tile: pltpu.SemaphoreType.DMA((1 + len(tiles(extent, tile)),))
 
-    near = dict(in_specs=[VMEM, VMEM, HBM], scratch=[held, sems(768)])
-
     message = call(
         message_kernel,
         "message",
@@ -229,16 +230,23 @@
         scratch=[held, sems(512)],
         mib=60,
     )(start, own)
+    own, message = lax.optimization_barrier((own, message))
     left = shifted(message, 1)
-    left_own = shifted(lax.optimization_barrier((own, message))[0], 1)
+    left_first = shifted(own[:FIRST], 1)
     copies = call(rows_kernel, "rows", shape(ranks // 2, rank, width), VMEM, COST["rows"])(left, own)
     along_y = [[2 * y + x for y in range(ranks // 2)] for x in range(2)]
-    rows = jnp.sum(lax.all_to_all(copies, "tensor", 0, 0, axis_index_groups=along_y, tiled=True), axis=0)
+    parts = lax.all_to_all(copies, "tensor", 0, 0, axis_index_groups=along_y, tiled=True)
+    rows = call(sum_kernel, "sum", shape(rank, width), VMEM, COST["sum"], mib=4)(parts)
     other = lax.ppermute(rows, "tensor", [(t, t ^ 1) for t in range(ranks)])
-    basis = call(basis_kernel, "basis", shape(rank, width), VMEM, COST["basis"], mib=4)(rows, other)
-    copies = call(power_kernel, "power", shape(ranks, rank, width), VMEM, COST["power"], **near)(basis, own, left_own)
+    rest, rows = lax.optimization_barrier((own[FIRST:], rows))
+    left_rest = shifted(rest, 1)
+    both = (shape(rank, width),) * 2
+    basis, total = call(basis_kernel, "basis", both, (VMEM, VMEM), COST["basis"])(rows, other, own, left_first)
+    copies = call(power_kernel, "power", shape(ranks, rank, width), VMEM, COST["power"])(
+        basis, total, own, left_rest
+    )
     parts = lax.all_to_all(copies, "tensor", 0, 0, tiled=True)
-    factor = call(factor_kernel, "factor", whole, VMEM, COST["factor"], **near)(parts, own, left_own)
+    factor = call(factor_kernel, "factor", whole, VMEM, COST["factor"])(parts, own, left_first, left_rest)
     right = shifted(factor, -1)
     half = call(half_kernel, "half", shape(extent, width), VMEM, COST["half"])(factor, own)
     new, cols = call(

time: 77.4 us -> 71.6 us (0.925)
  waiting for transfers between devices: 27.4 us -> 10.6 us
  starting transfers between devices: 14.6 us -> 27.9 us
  Pallas kernels: 16 us -> 13.7 us
    ppermute x1, waiting for transfers between devices: 22.1 us -> 7.28 us  [shards(): other = lax.ppermute(rows, 'tensor', [(t, t ^ 1) for t in range(ranks)])]
    ppermute x3 -> x4, starting transfers between devices: 10.6 us -> 23.9 us  [shifted(): lax.ppermute(block, 'blk', [(i, (i + distance) % devices) for i in range(...]
    pallas_call x7 -> x8, Pallas kernels: 16 us -> 13.7 us  [call(): pl.pallas_call(kernel, out_shape=out_shape, in_specs=in_specs or [VMEM] *...]
    ppermute x3 -> x4, waiting for transfers between devices: 5.38 us -> 3.36 us  [shifted(): lax.ppermute(block, 'blk', [(i, (i + distance) % devices) for i in range(...]
  transfers between devices with their start and end apart: 4 -> 5, of which waited for: 3 -> 3; matrix products, arithmetic and copies ran while one was open for 0% -> 0% of each run, Pallas kernels for 4% -> 7%
where the time goes in v7:
time: 71.6 us; the launch traced here: 71.3 us
  starting transfers between devices  27.9 us (39%)
  blocking collectives  18.2 us (25%)
  Pallas kernels  13.7 us (19%)
  waiting for transfers between devices  10.6 us (15%)
  between operations  0.74 us (1%)
    ppermute x4, starting transfers between devices, shifted(): lax.ppermute(block, 'blk', [(i, (i + distance) % devices) for i in range(...  23.9 us
    pallas_call x8, Pallas kernels, call(): pl.pallas_call(kernel, out_shape=out_shape, in_specs=in_specs or [VMEM] *...  13.7 us
    all_to_all x1, blocking collectives, shards(): parts = lax.all_to_all(copies, 'tensor', 0, 0, tiled=True)  11 us
    ppermute x1, waiting for transfers between devices, shards(): other = lax.ppermute(rows, 'tensor', [(t, t ^ 1) for t in range(ranks)])  7.28 us
    all_to_all x1, blocking collectives, shards(): lax.all_to_all(copies, 'tensor', 0, 0, axis_index_groups=along_y, tiled=T...  7.14 us
    ppermute x1, starting transfers between devices, shards(): other = lax.ppermute(rows, 'tensor', [(t, t ^ 1) for t in range(ranks)])  3.96 us
    ppermute x4, waiting for transfers between devices, shifted(): lax.ppermute(block, 'blk', [(i, (i + distance) % devices) for i in range(...  3.36 us
  transfers between devices with their start and end apart: 5, of which 3 were waited for; matrix products, arithmetic and copies ran while one was open for 0% of the time, Pallas kernels for 7%

profile of v7, /device:TPU:1, one launch (start us, length us, event | category | flops | bytes accessed | tf_op | source)
XLA Modules:
  0.0 71.3 jit_solution(9531157892150190493)
XLA Ops:
  0.6 0.0 copy-start
  0.6 3.2 %message.1 = f32[16,2624]{1,0:T(8,128)} custom-call(f32[16,2368]{1,0:T(8,128)} %bitcast.16, f32[2368,256]{1,0:T(8,128)} %bitcast.8), custom_call_target="tpu_custom_call" | custom-call | flops 2300000000 | tf_op jit(solution)/shard_map/message/pallas_call | solution.py:196
  3.9 4.9 %collective-permute-start = (f32[16,2624]{1,0:T(8,128)}, f32[16,2624]{1,0:T(8,128)S(1)}, u32[]{:S(2)}, u32[]{:S(2)}) collective-permute-start(f32[16,2624]{1,0:T(8,128)} %message.1), channel_id=1, source_target_pairs={{0,8},{8,16},{16,24},{24,32},{32,40},{40,48},{48,56},{56,64},{64,7... | collective-permute-start | bytes 503816 | tf_op jit(solution)/shard_map/ppermute | solution.py:22
  8.8 0.0 copy-done
  8.8 0.1 slice.7
  8.9 1.9 %collective-permute-start.2 = (f32[1536,256]{1,0:T(8,128)S(1)}, f32[1536,256]{1,0:T(8,128)S(1)}, u32[]{:S(2)}, u32[]{:S(2)}) collective-permute-start(f32[1536,256]{1,0:T(8,128)S(1)} %slice.7), channel_id=1, source_target_pairs={{0,8},{8,16},{16,24},{24,32},{32,40},{40,48},{48,56},{56,64},{64,7... | collective-permute-start | bytes 4718600 | tf_op jit(solution)/shard_map/ppermute | solution.py:22
  10.9 2.9 %collective-permute-done.left_ref = f32[16,2624]{1,0:T(8,128)S(1)} collective-permute-done((f32[16,2624]{1,0:T(8,128)}, f32[16,2624]{1,0:T(8,128)S(1)}, u32[]{:S(2)}, u32[]{:S(2)}) %collective-permute-start) | collective-permute-done | bytes 167968 | tf_op jit(solution)/shard_map/ppermute | solution.py:22
  13.8 0.8 %rows.1 = f32[4,16,256]{2,1,0:T(8,128)S(1)} custom-call(f32[16,2624]{1,0:T(8,128)S(1)} %collective-permute-done.left_ref, f32[2368,256]{1,0:T(8,128)S(1)} %bitcast.10), custom_call_target="tpu_custom_call" | custom-call | flops 23000000512 | tf_op jit(solution)/shard_map/rows/pallas_call | solution.py:196
  14.5 7.1 %all_to_all.10.parts_ref = f32[4,16,256]{2,1,0:T(8,128)S(1)} all-to-all(f32[4,16,256]{2,1,0:T(8,128)S(1)} %rows.1), channel_id=1, replica_groups={{0,2,4,6},{1,3,5,7},{8,10,12,14},{9,11,13,15},{16,18,20,22},{17,19,21,2..., dimensions={0} | all-to-all | bytes 131072 | tf_op jit(solution)/shard_map/all_to_all | solution.py:238
  21.7 4.0 %collective-permute-start.1 = (f32[16,256]{1,0:T(8,128)S(1)}, f32[16,256]{1,0:T(8,128)S(1)}, u32[]{:S(2)}, u32[]{:S(2)}) collective-permute-start(f32[16,256]{1,0:T(8,128)S(1)} %sum.1.mine_ref), channel_id=1, source_target_pairs={{0,1},{1,0},{2,3},{3,2},{4,5},{5,4},{6,7},{7,6},{8,9},{9,8},{10,11... | collective-permute-start | bytes 49160 | tf_op jit(solution)/shard_map/ppermute | solution.py:240
  25.6 0.1 slice.6
  25.7 5.7 %collective-permute-start.3 = (f32[832,256]{1,0:T(8,128)S(1)}, f32[832,256]{1,0:T(8,128)S(1)}, u32[]{:S(2)}, u32[]{:S(2)}) collective-permute-start(f32[832,256]{1,0:T(8,128)S(1)} %slice.6), channel_id=1, source_target_pairs={{0,8},{8,16},{16,24},{24,32},{32,40},{40,48},{48,56},{56,64},{64,7... | collective-permute-start | bytes 2555912 | tf_op jit(solution)/shard_map/ppermute | solution.py:22
  31.4 7.3 %collective-permute-done.1.other_ref = f32[16,256]{1,0:T(8,128)S(1)} collective-permute-done((f32[16,256]{1,0:T(8,128)S(1)}, f32[16,256]{1,0:T(8,128)S(1)}, u32[]{:S(2)}, u32[]{:S(2)}) %collective-permute-start.1) | collective-permute-done | bytes 16416 | tf_op jit(solution)/shard_map/ppermute | solution.py:240
  38.7 0.0 collective-permute-done.2.left_ref.rest_0_
  38.7 3.4 %basis.1 = (f32[16,256]{1,0:T(8,128)S(1)}, f32[16,256]{1,0:T(8,128)S(1)}) custom-call(f32[16,256]{1,0:T(8,128)S(1)} %sum.1.mine_ref, f32[16,256]{1,0:T(8,128)S(1)} %collective-permute-done.1.other_ref, f32[2368,256]{1,0:T(8,128)S(1)} %bitcast.12, f32[1536,256]{1,0:T(8,128)S(1)} %collective-permute-done.2.left_ref.rest_0_), custom_call_target="tpu_custom_call" | custom-call | flops 16099999744 | tf_op jit(solution)/shard_map/basis/pallas_call | solution.py:196
  42.1 0.0 collective-permute-done.3.left_ref.rest_1_
  42.1 1.2 %power.1 = f32[8,16,256]{2,1,0:T(8,128)S(1)} custom-call(f32[16,256]{1,0:T(8,128)S(1)} %get-tuple-element.13.basis_ref, f32[16,256]{1,0:T(8,128)S(1)} %get-tuple-element.14.total_ref, f32[2368,256]{1,0:T(8,128)S(1)} %bitcast.13, f32[832,256]{1,0:T(8,128)S(1)} %collective-permute-done.3.left_ref.rest_1_), custom_call_target="tpu_custom_call" | custom-call | flops 3449999872 | tf_op jit(solution)/shard_map/power/pallas_call | solution.py:196
  43.3 11.0 %all_to_all.11.parts_ref = f32[8,16,256]{2,1,0:T(8,128)S(1)} all-to-all(f32[8,16,256]{2,1,0:T(8,128)S(1)} %power.1), channel_id=1, replica_groups=mesh['blk'=64,'tensor'=8] {'tensor'}, dimensions={0} | all-to-all | bytes 262144 | tf_op jit(solution)/shard_map/all_to_all | solution.py:248
  54.4 2.8 %factor.1.message_ref = f32[16,2624]{1,0:T(8,128)S(1)} custom-call(f32[8,16,256]{2,1,0:T(8,128)S(1)} %all_to_all.11.parts_ref, f32[2368,256]{1,0:T(8,128)S(1)} %bitcast.14, f32[1536,256]{1,0:T(8,128)S(1)} %collective-permute-done.2.left_ref.rest_0_, f32[832,256]{1,0:T(8,128)S(1)} %collective-permute-done.3.left_ref.rest_1_), custom_call_target="tpu_custom_call" | custom-call | flops 3449999872 | tf_op jit(solution)/shard_map/factor/pallas_call | solution.py:196
  57.1 11.3 %collective-permute-start.4 = (f32[16,2624]{1,0:T(8,128)S(1)}, f32[16,2624]{1,0:T(8,128)S(1)}, u32[]{:S(2)}, u32[]{:S(2)}) collective-permute-start(f32[16,2624]{1,0:T(8,128)S(1)} %factor.1.message_ref), channel_id=1, source_target_pairs={{0,504},{8,0},{16,8},{24,16},{32,24},{40,32},{48,40},{56,48},{64,5... | collective-permute-start | bytes 503816 | tf_op jit(solution)/shard_map/ppermute | solution.py:22
  68.5 0.6 half.1.half_ref
  69.0 0.5 collective-permute-done.4.message_ref
  69.5 1.8 %final.1 = (f32[2368,256]{1,0:T(8,128)}, f32[16,2368]{1,0:T(8,128)}) custom-call(f32[16,2624]{1,0:T(8,128)S(1)} %collective-permute-done.4.message_ref, f32[2368,256]{1,0:T(8,128)S(1)} %half.1.half_ref), custom_call_target="tpu_custom_call" | custom-call | flops 3449999872 | tf_op jit(solution)/shard_map/final/pallas_call | solution.py:196
  (1 shorter events, 0.0 us)
Async XLA Ops:
  0.6 8.2 %copy-start = (f32[256,2368]{0,1:T(8,128)S(1)}, f32[256,2368]{0,1:T(8,128)}, u32[]{:S(2)}) copy-start(f32[256,2368]{0,1:T(8,128)} %param.2) | copy-start | bytes 7274500
  3.9 9.9 %collective-permute-start = (f32[16,2624]{1,0:T(8,128)}, f32[16,2624]{1,0:T(8,128)S(1)}, u32[]{:S(2)}, u32[]{:S(2)}) collective-permute-start(f32[16,2624]{1,0:T(8,128)} %message.1), channel_id=1, source_target_pairs={{0,8},{8,16},{16,24},{24,32},{32,40},{40,48},{48,56},{56,64},{64,7... | collective-permute-start | bytes 503816 | tf_op jit(solution)/shard_map/ppermute | solution.py:22
  8.9 29.8 %collective-permute-start.2 = (f32[1536,256]{1,0:T(8,128)S(1)}, f32[1536,256]{1,0:T(8,128)S(1)}, u32[]{:S(2)}, u32[]{:S(2)}) collective-permute-start(f32[1536,256]{1,0:T(8,128)S(1)} %slice.7), channel_id=1, source_target_pairs={{0,8},{8,16},{16,24},{24,32},{32,40},{40,48},{48,56},{56,64},{64,7... | collective-permute-start | bytes 4718600 | tf_op jit(solution)/shard_map/ppermute | solution.py:22
  21.7 17.0 %collective-permute-start.1 = (f32[16,256]{1,0:T(8,128)S(1)}, f32[16,256]{1,0:T(8,128)S(1)}, u32[]{:S(2)}, u32[]{:S(2)}) collective-permute-start(f32[16,256]{1,0:T(8,128)S(1)} %sum.1.mine_ref), channel_id=1, source_target_pairs={{0,1},{1,0},{2,3},{3,2},{4,5},{5,4},{6,7},{7,6},{8,9},{9,8},{10,11... | collective-permute-start | bytes 49160 | tf_op jit(solution)/shard_map/ppermute | solution.py:240
  25.7 16.4 %collective-permute-start.3 = (f32[832,256]{1,0:T(8,128)S(1)}, f32[832,256]{1,0:T(8,128)S(1)}, u32[]{:S(2)}, u32[]{:S(2)}) collective-permute-start(f32[832,256]{1,0:T(8,128)S(1)} %slice.6), channel_id=1, source_target_pairs={{0,8},{8,16},{16,24},{24,32},{32,40},{40,48},{48,56},{56,64},{64,7... | collective-permute-start | bytes 2555912 | tf_op jit(solution)/shard_map/ppermute | solution.py:22
  57.1 12.4 %collective-permute-start.4 = (f32[16,2624]{1,0:T(8,128)S(1)}, f32[16,2624]{1,0:T(8,128)S(1)}, u32[]{:S(2)}, u32[]{:S(2)}) collective-permute-start(f32[16,2624]{1,0:T(8,128)S(1)} %factor.1.message_ref), channel_id=1, source_target_pairs={{0,504},{8,0},{16,8},{24,16},{32,24},{40,32},{48,40},{56,48},{64,5... | collective-permute-start | bytes 503816 | tf_op jit(solution)/shard_map/ppermute | solution.py:22

commit v8 on v7

--- a/solution.py
+++ b/solution.py
@@ -120,7 +120,7 @@
 def powered(total, basis, own_ref, left_ref, first):
     rank = basis.shape[0]
     right = right_side(basis)
-    for at, size in tiles(left_ref.shape[0], 768):
+    for at, size in tiles(left_ref.shape[0], 896):
         difference = planes(left_ref[pl.ds(at, size)] - own_ref[pl.ds(first + at, size)])
         total = total + product(planes(columns(difference, right, rank)), difference)
     return total
@@ -151,7 +151,7 @@
     out_ref[:, pl.ds(0, width)] = basis
     first = 0
     for left_ref in left_refs:
-        for at, size in tiles(left_ref.shape[0], 768):
+        for at, size in tiles(left_ref.shape[0], 896):
             difference = planes(left_ref[pl.ds(at, size)] - own_ref[pl.ds(first + at, size)])
             out_ref[:, pl.ds(width + first + at, size)] = columns(difference, right, rank)
         first += left_ref.shape[0]
@@ -173,7 +173,7 @@
 def half_kernel(message_ref, own_ref, out_ref):
     width = own_ref.shape[1]
     side = change_side(step_size * message_ref[:, pl.ds(0, width)])
-    for at, size in tiles(own_ref.shape[0], 768):
+    for at, size in tiles(own_ref.shape[0], 896):
         part = pl.ds(at, size)
         out_ref[part] = own_ref[part] + change(message_ref[:, pl.ds(width + at, size)], side)
 
@@ -206,7 +206,7 @@
 
 
 COST = dict(message=2, sum=1, rows=20, basis=14, power=3, factor=3, half=3, final=3)
-FIRST = 1536
+FIRST = 1792
 
 
 def shards(weights, warm_q):
@@ -220,17 +220,16 @@
     held = pltpu.VMEM((extent, width), f32)
     sems = lambda tile: pltpu.SemaphoreType.DMA((1 + len(tiles(extent, tile)),))
 
-    message = call(
+    message, own = call(
         message_kernel,
         "message",
-        whole,
-        VMEM,
+        (whole, shape(extent, width)),
+        (VMEM, VMEM),
         COST["message"],
         in_specs=[HBM, HBM],
-        scratch=[held, sems(512)],
-        mib=60,
+        scratch=[sems(512)],
+        mib=51,
     )(start, own)
-    own, message = lax.optimization_barrier((own, message))
     left = shifted(message, 1)
     left_first = shifted(own[:FIRST], 1)
     copies = call(rows_kernel, "rows", shape(ranks // 2, rank, width), VMEM, COST["rows"])(left, own)

time: 71.6 us -> 75.2 us (1.050)
  starting transfers between devices: 27.9 us -> 20.4 us
  blocking collectives: 18.2 us -> 24.5 us
  waiting for transfers between devices: 10.6 us -> 15.3 us
  local copies, waits for them, and re-layouts: 0.16 us -> 1.07 us
  Pallas kernels: 13.7 us -> 12.9 us
    ppermute x4, starting transfers between devices: 23.9 us -> 16.5 us  [shifted(): lax.ppermute(block, 'blk', [(i, (i + distance) % devices) for i in range(...]
    all_to_all x1, blocking collectives: 11 us -> 17.4 us  [shards(): parts = lax.all_to_all(copies, 'tensor', 0, 0, tiled=True)]
    ppermute x1, waiting for transfers between devices: 7.28 us -> 10.3 us  [shards(): other = lax.ppermute(rows, 'tensor', [(t, t ^ 1) for t in range(ranks)])]
    ppermute x4, waiting for transfers between devices: 3.36 us -> 5 us  [shifted(): lax.ppermute(block, 'blk', [(i, (i + distance) % devices) for i in range(...]
    unnamed x2, local copies, waits for them, and re-layouts: 0.01 us -> 0.91 us
    pallas_call x8, Pallas kernels: 13.7 us -> 12.9 us  [call(): pl.pallas_call(kernel, out_shape=out_shape, in_specs=in_specs or [VMEM] *...]
where the time goes in v8:
time: 75.2 us; the launch traced here: 74.9 us
  blocking collectives  24.5 us (33%)
  starting transfers between devices  20.4 us (27%)
  waiting for transfers between devices  15.3 us (20%)
  Pallas kernels  12.9 us (17%)
  local copies, waits for them, and re-layouts  1.07 us (1%)
    all_to_all x1, blocking collectives, shards(): parts = lax.all_to_all(copies, 'tensor', 0, 0, tiled=True)  17.4 us
    ppermute x4, starting transfers between devices, shifted(): lax.ppermute(block, 'blk', [(i, (i + distance) % devices) for i in range(...  16.5 us
    pallas_call x8, Pallas kernels, call(): pl.pallas_call(kernel, out_shape=out_shape, in_specs=in_specs or [VMEM] *...  12.9 us
    ppermute x1, waiting for transfers between devices, shards(): other = lax.ppermute(rows, 'tensor', [(t, t ^ 1) for t in range(ranks)])  10.3 us
    all_to_all x1, blocking collectives, shards(): lax.all_to_all(copies, 'tensor', 0, 0, axis_index_groups=along_y, tiled=T...  7.14 us
    ppermute x4, waiting for transfers between devices, shifted(): lax.ppermute(block, 'blk', [(i, (i + distance) % devices) for i in range(...  5 us
    ppermute x1, starting transfers between devices, shards(): other = lax.ppermute(rows, 'tensor', [(t, t ^ 1) for t in range(ranks)])  3.85 us
  transfers between devices with their start and end apart: 5, of which 3 were waited for; matrix products, arithmetic and copies ran while one was open for 0% of the time, Pallas kernels for 7%

profile of v8, /device:TPU:1, one launch (start us, length us, event | category | flops | bytes accessed | tf_op | source)
XLA Modules:
  0.0 74.9 jit_solution(7321322047997331267)
XLA Ops:
  0.6 0.0 copy-start
  0.6 0.9 %copy-done = f32[1,2368,16]{1,2,0:T(8,128)S(1)} copy-done((f32[1,2368,16]{1,2,0:T(8,128)S(1)}, f32[1,2368,16]{1,2,0:T(8,128)}, u32[]{:S(2)}) %copy-start) | copy-done | bytes 151576
  1.5 2.4 %message.1 = (f32[16,2624]{1,0:T(8,128)S(1)}, f32[2368,256]{1,0:T(8,128)S(1)}) custom-call(f32[16,2368]{1,0:T(8,128)S(1)} %bitcast.8, f32[2368,256]{1,0:T(8,128)} %bitcast.9), custom_call_target="tpu_custom_call" | custom-call | flops 2300000000 | tf_op jit(solution)/shard_map/message/pallas_call | solution.py:196
  4.0 4.9 %collective-permute-start = (f32[16,2624]{1,0:T(8,128)S(1)}, f32[16,2624]{1,0:T(8,128)S(1)}, u32[]{:S(2)}, u32[]{:S(2)}) collective-permute-start(f32[16,2624]{1,0:T(8,128)S(1)} %get-tuple-element.11), channel_id=1, source_target_pairs={{0,8},{8,16},{16,24},{24,32},{32,40},{40,48},{48,56},{56,64},{64,7... | collective-permute-start | bytes 503816 | tf_op jit(solution)/shard_map/ppermute | solution.py:22
  8.9 0.1 slice.7
  9.0 1.9 %collective-permute-start.2 = (f32[1792,256]{1,0:T(8,128)S(1)}, f32[1792,256]{1,0:T(8,128)S(1)}, u32[]{:S(2)}, u32[]{:S(2)}) collective-permute-start(f32[1792,256]{1,0:T(8,128)S(1)} %slice.7), channel_id=1, source_target_pairs={{0,8},{8,16},{16,24},{24,32},{32,40},{40,48},{48,56},{56,64},{64,7... | collective-permute-start | bytes 5505032 | tf_op jit(solution)/shard_map/ppermute | solution.py:22
  11.0 2.7 %collective-permute-done.left_ref = f32[16,2624]{1,0:T(8,128)S(1)} collective-permute-done((f32[16,2624]{1,0:T(8,128)S(1)}, f32[16,2624]{1,0:T(8,128)S(1)}, u32[]{:S(2)}, u32[]{:S(2)}) %collective-permute-start) | collective-permute-done | bytes 167968 | tf_op jit(solution)/shard_map/ppermute | solution.py:22
  13.6 0.7 %rows.1 = f32[4,16,256]{2,1,0:T(8,128)S(1)} custom-call(f32[16,2624]{1,0:T(8,128)S(1)} %collective-permute-done.left_ref, f32[2368,256]{1,0:T(8,128)S(1)} %get-tuple-element.10.own_ref), custom_call_target="tpu_custom_call" | custom-call | flops 23000000512 | tf_op jit(solution)/shard_map/rows/pallas_call | solution.py:196
  14.4 7.1 %all_to_all.10.parts_ref = f32[4,16,256]{2,1,0:T(8,128)S(1)} all-to-all(f32[4,16,256]{2,1,0:T(8,128)S(1)} %rows.1), channel_id=1, replica_groups={{0,2,4,6},{1,3,5,7},{8,10,12,14},{9,11,13,15},{16,18,20,22},{17,19,21,2..., dimensions={0} | all-to-all | bytes 131072 | tf_op jit(solution)/shard_map/all_to_all | solution.py:237
  21.5 3.9 %collective-permute-start.1 = (f32[16,256]{1,0:T(8,128)S(1)}, f32[16,256]{1,0:T(8,128)S(1)}, u32[]{:S(2)}, u32[]{:S(2)}) collective-permute-start(f32[16,256]{1,0:T(8,128)S(1)} %sum.1.mine_ref), channel_id=1, source_target_pairs={{0,1},{1,0},{2,3},{3,2},{4,5},{5,4},{6,7},{7,6},{8,9},{9,8},{10,11... | collective-permute-start | bytes 49160 | tf_op jit(solution)/shard_map/ppermute | solution.py:239
  25.4 5.8 %collective-permute-start.3 = (f32[576,256]{1,0:T(8,128)S(1)}, f32[576,256]{1,0:T(8,128)S(1)}, u32[]{:S(2)}, u32[]{:S(2)}) collective-permute-start(f32[576,256]{1,0:T(8,128)S(1)} %slice.6), channel_id=1, source_target_pairs={{0,8},{8,16},{16,24},{24,32},{32,40},{40,48},{48,56},{56,64},{64,7... | collective-permute-start | bytes 1769480 | tf_op jit(solution)/shard_map/ppermute | solution.py:22
  31.3 10.3 %collective-permute-done.1.other_ref = f32[16,256]{1,0:T(8,128)S(1)} collective-permute-done((f32[16,256]{1,0:T(8,128)S(1)}, f32[16,256]{1,0:T(8,128)S(1)}, u32[]{:S(2)}, u32[]{:S(2)}) %collective-permute-start.1) | collective-permute-done | bytes 16416 | tf_op jit(solution)/shard_map/ppermute | solution.py:239
  41.6 0.0 collective-permute-done.2.left_ref.rest_0_
  41.6 3.7 %basis.1 = (f32[16,256]{1,0:T(8,128)S(1)}, f32[16,256]{1,0:T(8,128)S(1)}) custom-call(f32[16,256]{1,0:T(8,128)S(1)} %sum.1.mine_ref, f32[16,256]{1,0:T(8,128)S(1)} %collective-permute-done.1.other_ref, f32[2368,256]{1,0:T(8,128)S(1)} %get-tuple-element.10.own_ref, f32[1792,256]{1,0:T(8,128)S(1)} %collective-permute-done.2.left_ref.rest_0_), custom_call_target="tpu_custom_call" | custom-call | flops 16099999744 | tf_op jit(solution)/shard_map/basis/pallas_call | solution.py:196
  45.3 0.0 collective-permute-done.3.left_ref.rest_1_
  45.3 1.0 %power.1 = f32[8,16,256]{2,1,0:T(8,128)S(1)} custom-call(f32[16,256]{1,0:T(8,128)S(1)} %get-tuple-element.13.basis_ref, f32[16,256]{1,0:T(8,128)S(1)} %get-tuple-element.14.total_ref, f32[2368,256]{1,0:T(8,128)S(1)} %get-tuple-element.10.own_ref, f32[576,256]{1,0:T(8,128)S(1)} %collective-permute-done.3.left_ref.rest_1_), custom_call_target="tpu_custom_call" | custom-call | flops 3449999872 | tf_op jit(solution)/shard_map/power/pallas_call | solution.py:196
  46.2 17.4 %all_to_all.11.parts_ref = f32[8,16,256]{2,1,0:T(8,128)S(1)} all-to-all(f32[8,16,256]{2,1,0:T(8,128)S(1)} %power.1), channel_id=1, replica_groups=mesh['blk'=64,'tensor'=8] {'tensor'}, dimensions={0} | all-to-all | bytes 262144 | tf_op jit(solution)/shard_map/all_to_all | solution.py:247
  63.6 2.8 %factor.1.message_ref = f32[16,2624]{1,0:T(8,128)S(1)} custom-call(f32[8,16,256]{2,1,0:T(8,128)S(1)} %all_to_all.11.parts_ref, f32[2368,256]{1,0:T(8,128)S(1)} %get-tuple-element.10.own_ref, f32[1792,256]{1,0:T(8,128)S(1)} %collective-permute-done.2.left_ref.rest_0_, f32[576,256]{1,0:T(8,128)S(1)} %collective-permute-done.3.left_ref.rest_1_), custom_call_target="tpu_custom_call" | custom-call | flops 3449999872 | tf_op jit(solution)/shard_map/factor/pallas_call | solution.py:196
  66.4 3.8 %collective-permute-start.4 = (f32[16,2624]{1,0:T(8,128)S(1)}, f32[16,2624]{1,0:T(8,128)S(1)}, u32[]{:S(2)}, u32[]{:S(2)}) collective-permute-start(f32[16,2624]{1,0:T(8,128)S(1)} %factor.1.message_ref), channel_id=1, source_target_pairs={{0,504},{8,0},{16,8},{24,16},{32,24},{40,32},{48,40},{56,48},{64,5... | collective-permute-start | bytes 503816 | tf_op jit(solution)/shard_map/ppermute | solution.py:22
  70.2 0.6 half.1.half_ref
  70.8 2.3 %collective-permute-done.4.message_ref = f32[16,2624]{1,0:T(8,128)S(1)} collective-permute-done((f32[16,2624]{1,0:T(8,128)S(1)}, f32[16,2624]{1,0:T(8,128)S(1)}, u32[]{:S(2)}, u32[]{:S(2)}) %collective-permute-start.4) | collective-permute-done | bytes 167968 | tf_op jit(solution)/shard_map/ppermute | solution.py:22
  73.1 1.8 %final.1 = (f32[2368,256]{1,0:T(8,128)}, f32[16,2368]{1,0:T(8,128)}) custom-call(f32[16,2624]{1,0:T(8,128)S(1)} %collective-permute-done.4.message_ref, f32[2368,256]{1,0:T(8,128)S(1)} %half.1.half_ref), custom_call_target="tpu_custom_call" | custom-call | flops 3449999872 | tf_op jit(solution)/shard_map/final/pallas_call | solution.py:196
  (2 shorter events, 0.0 us)
Async XLA Ops:
  0.6 0.9 %copy-start = (f32[1,2368,16]{1,2,0:T(8,128)S(1)}, f32[1,2368,16]{1,2,0:T(8,128)}, u32[]{:S(2)}) copy-start(f32[1,2368,16]{1,2,0:T(8,128)} %param.3) | copy-start | bytes 454660
  4.0 9.7 %collective-permute-start = (f32[16,2624]{1,0:T(8,128)S(1)}, f32[16,2624]{1,0:T(8,128)S(1)}, u32[]{:S(2)}, u32[]{:S(2)}) collective-permute-start(f32[16,2624]{1,0:T(8,128)S(1)} %get-tuple-element.11), channel_id=1, source_target_pairs={{0,8},{8,16},{16,24},{24,32},{32,40},{40,48},{48,56},{56,64},{64,7... | collective-permute-start | bytes 503816 | tf_op jit(solution)/shard_map/ppermute | solution.py:22
  9.0 32.6 %collective-permute-start.2 = (f32[1792,256]{1,0:T(8,128)S(1)}, f32[1792,256]{1,0:T(8,128)S(1)}, u32[]{:S(2)}, u32[]{:S(2)}) collective-permute-start(f32[1792,256]{1,0:T(8,128)S(1)} %slice.7), channel_id=1, source_target_pairs={{0,8},{8,16},{16,24},{24,32},{32,40},{40,48},{48,56},{56,64},{64,7... | collective-permute-start | bytes 5505032 | tf_op jit(solution)/shard_map/ppermute | solution.py:22
  21.5 20.0 %collective-permute-start.1 = (f32[16,256]{1,0:T(8,128)S(1)}, f32[16,256]{1,0:T(8,128)S(1)}, u32[]{:S(2)}, u32[]{:S(2)}) collective-permute-start(f32[16,256]{1,0:T(8,128)S(1)} %sum.1.mine_ref), channel_id=1, source_target_pairs={{0,1},{1,0},{2,3},{3,2},{4,5},{5,4},{6,7},{7,6},{8,9},{9,8},{10,11... | collective-permute-start | bytes 49160 | tf_op jit(solution)/shard_map/ppermute | solution.py:239
  25.4 19.8 %collective-permute-start.3 = (f32[576,256]{1,0:T(8,128)S(1)}, f32[576,256]{1,0:T(8,128)S(1)}, u32[]{:S(2)}, u32[]{:S(2)}) collective-permute-start(f32[576,256]{1,0:T(8,128)S(1)} %slice.6), channel_id=1, source_target_pairs={{0,8},{8,16},{16,24},{24,32},{32,40},{40,48},{48,56},{56,64},{64,7... | collective-permute-start | bytes 1769480 | tf_op jit(solution)/shard_map/ppermute | solution.py:22
  66.4 6.7 %collective-permute-start.4 = (f32[16,2624]{1,0:T(8,128)S(1)}, f32[16,2624]{1,0:T(8,128)S(1)}, u32[]{:S(2)}, u32[]{:S(2)}) collective-permute-start(f32[16,2624]{1,0:T(8,128)S(1)} %factor.1.message_ref), channel_id=1, source_target_pairs={{0,504},{8,0},{16,8},{24,16},{32,24},{40,32},{48,40},{56,48},{64,5... | collective-permute-start | bytes 503816 | tf_op jit(solution)/shard_map/ppermute | solution.py:22

commit v9 on v7

--- a/solution.py
+++ b/solution.py
@@ -90,6 +90,16 @@
     out_ref[:, pl.ds(0, width)] = total
 
 
+def cut_kernel(own_ref, out_ref, sems):
+    copies = []
+    for k, (at, size) in enumerate(tiles(out_ref.shape[0], 768)):
+        part = pl.ds(at, size)
+        copies.append(pltpu.make_async_copy(own_ref.at[part], out_ref.at[part], sems.at[k]))
+        copies[-1].start()
+    for copy in copies:
+        copy.wait()
+
+
 def rows_kernel(left_ref, own_ref, out_ref):
     width = own_ref.shape[1]
     rows = left_ref[:, pl.ds(0, width)]
@@ -205,7 +215,7 @@
     )(*args)
 
 
-COST = dict(message=2, sum=1, rows=20, basis=14, power=3, factor=3, half=3, final=3)
+COST = dict(message=2, cut=1, sum=1, rows=20, basis=14, power=3, factor=3, half=3, final=3)
 FIRST = 1536
 
 
@@ -228,11 +238,14 @@
         COST["message"],
         in_specs=[HBM, HBM],
         scratch=[held, sems(512)],
-        mib=60,
+        mib=62,
     )(start, own)
     own, message = lax.optimization_barrier((own, message))
     left = shifted(message, 1)
-    left_first = shifted(own[:FIRST], 1)
+    first = call(
+        cut_kernel, "cut", shape(FIRST, width), VMEM, COST["cut"], in_specs=[HBM], scratch=[sems(768)], mib=51
+    )(own)
+    left_first = shifted(first, 1)
     copies = call(rows_kernel, "rows", shape(ranks // 2, rank, width), VMEM, COST["rows"])(left, own)
     along_y = [[2 * y + x for y in range(ranks // 2)] for x in range(2)]
     parts = lax.all_to_all(copies, "tensor", 0, 0, axis_index_groups=along_y, tiled=True)

time: 71.6 us -> 74.7 us (1.043)
  the two profiles are of different devices: /device:TPU:1 before, /device:TPU:3 now
where the time goes in v9:
time: 74.7 us; the launch traced here: 74.4 us
  blocking collectives  28.9 us (39%)
  starting transfers between devices  19.1 us (26%)
  Pallas kernels  15 us (20%)
  waiting for transfers between devices  10.5 us (14%)
  between operations  0.75 us (1%)
    all_to_all x1, blocking collectives, shards(): parts = lax.all_to_all(copies, 'tensor', 0, 0, tiled=True)  20.2 us
    ppermute x4, starting transfers between devices, shifted(): lax.ppermute(block, 'blk', [(i, (i + distance) % devices) for i in range(...  15.3 us
    pallas_call x9, Pallas kernels, call(): pl.pallas_call(kernel, out_shape=out_shape, in_specs=in_specs or [VMEM] *...  15 us
    all_to_all x1, blocking collectives, shards(): lax.all_to_all(copies, 'tensor', 0, 0, axis_index_groups=along_y, tiled=T...  8.75 us
    ppermute x1, waiting for transfers between devices, shards(): other = lax.ppermute(rows, 'tensor', [(t, t ^ 1) for t in range(ranks)])  8.21 us
    ppermute x1, starting transfers between devices, shards(): other = lax.ppermute(rows, 'tensor', [(t, t ^ 1) for t in range(ranks)])  3.74 us
    ppermute x4, waiting for transfers between devices, shifted(): lax.ppermute(block, 'blk', [(i, (i + distance) % devices) for i in range(...  2.34 us
  transfers between devices with their start and end apart: 5, of which 2 were waited for; matrix products, arithmetic and copies ran while one was open for 0% of the time, Pallas kernels for 8%

profile of v9, /device:TPU:3, one launch (start us, length us, event | category | flops | bytes accessed | tf_op | source)
XLA Modules:
  0.0 74.4 jit_solution(8553980989826228520)
XLA Ops:
  0.6 3.1 %message.1 = f32[16,2624]{1,0:T(8,128)} custom-call(f32[16,2368]{1,0:T(8,128)} %bitcast.16, f32[2368,256]{1,0:T(8,128)} %bitcast.8), custom_call_target="tpu_custom_call" | custom-call | flops 2300000000 | tf_op jit(solution)/shard_map/message/pallas_call | solution.py:206
  3.7 0.0 copy-start
  3.7 4.2 %collective-permute-start = (f32[16,2624]{1,0:T(8,128)}, f32[16,2624]{1,0:T(8,128)S(1)}, u32[]{:S(2)}, u32[]{:S(2)}) collective-permute-start(f32[16,2624]{1,0:T(8,128)} %message.1), channel_id=1, source_target_pairs={{0,8},{8,16},{16,24},{24,32},{32,40},{40,48},{48,56},{56,64},{64,7... | collective-permute-start | bytes 503816 | tf_op jit(solution)/shard_map/ppermute | solution.py:22
  8.0 1.4 %cut.1 = f32[1536,256]{1,0:T(8,128)S(1)} custom-call(f32[2368,256]{1,0:T(8,128)} %bitcast.9), custom_call_target="tpu_custom_call" | custom-call | flops 1150000000 | tf_op jit(solution)/shard_map/cut/pallas_call | solution.py:206
  9.4 1.9 %collective-permute-start.2 = (f32[1536,256]{1,0:T(8,128)S(1)}, f32[1536,256]{1,0:T(8,128)S(1)}, u32[]{:S(2)}, u32[]{:S(2)}) collective-permute-start(f32[1536,256]{1,0:T(8,128)S(1)} %cut.1), channel_id=1, source_target_pairs={{0,8},{8,16},{16,24},{24,32},{32,40},{40,48},{48,56},{56,64},{64,7... | collective-permute-start | bytes 4718600 | tf_op jit(solution)/shard_map/ppermute | solution.py:22
  11.3 0.0 collective-permute-done.left_ref
  11.3 0.0 copy-done
  11.3 0.8 %rows.1 = f32[4,16,256]{2,1,0:T(8,128)S(1)} custom-call(f32[16,2624]{1,0:T(8,128)S(1)} %collective-permute-done.left_ref, f32[2368,256]{1,0:T(8,128)S(1)} %bitcast.10), custom_call_target="tpu_custom_call" | custom-call | flops 23000000512 | tf_op jit(solution)/shard_map/rows/pallas_call | solution.py:206
  12.1 8.8 %all_to_all.10.parts_ref = f32[4,16,256]{2,1,0:T(8,128)S(1)} all-to-all(f32[4,16,256]{2,1,0:T(8,128)S(1)} %rows.1), channel_id=1, replica_groups={{0,2,4,6},{1,3,5,7},{8,10,12,14},{9,11,13,15},{16,18,20,22},{17,19,21,2..., dimensions={0} | all-to-all | bytes 131072 | tf_op jit(solution)/shard_map/all_to_all | solution.py:251
  20.9 3.7 %collective-permute-start.1 = (f32[16,256]{1,0:T(8,128)S(1)}, f32[16,256]{1,0:T(8,128)S(1)}, u32[]{:S(2)}, u32[]{:S(2)}) collective-permute-start(f32[16,256]{1,0:T(8,128)S(1)} %sum.1.mine_ref), channel_id=1, source_target_pairs={{0,1},{1,0},{2,3},{3,2},{4,5},{5,4},{6,7},{7,6},{8,9},{9,8},{10,11... | collective-permute-start | bytes 49160 | tf_op jit(solution)/shard_map/ppermute | solution.py:253
  24.6 0.1 slice.3
  24.7 5.3 %collective-permute-start.3 = (f32[832,256]{1,0:T(8,128)S(1)}, f32[832,256]{1,0:T(8,128)S(1)}, u32[]{:S(2)}, u32[]{:S(2)}) collective-permute-start(f32[832,256]{1,0:T(8,128)S(1)} %slice.3), channel_id=1, source_target_pairs={{0,8},{8,16},{16,24},{24,32},{32,40},{40,48},{48,56},{56,64},{64,7... | collective-permute-start | bytes 2555912 | tf_op jit(solution)/shard_map/ppermute | solution.py:22
  30.0 8.2 %collective-permute-done.1.other_ref = f32[16,256]{1,0:T(8,128)S(1)} collective-permute-done((f32[16,256]{1,0:T(8,128)S(1)}, f32[16,256]{1,0:T(8,128)S(1)}, u32[]{:S(2)}, u32[]{:S(2)}) %collective-permute-start.1) | collective-permute-done | bytes 16416 | tf_op jit(solution)/shard_map/ppermute | solution.py:253
  38.2 0.0 collective-permute-done.2.left_ref.rest_0_
  38.2 3.4 %basis.1 = (f32[16,256]{1,0:T(8,128)S(1)}, f32[16,256]{1,0:T(8,128)S(1)}) custom-call(f32[16,256]{1,0:T(8,128)S(1)} %sum.1.mine_ref, f32[16,256]{1,0:T(8,128)S(1)} %collective-permute-done.1.other_ref, f32[2368,256]{1,0:T(8,128)S(1)} %bitcast.12, f32[1536,256]{1,0:T(8,128)S(1)} %collective-permute-done.2.left_ref.rest_0_), custom_call_target="tpu_custom_call" | custom-call | flops 16099999744 | tf_op jit(solution)/shard_map/basis/pallas_call | solution.py:206
  41.7 0.0 collective-permute-done.3.left_ref.rest_1_
  41.7 1.2 %power.1 = f32[8,16,256]{2,1,0:T(8,128)S(1)} custom-call(f32[16,256]{1,0:T(8,128)S(1)} %get-tuple-element.13.basis_ref, f32[16,256]{1,0:T(8,128)S(1)} %get-tuple-element.14.total_ref, f32[2368,256]{1,0:T(8,128)S(1)} %bitcast.13, f32[832,256]{1,0:T(8,128)S(1)} %collective-permute-done.3.left_ref.rest_1_), custom_call_target="tpu_custom_call" | custom-call | flops 3449999872 | tf_op jit(solution)/shard_map/power/pallas_call | solution.py:206
  42.9 20.2 %all_to_all.11.parts_ref = f32[8,16,256]{2,1,0:T(8,128)S(1)} all-to-all(f32[8,16,256]{2,1,0:T(8,128)S(1)} %power.1), channel_id=1, replica_groups=mesh['blk'=64,'tensor'=8] {'tensor'}, dimensions={0} | all-to-all | bytes 262144 | tf_op jit(solution)/shard_map/all_to_all | solution.py:261
  63.1 2.8 %factor.1.message_ref = f32[16,2624]{1,0:T(8,128)S(1)} custom-call(f32[8,16,256]{2,1,0:T(8,128)S(1)} %all_to_all.11.parts_ref, f32[2368,256]{1,0:T(8,128)S(1)} %bitcast.14, f32[1536,256]{1,0:T(8,128)S(1)} %collective-permute-done.2.left_ref.rest_0_, f32[832,256]{1,0:T(8,128)S(1)} %collective-permute-done.3.left_ref.rest_1_), custom_call_target="tpu_custom_call" | custom-call | flops 3449999872 | tf_op jit(solution)/shard_map/factor/pallas_call | solution.py:206
  65.9 3.8 %collective-permute-start.4 = (f32[16,2624]{1,0:T(8,128)S(1)}, f32[16,2624]{1,0:T(8,128)S(1)}, u32[]{:S(2)}, u32[]{:S(2)}) collective-permute-start(f32[16,2624]{1,0:T(8,128)S(1)} %factor.1.message_ref), channel_id=1, source_target_pairs={{0,504},{8,0},{16,8},{24,16},{32,24},{40,32},{48,40},{56,48},{64,5... | collective-permute-start | bytes 503816 | tf_op jit(solution)/shard_map/ppermute | solution.py:22
  69.7 0.6 half.1.half_ref
  70.3 2.3 %collective-permute-done.4.message_ref = f32[16,2624]{1,0:T(8,128)S(1)} collective-permute-done((f32[16,2624]{1,0:T(8,128)S(1)}, f32[16,2624]{1,0:T(8,128)S(1)}, u32[]{:S(2)}, u32[]{:S(2)}) %collective-permute-start.4) | collective-permute-done | bytes 167968 | tf_op jit(solution)/shard_map/ppermute | solution.py:22
  72.6 1.8 %final.1 = (f32[2368,256]{1,0:T(8,128)}, f32[16,2368]{1,0:T(8,128)}) custom-call(f32[16,2624]{1,0:T(8,128)S(1)} %collective-permute-done.4.message_ref, f32[2368,256]{1,0:T(8,128)S(1)} %half.1.half_ref), custom_call_target="tpu_custom_call" | custom-call | flops 3449999872 | tf_op jit(solution)/shard_map/final/pallas_call | solution.py:206
  (1 shorter events, 0.0 us)
Async XLA Ops:
  3.7 7.6 %copy-start = (f32[256,2368]{0,1:T(8,128)S(1)}, f32[256,2368]{0,1:T(8,128)}, u32[]{:S(2)}) copy-start(f32[256,2368]{0,1:T(8,128)} %param.2) | copy-start | bytes 7274500
  3.7 7.6 %collective-permute-start = (f32[16,2624]{1,0:T(8,128)}, f32[16,2624]{1,0:T(8,128)S(1)}, u32[]{:S(2)}, u32[]{:S(2)}) collective-permute-start(f32[16,2624]{1,0:T(8,128)} %message.1), channel_id=1, source_target_pairs={{0,8},{8,16},{16,24},{24,32},{32,40},{40,48},{48,56},{56,64},{64,7... | collective-permute-start | bytes 503816 | tf_op jit(solution)/shard_map/ppermute | solution.py:22
  9.4 28.8 %collective-permute-start.2 = (f32[1536,256]{1,0:T(8,128)S(1)}, f32[1536,256]{1,0:T(8,128)S(1)}, u32[]{:S(2)}, u32[]{:S(2)}) collective-permute-start(f32[1536,256]{1,0:T(8,128)S(1)} %cut.1), channel_id=1, source_target_pairs={{0,8},{8,16},{16,24},{24,32},{32,40},{40,48},{48,56},{56,64},{64,7... | collective-permute-start | bytes 4718600 | tf_op jit(solution)/shard_map/ppermute | solution.py:22
  20.9 17.4 %collective-permute-start.1 = (f32[16,256]{1,0:T(8,128)S(1)}, f32[16,256]{1,0:T(8,128)S(1)}, u32[]{:S(2)}, u32[]{:S(2)}) collective-permute-start(f32[16,256]{1,0:T(8,128)S(1)} %sum.1.mine_ref), channel_id=1, source_target_pairs={{0,1},{1,0},{2,3},{3,2},{4,5},{5,4},{6,7},{7,6},{8,9},{9,8},{10,11... | collective-permute-start | bytes 49160 | tf_op jit(solution)/shard_map/ppermute | solution.py:253
  24.7 17.0 %collective-permute-start.3 = (f32[832,256]{1,0:T(8,128)S(1)}, f32[832,256]{1,0:T(8,128)S(1)}, u32[]{:S(2)}, u32[]{:S(2)}) collective-permute-start(f32[832,256]{1,0:T(8,128)S(1)} %slice.3), channel_id=1, source_target_pairs={{0,8},{8,16},{16,24},{24,32},{32,40},{40,48},{48,56},{56,64},{64,7... | collective-permute-start | bytes 2555912 | tf_op jit(solution)/shard_map/ppermute | solution.py:22
  65.9 6.7 %collective-permute-start.4 = (f32[16,2624]{1,0:T(8,128)S(1)}, f32[16,2624]{1,0:T(8,128)S(1)}, u32[]{:S(2)}, u32[]{:S(2)}) collective-permute-start(f32[16,2624]{1,0:T(8,128)S(1)} %factor.1.message_ref), channel_id=1, source_target_pairs={{0,504},{8,0},{16,8},{24,16},{32,24},{40,32},{48,40},{56,48},{64,5... | collective-permute-start | bytes 503816 | tf_op jit(solution)/shard_map/ppermute | solution.py:22

commit v10 on v7

--- a/solution.py
+++ b/solution.py
@@ -206,7 +206,7 @@
 
 
 COST = dict(message=2, sum=1, rows=20, basis=14, power=3, factor=3, half=3, final=3)
-FIRST = 1536
+FIRST = 1408
 
 
 def shards(weights, warm_q):

time: 71.6 us -> 73.4 us (1.025)
  starting transfers between devices: 27.9 us -> 30.2 us
  blocking collectives: 18.2 us -> 17 us
    ppermute x4, starting transfers between devices: 23.9 us -> 26.2 us  [shifted(): lax.ppermute(block, 'blk', [(i, (i + distance) % devices) for i in range(...]
    ppermute x4, waiting for transfers between devices: 3.36 us -> 5.51 us  [shifted(): lax.ppermute(block, 'blk', [(i, (i + distance) % devices) for i in range(...]
    ppermute x1, waiting for transfers between devices: 7.28 us -> 5.5 us  [shards(): other = lax.ppermute(rows, 'tensor', [(t, t ^ 1) for t in range(ranks)])]
    all_to_all x1, blocking collectives: 11 us -> 9.83 us  [shards(): parts = lax.all_to_all(copies, 'tensor', 0, 0, tiled=True)]
  transfers between devices with their start and end apart: 5 -> 5, of which waited for: 3 -> 4; matrix products, arithmetic and copies ran while one was open for 0% -> 0% of each run, Pallas kernels for 7% -> 6%
where the time goes in v10:
time: 73.4 us; the launch traced here: 73.1 us
  starting transfers between devices  30.2 us (41%)
  blocking collectives  17 us (23%)
  Pallas kernels  14.1 us (19%)
  waiting for transfers between devices  11 us (15%)
  between operations  0.74 us (1%)
    ppermute x4, starting transfers between devices, shifted(): lax.ppermute(block, 'blk', [(i, (i + distance) % devices) for i in range(...  26.2 us
    pallas_call x8, Pallas kernels, call(): pl.pallas_call(kernel, out_shape=out_shape, in_specs=in_specs or [VMEM] *...  14.1 us
    all_to_all x1, blocking collectives, shards(): parts = lax.all_to_all(copies, 'tensor', 0, 0, tiled=True)  9.83 us
    all_to_all x1, blocking collectives, shards(): lax.all_to_all(copies, 'tensor', 0, 0, axis_index_groups=along_y, tiled=T...  7.14 us
    ppermute x4, waiting for transfers between devices, shifted(): lax.ppermute(block, 'blk', [(i, (i + distance) % devices) for i in range(...  5.51 us
    ppermute x1, waiting for transfers between devices, shards(): other = lax.ppermute(rows, 'tensor', [(t, t ^ 1) for t in range(ranks)])  5.5 us
    ppermute x1, starting transfers between devices, shards(): other = lax.ppermute(rows, 'tensor', [(t, t ^ 1) for t in range(ranks)])  3.96 us
  transfers between devices with their start and end apart: 5, of which 4 were waited for; matrix products, arithmetic and copies ran while one was open for 0% of the time, Pallas kernels for 6%

profile of v10, /device:TPU:1, one launch (start us, length us, event | category | flops | bytes accessed | tf_op | source)
XLA Modules:
  0.0 73.1 jit_solution(10542704472164717549)
XLA Ops:
  0.6 0.0 copy-start
  0.6 3.2 %message.1 = f32[16,2624]{1,0:T(8,128)} custom-call(f32[16,2368]{1,0:T(8,128)} %bitcast.16, f32[2368,256]{1,0:T(8,128)} %bitcast.8), custom_call_target="tpu_custom_call" | custom-call | flops 2300000000 | tf_op jit(solution)/shard_map/message/pallas_call | solution.py:196
  3.9 4.9 %collective-permute-start = (f32[16,2624]{1,0:T(8,128)}, f32[16,2624]{1,0:T(8,128)S(1)}, u32[]{:S(2)}, u32[]{:S(2)}) collective-permute-start(f32[16,2624]{1,0:T(8,128)} %message.1), channel_id=1, source_target_pairs={{0,8},{8,16},{16,24},{24,32},{32,40},{40,48},{48,56},{56,64},{64,7... | collective-permute-start | bytes 503816 | tf_op jit(solution)/shard_map/ppermute | solution.py:22
  8.8 0.0 copy-done
  8.8 0.1 slice.7
  8.9 1.9 %collective-permute-start.2 = (f32[1408,256]{1,0:T(8,128)S(1)}, f32[1408,256]{1,0:T(8,128)S(1)}, u32[]{:S(2)}, u32[]{:S(2)}) collective-permute-start(f32[1408,256]{1,0:T(8,128)S(1)} %slice.7), channel_id=1, source_target_pairs={{0,8},{8,16},{16,24},{24,32},{32,40},{40,48},{48,56},{56,64},{64,7... | collective-permute-start | bytes 4325384 | tf_op jit(solution)/shard_map/ppermute | solution.py:22
  10.9 2.9 %collective-permute-done.left_ref = f32[16,2624]{1,0:T(8,128)S(1)} collective-permute-done((f32[16,2624]{1,0:T(8,128)}, f32[16,2624]{1,0:T(8,128)S(1)}, u32[]{:S(2)}, u32[]{:S(2)}) %collective-permute-start) | collective-permute-done | bytes 167968 | tf_op jit(solution)/shard_map/ppermute | solution.py:22
  13.8 0.8 %rows.1 = f32[4,16,256]{2,1,0:T(8,128)S(1)} custom-call(f32[16,2624]{1,0:T(8,128)S(1)} %collective-permute-done.left_ref, f32[2368,256]{1,0:T(8,128)S(1)} %bitcast.10), custom_call_target="tpu_custom_call" | custom-call | flops 23000000512 | tf_op jit(solution)/shard_map/rows/pallas_call | solution.py:196
  14.5 7.1 %all_to_all.10.parts_ref = f32[4,16,256]{2,1,0:T(8,128)S(1)} all-to-all(f32[4,16,256]{2,1,0:T(8,128)S(1)} %rows.1), channel_id=1, replica_groups={{0,2,4,6},{1,3,5,7},{8,10,12,14},{9,11,13,15},{16,18,20,22},{17,19,21,2..., dimensions={0} | all-to-all | bytes 131072 | tf_op jit(solution)/shard_map/all_to_all | solution.py:238
  21.7 4.0 %collective-permute-start.1 = (f32[16,256]{1,0:T(8,128)S(1)}, f32[16,256]{1,0:T(8,128)S(1)}, u32[]{:S(2)}, u32[]{:S(2)}) collective-permute-start(f32[16,256]{1,0:T(8,128)S(1)} %sum.1.mine_ref), channel_id=1, source_target_pairs={{0,1},{1,0},{2,3},{3,2},{4,5},{5,4},{6,7},{7,6},{8,9},{9,8},{10,11... | collective-permute-start | bytes 49160 | tf_op jit(solution)/shard_map/ppermute | solution.py:240
  25.6 0.1 slice.6
  25.7 5.7 %collective-permute-start.3 = (f32[960,256]{1,0:T(8,128)S(1)}, f32[960,256]{1,0:T(8,128)S(1)}, u32[]{:S(2)}, u32[]{:S(2)}) collective-permute-start(f32[960,256]{1,0:T(8,128)S(1)} %slice.6), channel_id=1, source_target_pairs={{0,8},{8,16},{16,24},{24,32},{32,40},{40,48},{48,56},{56,64},{64,7... | collective-permute-start | bytes 2949128 | tf_op jit(solution)/shard_map/ppermute | solution.py:22
  31.4 5.5 %collective-permute-done.1.other_ref = f32[16,256]{1,0:T(8,128)S(1)} collective-permute-done((f32[16,256]{1,0:T(8,128)S(1)}, f32[16,256]{1,0:T(8,128)S(1)}, u32[]{:S(2)}, u32[]{:S(2)}) %collective-permute-start.1) | collective-permute-done | bytes 16416 | tf_op jit(solution)/shard_map/ppermute | solution.py:240
  36.9 0.0 collective-permute-done.2.left_ref.rest_0_
  36.9 3.4 %basis.1 = (f32[16,256]{1,0:T(8,128)S(1)}, f32[16,256]{1,0:T(8,128)S(1)}) custom-call(f32[16,256]{1,0:T(8,128)S(1)} %sum.1.mine_ref, f32[16,256]{1,0:T(8,128)S(1)} %collective-permute-done.1.other_ref, f32[2368,256]{1,0:T(8,128)S(1)} %bitcast.12, f32[1408,256]{1,0:T(8,128)S(1)} %collective-permute-done.2.left_ref.rest_0_), custom_call_target="tpu_custom_call" | custom-call | flops 16099999744 | tf_op jit(solution)/shard_map/basis/pallas_call | solution.py:196
  40.3 2.1 %collective-permute-done.3.left_ref.rest_1_ = f32[960,256]{1,0:T(8,128)S(1)} collective-permute-done((f32[960,256]{1,0:T(8,128)S(1)}, f32[960,256]{1,0:T(8,128)S(1)}, u32[]{:S(2)}, u32[]{:S(2)}) %collective-permute-start.3) | collective-permute-done | bytes 983072 | tf_op jit(solution)/shard_map/ppermute | solution.py:22
  42.4 1.6 %power.1 = f32[8,16,256]{2,1,0:T(8,128)S(1)} custom-call(f32[16,256]{1,0:T(8,128)S(1)} %get-tuple-element.13.basis_ref, f32[16,256]{1,0:T(8,128)S(1)} %get-tuple-element.14.total_ref, f32[2368,256]{1,0:T(8,128)S(1)} %bitcast.13, f32[960,256]{1,0:T(8,128)S(1)} %collective-permute-done.3.left_ref.rest_1_), custom_call_target="tpu_custom_call" | custom-call | flops 3449999872 | tf_op jit(solution)/shard_map/power/pallas_call | solution.py:196
  44.0 9.8 %all_to_all.11.parts_ref = f32[8,16,256]{2,1,0:T(8,128)S(1)} all-to-all(f32[8,16,256]{2,1,0:T(8,128)S(1)} %power.1), channel_id=1, replica_groups=mesh['blk'=64,'tensor'=8] {'tensor'}, dimensions={0} | all-to-all | bytes 262144 | tf_op jit(solution)/shard_map/all_to_all | solution.py:248
  53.9 2.8 %factor.1.message_ref = f32[16,2624]{1,0:T(8,128)S(1)} custom-call(f32[8,16,256]{2,1,0:T(8,128)S(1)} %all_to_all.11.parts_ref, f32[2368,256]{1,0:T(8,128)S(1)} %bitcast.14, f32[1408,256]{1,0:T(8,128)S(1)} %collective-permute-done.2.left_ref.rest_0_, f32[960,256]{1,0:T(8,128)S(1)} %collective-permute-done.3.left_ref.rest_1_), custom_call_target="tpu_custom_call" | custom-call | flops 3449999872 | tf_op jit(solution)/shard_map/factor/pallas_call | solution.py:196
  56.7 13.7 %collective-permute-start.4 = (f32[16,2624]{1,0:T(8,128)S(1)}, f32[16,2624]{1,0:T(8,128)S(1)}, u32[]{:S(2)}, u32[]{:S(2)}) collective-permute-start(f32[16,2624]{1,0:T(8,128)S(1)} %factor.1.message_ref), channel_id=1, source_target_pairs={{0,504},{8,0},{16,8},{24,16},{32,24},{40,32},{48,40},{56,48},{64,5... | collective-permute-start | bytes 503816 | tf_op jit(solution)/shard_map/ppermute | solution.py:22
  70.3 0.6 half.1.half_ref
  70.9 0.5 collective-permute-done.4.message_ref
  71.4 1.8 %final.1 = (f32[2368,256]{1,0:T(8,128)}, f32[16,2368]{1,0:T(8,128)}) custom-call(f32[16,2624]{1,0:T(8,128)S(1)} %collective-permute-done.4.message_ref, f32[2368,256]{1,0:T(8,128)S(1)} %half.1.half_ref), custom_call_target="tpu_custom_call" | custom-call | flops 3449999872 | tf_op jit(solution)/shard_map/final/pallas_call | solution.py:196
  (1 shorter events, 0.0 us)
Async XLA Ops:
  0.6 8.2 %copy-start = (f32[256,2368]{0,1:T(8,128)S(1)}, f32[256,2368]{0,1:T(8,128)}, u32[]{:S(2)}) copy-start(f32[256,2368]{0,1:T(8,128)} %param.2) | copy-start | bytes 7274500
  3.9 9.9 %collective-permute-start = (f32[16,2624]{1,0:T(8,128)}, f32[16,2624]{1,0:T(8,128)S(1)}, u32[]{:S(2)}, u32[]{:S(2)}) collective-permute-start(f32[16,2624]{1,0:T(8,128)} %message.1), channel_id=1, source_target_pairs={{0,8},{8,16},{16,24},{24,32},{32,40},{40,48},{48,56},{56,64},{64,7... | collective-permute-start | bytes 503816 | tf_op jit(solution)/shard_map/ppermute | solution.py:22
  8.9 28.0 %collective-permute-start.2 = (f32[1408,256]{1,0:T(8,128)S(1)}, f32[1408,256]{1,0:T(8,128)S(1)}, u32[]{:S(2)}, u32[]{:S(2)}) collective-permute-start(f32[1408,256]{1,0:T(8,128)S(1)} %slice.7), channel_id=1, source_target_pairs={{0,8},{8,16},{16,24},{24,32},{32,40},{40,48},{48,56},{56,64},{64,7... | collective-permute-start | bytes 4325384 | tf_op jit(solution)/shard_map/ppermute | solution.py:22
  21.7 15.2 %collective-permute-start.1 = (f32[16,256]{1,0:T(8,128)S(1)}, f32[16,256]{1,0:T(8,128)S(1)}, u32[]{:S(2)}, u32[]{:S(2)}) collective-permute-start(f32[16,256]{1,0:T(8,128)S(1)} %sum.1.mine_ref), channel_id=1, source_target_pairs={{0,1},{1,0},{2,3},{3,2},{4,5},{5,4},{6,7},{7,6},{8,9},{9,8},{10,11... | collective-permute-start | bytes 49160 | tf_op jit(solution)/shard_map/ppermute | solution.py:240
  25.7 16.7 %collective-permute-start.3 = (f32[960,256]{1,0:T(8,128)S(1)}, f32[960,256]{1,0:T(8,128)S(1)}, u32[]{:S(2)}, u32[]{:S(2)}) collective-permute-start(f32[960,256]{1,0:T(8,128)S(1)} %slice.6), channel_id=1, source_target_pairs={{0,8},{8,16},{16,24},{24,32},{32,40},{40,48},{48,56},{56,64},{64,7... | collective-permute-start | bytes 2949128 | tf_op jit(solution)/shard_map/ppermute | solution.py:22
  56.7 14.7 %collective-permute-start.4 = (f32[16,2624]{1,0:T(8,128)S(1)}, f32[16,2624]{1,0:T(8,128)S(1)}, u32[]{:S(2)}, u32[]{:S(2)}) collective-permute-start(f32[16,2624]{1,0:T(8,128)S(1)} %factor.1.message_ref), channel_id=1, source_target_pairs={{0,504},{8,0},{16,8},{24,16},{32,24},{40,32},{48,40},{56,48},{64,5... | collective-permute-start | bytes 503816 | tf_op jit(solution)/shard_map/ppermute | solution.py:22
